TPU v7x, 128 devices: a whole 4x4x4 slice. The times are simulated.
128 devices in a mesh: pipe: 16 (over y, z_lo, core), tensor: 4 (over x), dp: 2 (over z_hi).
Axes of the slice: x: 4, y: 4, z: 4 (z_hi: 2, z_lo: 2; z = z_hi * 2 + z_lo), core: 2. Of those that a mesh axis runs over, the one named last changes fastest.
Arguments:
- hidden: bfloat16 [16, 256, 8192], P('pipe', 'dp', 'tensor'), may hold values from -3 to 3
- section_cotangent: bfloat16 [16, 256, 8192], P('pipe', 'dp', 'tensor'), may hold values from -3 to 3
- norm_gain: float32 [8192], P('tensor'), may hold values from 0.5 to 1.5
- head: bfloat16 [65536, 8192], P(('pipe', 'tensor', 'dp')), may hold values from -16 to 16
- labels: int32 [256], P('dp'), may hold values from 0 to 65535
- loss_mask: int32 [256], P('dp'), may hold values from 0 to 1
- exit_on: int32 [16], replicated, may hold values from 0 to 1, as said below
Outputs:
- head_grad: bfloat16 [65536, 8192], P(('pipe', 'tensor', 'dp'))
- residual_grad: bfloat16 [16, 256, 8192], P('pipe', 'dp', 'tensor')
- gain_grad: float32 [8192], P('tensor')
Inputs may be any that keep to these rules, and one draw needn't show every extreme that they name: `exit_on`: exactly 2 entries are 1.
All inputs are finite; a program needn't handle non-finite values.
Results may differ from a plain program's by a relative error of at most 0.0045.
The roundings to bfloat16 on the way count: a program that leaves them out, or rounds other values in their place, can miss the bound.
Values may be sent and summed in bfloat16 or wider, within the bound.
No kernel may reach another device: no remote copies, remote signals or barrier semaphores. Data moves between devices by JAX's collectives and lax.ppermute only.
A program may use at most 128 MiB of HBM per device.

v0:
```python
import jax
import jax.numpy as jnp
from jax import lax
from jax.sharding import PartitionSpec as P

E_ON = 2


NORM_EPS = 1e-05


def passed_along(block, axis, distance):
    devices = range(lax.axis_size(axis))
    route = [(i - distance, i) for i in devices if i - distance in devices]
    return lax.ppermute(block, axis, route)


def local(hidden, section_cotangent, norm_gain, head, labels, loss_mask, exit_on):
    section_count = exit_on.shape[0]
    model_width = norm_gain.shape[0] * lax.axis_size("tensor")
    tok_rows = hidden.shape[1]
    slice_width = hidden.shape[2]
    vocab_rows = head.shape[0]
    replicas = lax.axis_size("dp")
    section_here = lax.axis_index("pipe")
    section_ids = jnp.arange(section_count, dtype=jnp.int32)
    enabled = jnp.argsort(1 - exit_on, stable=True)[:E_ON]
    scores = (exit_on * (section_ids + 1)).astype(jnp.float32)
    weights = scores / jnp.sum(scores)
    widened = hidden[0].astype(jnp.float32)
    squares = lax.psum(jnp.sum(widened * widened, axis=1), "tensor")
    inverse_rms = lax.rsqrt(squares / model_width + NORM_EPS)[:, None]
    unit_rows = widened * inverse_rms
    normed = (unit_rows * norm_gain).astype(jnp.bfloat16)
    every_section = lax.all_gather(normed[None], "pipe", axis=0, tiled=True)
    chosen = every_section[enabled]
    chosen, label_all, mask_all = (
        lax.all_gather(chosen, "dp", axis=1, tiled=True),
        lax.all_gather(labels, "dp", axis=0, tiled=True),
        lax.all_gather(loss_mask, "dp", axis=0, tiled=True),
    )
    gathered = lax.all_gather(chosen, "tensor", axis=2, tiled=True)
    tokens_all = label_all.shape[0]
    flattened = gathered.reshape(E_ON * tokens_all, model_width)
    logits = lax.dot_general(
        flattened, head, (((1,), (1,)), ((), ())), preferred_element_type=jnp.float32
    )
    local_top = jnp.max(logits, axis=1)
    row_top = lax.pmax(local_top, ("pipe", "tensor", "dp"))
    row_total = lax.psum(
        jnp.sum(jnp.exp(logits - row_top[:, None]), axis=1), ("pipe", "tensor", "dp")
    )
    log_total = row_top + jnp.log(row_total)
    softmax_rows = jnp.exp(logits - log_total[:, None])
    vocab_start = lax.axis_index(("pipe", "tensor", "dp")) * vocab_rows
    label_rows = jnp.tile(label_all, E_ON)
    vocab_ids = vocab_start + jnp.arange(vocab_rows, dtype=jnp.int32)
    onehot = (label_rows[:, None] == vocab_ids[None, :]).astype(jnp.float32)
    row_weights = (weights[enabled][:, None] * mask_all[None, :].astype(jnp.float32)).reshape(-1)
    dlogits = (row_weights[:, None] * (softmax_rows - onehot)).astype(jnp.bfloat16)
    head_grad = lax.dot_general(
        dlogits, flattened, (((0,), (0,)), ((), ())), preferred_element_type=jnp.float32
    ).astype(jnp.bfloat16)
    block_rows = E_ON * tok_rows
    dlogit_blocks = dlogits.reshape(E_ON, tokens_all, vocab_rows)
    row_start = jnp.int32(0)
    results = []
    for offset in range(block_rows * lax.axis_size(("tensor", "dp")) // block_rows):
        block_index = row_start // block_rows + offset
        column = block_index // replicas
        replica = block_index % replicas
        chosen_rows = lax.dynamic_slice_in_dim(
            dlogit_blocks, replica * tok_rows, tok_rows, 1
        ).reshape(block_rows, vocab_rows)
        head_cols = lax.dynamic_slice_in_dim(head, column * slice_width, slice_width, 1)
        results.append(jnp.dot(chosen_rows, head_cols, preferred_element_type=jnp.float32))
    own_part = lax.psum_scatter(
        jnp.concatenate(results, axis=0), ("tensor", "dp"), scatter_dimension=0, tiled=True
    )
    every_exit = lax.psum(own_part.reshape(E_ON, tok_rows, slice_width), "pipe")
    selector = (enabled == section_here).astype(jnp.float32)
    grad_in = jnp.sum(selector[:, None, None] * every_exit, axis=0)
    gated_grad = grad_in * norm_gain
    inner_sums = lax.psum(jnp.sum(gated_grad * unit_rows, axis=1), "tensor")
    exit_grad = inverse_rms * (gated_grad - unit_rows * (inner_sums / model_width)[:, None])
    from_next = passed_along(section_cotangent, "pipe", -1)
    residual_grad = (exit_grad + from_next[0].astype(jnp.float32)).astype(jnp.bfloat16)[None]
    gain_grad = lax.psum(jnp.sum(grad_in * unit_rows, axis=0), ("pipe", "dp"))
    return (head_grad, residual_grad, gain_grad)


def solution(mesh):
    in_specs = (
        P("pipe", "dp", "tensor"),
        P("pipe", "dp", "tensor"),
        P("tensor"),
        P(("pipe", "tensor", "dp"), None),
        P("dp"),
        P("dp"),
        P(),
    )
    out_specs = (P(("pipe", "tensor", "dp"), None), P("pipe", "dp", "tensor"), P("tensor"))
    return jax.shard_map(local, mesh=mesh, in_specs=in_specs, out_specs=out_specs, check_vma=False)
```

profile of v0, /device:TPU:1, one launch (start us, length us, event | category | flops | bytes accessed | tf_op | source)
XLA Modules:
  0.0 766.3 jit_solution(11272487505903639750)
XLA Ops:
  8.4 9.3 %psum.35 = f32[128]{0:T(128)S(1)} all-reduce(f32[128]{0:T(128)S(1)} %fusion.21), channel_id=1, replica_groups=mesh['pipe'=16,'tensor'=4,'dp'=2] {'tensor'}, use_global_device_ids=true, to_apply=%region_3.4 | all-reduce | flops 128 | bytes 1024 | tf_op jit(solution)/shard_map/psum | solution.py:31
  17.7 2.0 fusion.14
  21.8 53.0 %all-gather.8.cloned.1.call-done = bf16[16,128,2048]{2,1,0:T(8,128)(2,1)} async-done(((bf16[1,128,2048]{2,1,0:T(8,128)(2,1)}), bf16[16,128,2048]{2,1,0:T(8,128)(2,1)}) %all-gather.8.cloned.1.call-update) | async-done | bytes 8388624 | tf_op jit(solution)/shard_map/all_gather | solution.py:35
  74.8 5.0 gather_fusion.1
  79.8 37.8 %all-gather.10.cloned.1.call-done = bf16[2,256,2048]{2,1,0:T(8,128)(2,1)} async-done(((bf16[2,128,2048]{2,1,0:T(8,128)(2,1)}), bf16[2,256,2048]{2,1,0:T(8,128)(2,1)}) %all-gather.10.cloned.1.call-update) | async-done | bytes 2097168 | tf_op jit(solution)/shard_map/all_gather | solution.py:38
  117.7 4.7 all-gather.2
  125.7 4.7 all-gather.3
  130.4 71.2 %all-gather.12.cloned.1.call-done = bf16[2,256,8192]{2,1,0:T(8,128)(2,1)} async-done(((bf16[2,256,2048]{2,1,0:T(8,128)(2,1)}), bf16[2,256,8192]{2,1,0:T(8,128)(2,1)}) %all-gather.12.cloned.1.call-update) | async-done | bytes 8388624 | tf_op jit(solution)/shard_map/all_gather | solution.py:42
  201.6 9.8 %fusion.23 = (f32[512]{0:T(512)S(1)}, f32[512,512]{1,0:T(8,128)S(1)}) fusion(bf16[512,8192]{1,0:T(8,128)(2,1)} %bitcast.49, bf16[512,8192]{1,0:T(8,128)(2,1)} %param.10), kind=kOutput, calls=%fused_computation.53 | convolution fusion | flops 4295228928 | bytes 17827840 | tf_op jit(solution)/shard_map/dot_general | solution.py:45
  211.4 65.7 %pmax.7 = f32[512]{0:T(512)S(1)} all-reduce(f32[512]{0:T(512)S(1)} %get-tuple-element.9), channel_id=1, replica_groups=mesh['pipe'=16,'tensor'=4,'dp'=2] {'pipe','tensor','dp'}, use_global_device_ids=true, to_apply=%region_5.6 | all-reduce | flops 512 | bytes 4096 | tf_op jit(solution)/shard_map/pmax | solution.py:49
  277.4 63.0 %psum.36 = f32[512]{0:T(512)S(1)} all-reduce(f32[512]{0:T(512)S(1)} %exponential_reduce_fusion), channel_id=1, replica_groups=mesh['pipe'=16,'tensor'=4,'dp'=2] {'pipe','tensor','dp'}, use_global_device_ids=true, to_apply=%region_7.8 | all-reduce | flops 512 | bytes 4096 | tf_op jit(solution)/shard_map/psum | solution.py:50
  340.8 3.8 convolution_dynamic-update-slice_fusion.7
  344.7 3.8 convolution_dynamic-update-slice_fusion.6
  348.4 3.7 convolution_dynamic-update-slice_fusion.5
  352.1 3.7 convolution_dynamic-update-slice_fusion.4
  355.8 2.1 convolution_dynamic-update-slice_fusion.3
  359.9 2.1 convolution_dynamic-update-slice_fusion.1
  362.0 2.0 convolution_dynamic-update-slice_fusion
  364.1 187.1 %reduce-scatter.2.cloned.1.call-done = f32[256,2048]{1,0:T(8,128)} async-done(((f32[2048,2048]{1,0:T(8,128)}), f32[256,2048]{1,0:T(8,128)}) %reduce-scatter.2.cloned.1.call-update) | async-done | bytes 2097168 | tf_op jit(solution)/shard_map/reduce_scatter | solution.py:77
  551.3 5.1 collective-permute-start
  556.4 10.2 %convolution_convert_fusion = bf16[512,8192]{1,0:T(8,128)(2,1)} fusion(bf16[512,512]{1,0:T(8,128)(2,1)S(1)} %multiply_convert_fusion, bf16[512,8192]{1,0:T(8,128)(2,1)} %bitcast.50), kind=kOutput, calls=%fused_computation.2 | convolution fusion | flops 4299161600 | bytes 17301504 | tf_op jit(solution)/shard_map/dot_general | solution.py:61
  566.6 112.4 %all-reduce.2.cloned.1.call-done = f32[2,128,2048]{2,1,0:T(8,128)} async-done(((f32[2,128,2048]{2,1,0:T(8,128)}), f32[2,128,2048]{2,1,0:T(8,128)}) %all-reduce.2.cloned.1.call-update) | async-done | bytes 2097168 | tf_op jit(solution)/shard_map/psum | solution.py:80
  681.4 8.4 %psum.38 = f32[128]{0:T(128)S(1)} all-reduce(f32[128]{0:T(128)S(1)} %get-tuple-element.6), channel_id=1, replica_groups=mesh['pipe'=16,'tensor'=4,'dp'=2] {'tensor'}, use_global_device_ids=true, to_apply=%region_12.13 | all-reduce | flops 128 | bytes 1024 | tf_op jit(solution)/shard_map/psum | solution.py:84
  689.8 68.8 %psum.39 = f32[2048]{0:T(1024)} all-reduce(f32[2048]{0:T(1024)S(1)} %get-tuple-element.5), channel_id=1, replica_groups=mesh['pipe'=16,'tensor'=4,'dp'=2] {'pipe','dp'}, use_global_device_ids=true, to_apply=%region_14.15 | all-reduce | flops 2048 | bytes 16384 | tf_op jit(solution)/shard_map/psum | solution.py:88
  (48 shorter events, 13.0 us)
Async XLA Ops:
  7.2 67.6 %all-gather.8.cloned.1.call-start = ((), (), s32[]{:S(2)}) async-start(), calls=%async_computation.1 | async-start | bytes 8912896 | tf_op jit(solution)/shard_map/all_gather | solution.py:35
  19.8 97.8 %all-gather.10.cloned.1.call-start = ((), (), s32[]{:S(2)}) async-start(), calls=%async_computation.4 | async-start | bytes 3145728 | tf_op jit(solution)/shard_map/all_gather | solution.py:38
  79.8 121.8 %all-gather.12.cloned.1.call-start = ((), (), s32[]{:S(2)}) async-start(), calls=%async_computation.5 | async-start | bytes 10485760 | tf_op jit(solution)/shard_map/all_gather | solution.py:42
  117.7 433.6 %reduce-scatter.2.cloned.1.call-start = ((), (), s32[]{:S(2)}) async-start(), calls=%async_computation.2 | async-start | bytes 18874368 | tf_op jit(solution)/shard_map/reduce_scatter | solution.py:77
  340.8 15.0 %slice-start = ((s8[8388608]{0:T(1024)(128)(4,1)}), s8[4194304]{0:T(1024)(128)(4,1)S(1)}, s32[]{:S(2)}) async-start(s8[8388608]{0:T(1024)(128)(4,1)} %bitcast.47), calls=%async_computation.6 | async-start | bytes 8388608
  344.7 11.1 %slice-start.1 = ((s8[8388608]{0:T(1024)(128)(4,1)}), s8[4194304]{0:T(1024)(128)(4,1)S(1)}, s32[]{:S(2)}) async-start(s8[8388608]{0:T(1024)(128)(4,1)} %bitcast.47), calls=%async_computation.7 | async-start | bytes 8388608
  364.0 187.2 %copy-start.2 = (bf16[1,128,2048]{2,1,0:T(8,128)(2,1)S(1)}, bf16[1,128,2048]{2,1,0:T(8,128)(2,1)}, u32[]{:S(2)}) copy-start(bf16[1,128,2048]{2,1,0:T(8,128)(2,1)} %param.8) | copy-start | bytes 1572868
  364.0 315.0 %all-reduce.2.cloned.1.call-start = ((), (), s32[]{:S(2)}) async-start(), calls=%async_computation.3 | async-start | bytes 4194304 | tf_op jit(solution)/shard_map/psum | solution.py:80
  551.3 207.4 %collective-permute-start = (bf16[1,128,2048]{2,1,0:T(8,128)(2,1)S(1)}, bf16[1,128,2048]{2,1,0:T(8,128)(2,1)S(1)}, u32[]{:S(2)}, u32[]{:S(2)}) collective-permute-start(bf16[1,128,2048]{2,1,0:T(8,128)(2,1)S(1)} %copy-done.2), channel_id=1, source_target_pairs={{8,0},{16,8},{24,16},{32,24},{40,32},{48,40},{56,48},{64,56},{72,6... | collective-permute-start | bytes 1572872 | tf_op jit(solution)/shard_map/ppermute | solution.py:15
  556.4 124.6 %copy-start = (bf16[1,128,2048]{2,1,0:T(8,128)(2,1)S(1)}, bf16[1,128,2048]{2,1,0:T(8,128)(2,1)}, u32[]{:S(2)}) copy-start(bf16[1,128,2048]{2,1,0:T(8,128)(2,1)} %param.7) | copy-start | bytes 1572868
  556.4 124.6 %copy-start.1 = (f32[2048]{0:T(1024)S(1)}, f32[2048]{0:T(1024)}, u32[]{:S(2)}) copy-start(f32[2048]{0:T(1024)} %param.9) | copy-start | bytes 24580
Sparse Core Ops, SparseCore 0:
  19.9 54.8 all-gather.7
  79.9 37.7 all-gather.9
  119.3 82.2 all-gather.11
  364.2 187.0 reduce-scatter.1
  553.6 125.3 all-reduce.1
where the time goes:
time: 767 us; the launch traced here: 766 us
  waiting for transfers between devices  462 us (60%)
  blocking collectives  225 us (29%)
  matrix products  43.2 us (6%)
  between operations  13.9 us (2%)
  other arithmetic  12 us (2%)
    reduce_scatter x1, waiting for transfers between devices, local(): lax.psum_scatter(jnp.concatenate(results, axis=0), ('tensor', 'dp'), scat...  187 us
    psum x1, waiting for transfers between devices, local(): every_exit = lax.psum(own_part.reshape(E_ON, tok_rows, slice_width), 'pipe')  112 us
    all_gather x1, waiting for transfers between devices, local(): gathered = lax.all_gather(chosen, 'tensor', axis=2, tiled=True)  71.2 us
    psum x1, blocking collectives, local(): gain_grad = lax.psum(jnp.sum(grad_in * unit_rows, axis=0), ('pipe', 'dp'))  68.8 us
    pmax x1, blocking collectives, local(): row_top = lax.pmax(local_top, ('pipe', 'tensor', 'dp'))  65.7 us
    psum x1, blocking collectives, local(): lax.psum(jnp.sum(jnp.exp(logits - row_top[:, None]), axis=1), ('pipe', 't...  63 us
    all_gather x1, waiting for transfers between devices, local(): every_section = lax.all_gather(normed[None], 'pipe', axis=0, tiled=True)  53 us
    all_gather x1, waiting for transfers between devices, local(): lax.all_gather(chosen, 'dp', axis=1, tiled=True)  37.8 us
  transfers between devices with their start and end apart: 6, of which 5 were waited for; matrix products, arithmetic and copies ran while one was open for 2% of the time, Pallas kernels for 0%

commit v1 on v0

v1 whole, which is shorter than its diff:
```python
import functools

import jax
import jax.numpy as jnp
import numpy as np
from jax import lax
from jax.experimental import pallas as pl
from jax.experimental.pallas import tpu as pltpu
from jax.sharding import Mesh, PartitionSpec as P

NORM_EPS = 1e-05
AXES = ("y", "zl", "c", "x", "zh")
SIZES = (4, 2, 2, 4, 2)
CHIPS = ("y", "zl", "x", "zh")
PIPE = ("y", "zl", "c")
F32, BF16 = jnp.float32, jnp.bfloat16
NT = (((1,), (1,)), ((), ()))
NN = (((1,), (0,)), ((), ()))


def route(step):
    pairs = []
    for source in range(128):
        y, zl, c, x, zh = (int(i) for i in np.unravel_index(source, SIZES))
        there = step(y, 2 * zh + zl, c, x)
        if there is not None:
            y, z, c, x = there[0] % 4, there[1] % 4, there[2] % 2, there[3] % 4
            pairs.append((source, int(np.ravel_multi_index((y, z % 2, c, x, z // 2), SIZES))))
    return pairs


def move(block, step):
    return lax.ppermute(block, AXES, route(step))


def other_core(block):
    return move(block, lambda y, z, c, x: (y, z, 1 - c, x))


def logits_kernel(cols, own, other, head, logits, lse, total):
    step = pl.program_id(0)

    @pl.when(step == 0)
    def _():
        total[...] = lax.dot_general(head[...], own[...], NT, preferred_element_type=F32)

    @pl.when((step > 0) & (step < 4))
    def _():
        total[...] += lax.dot_general(head[...], own[...], NT, preferred_element_type=F32)

    @pl.when(step >= 4)
    def _():
        total[...] += lax.dot_general(head[...], other[...], NT, preferred_element_type=F32)

    @pl.when(step == 7)
    def _():
        values = total[...]
        logits[...] = values
        top = jnp.max(values, axis=0, keepdims=True)
        lse[...] = top + jnp.log(jnp.sum(jnp.exp(values - top), axis=0, keepdims=True))


def logits_call(cols, own, other, head):
    return pl.pallas_call(
        logits_kernel,
        grid_spec=pltpu.PrefetchScalarGridSpec(
            num_scalar_prefetch=1,
            grid=(8,),
            in_specs=[
                pl.BlockSpec((512, 1024), lambda s, cols: (0, jnp.minimum(s, 3))),
                pl.BlockSpec((512, 1024), lambda s, cols: (0, jnp.maximum(s - 4, 0))),
                pl.BlockSpec((512, 1024), lambda s, cols: (0, cols[s])),
            ],
            out_specs=[
                pl.BlockSpec((512, 512), lambda s, cols: (0, 0)),
                pl.BlockSpec((1, 512), lambda s, cols: (0, 0)),
            ],
            scratch_shapes=[pltpu.VMEM((512, 512), F32)],
        ),
        out_shape=[jax.ShapeDtypeStruct((512, 512), F32), jax.ShapeDtypeStruct((1, 512), F32)],
        compiler_params=pltpu.CompilerParams(vmem_limit_bytes=32 << 20),
    )(cols, own, other, head)


def dlogits_kernel(start, logits, parts, labels, weights, dlogits):
    lse = parts[...]
    top = jnp.max(lse, axis=0, keepdims=True)
    log_total = top + jnp.log(jnp.sum(jnp.exp(lse - top), axis=0, keepdims=True))
    probs = jnp.exp(logits[...] - log_total)
    ids = start[0] + lax.broadcasted_iota(jnp.int32, (512, 512), 0)
    hot = jnp.where(ids == labels[...], 1.0, 0.0)
    dlogits[...] = (weights[...] * (probs - hot)).astype(BF16)


def dlogits_call(start, logits, parts, labels, weights):
    vmem = pl.BlockSpec(memory_space=pltpu.VMEM)
    return pl.pallas_call(
        dlogits_kernel,
        in_specs=[pl.BlockSpec(memory_space=pltpu.SMEM), vmem, vmem, vmem, vmem],
        out_specs=vmem,
        out_shape=jax.ShapeDtypeStruct((512, 512), BF16),
        compiler_params=pltpu.CompilerParams(vmem_limit_bytes=32 << 20),
    )(start, logits, parts, labels, weights)


def back_kernel(cols, dlogits, head, out, turned):
    @pl.when(pl.program_id(0) == 0)
    def _():
        turned[...] = dlogits[...].T

    out[...] = jnp.dot(turned[...], head[...], preferred_element_type=F32).astype(BF16)


def back_call(cols, dlogits, head):
    return pl.pallas_call(
        back_kernel,
        grid_spec=pltpu.PrefetchScalarGridSpec(
            num_scalar_prefetch=1,
            grid=(4,),
            in_specs=[
                pl.BlockSpec((512, 512), lambda s, cols: (0, 0)),
                pl.BlockSpec((512, 1024), lambda s, cols: (0, cols[s])),
            ],
            out_specs=pl.BlockSpec((512, 1024), lambda s, cols: (0, s)),
            scratch_shapes=[pltpu.VMEM((512, 512), BF16)],
        ),
        out_shape=jax.ShapeDtypeStruct((512, 4096), BF16),
        cost_estimate=pl.CostEstimate(flops=2 * 512 * 512 * 4096, bytes_accessed=9 << 20, transcendentals=0),
        compiler_params=pltpu.CompilerParams(vmem_limit_bytes=32 << 20),
    )(cols, dlogits, head)


def head_kernel(cols, dlogits, own, other, out):
    @pl.when(pl.program_id(0) < 4)
    def _():
        out[...] = jnp.dot(dlogits[...], own[...], preferred_element_type=F32).astype(BF16)

    @pl.when(pl.program_id(0) >= 4)
    def _():
        out[...] = jnp.dot(dlogits[...], other[...], preferred_element_type=F32).astype(BF16)


def head_call(cols, dlogits, own, other):
    return pl.pallas_call(
        head_kernel,
        grid_spec=pltpu.PrefetchScalarGridSpec(
            num_scalar_prefetch=1,
            grid=(8,),
            in_specs=[
                pl.BlockSpec((512, 512), lambda s, cols: (0, 0)),
                pl.BlockSpec((512, 1024), lambda s, cols: (0, jnp.minimum(s, 3))),
                pl.BlockSpec((512, 1024), lambda s, cols: (0, jnp.maximum(s - 4, 0))),
            ],
            out_specs=pl.BlockSpec((512, 1024), lambda s, cols: (0, cols[s])),
        ),
        out_shape=jax.ShapeDtypeStruct((512, 8192), BF16),
        cost_estimate=pl.CostEstimate(flops=2 * 512 * 512 * 8192, bytes_accessed=17 << 20, transcendentals=0),
        compiler_params=pltpu.CompilerParams(vmem_limit_bytes=32 << 20),
    )(cols, dlogits, own, other)


def local(hidden, section_cotangent, norm_gain, head, labels, loss_mask, exit_on):
    core, x, zh = lax.axis_index("c"), lax.axis_index("x"), lax.axis_index("zh")
    device = lax.axis_index(AXES)

    from_next = move(section_cotangent, lambda y, z, c, x: back_one(y, z, c, x))
    token_info = jnp.stack([labels, loss_mask])
    other_info = move(token_info, lambda y, z, c, x: (y, z + 2, c, x))
    half = lax.dynamic_slice_in_dim(norm_gain.reshape(2, 8, 128), core, 1, 0)
    turns = [half] + [move(half, lambda y, z, c, x, k=k: (y, z, c, x + k)) for k in (1, 2, 3)]
    ring = jnp.concatenate(turns[::-1], axis=0)
    gain = lax.dynamic_slice_in_dim(jnp.concatenate([ring, ring], axis=0), (3 - x) % 4, 4, 0)

    section_ids = jnp.arange(16, dtype=jnp.int32)
    first = jnp.min(jnp.where(exit_on == 1, section_ids, 16))
    second = jnp.max(jnp.where(exit_on == 1, section_ids, -1))
    scores = jnp.stack([first + 1, second + 1]).astype(F32)
    weights = scores / jnp.sum(scores)

    slots = hidden.reshape(4, 2, 4, 2, 2, 2, 8, 128).transpose(0, 1, 5, 2, 3, 4, 6, 7).reshape(128, 16, 128)
    came = lax.all_to_all(slots, AXES, 0, 0, tiled=True).reshape(16, 4, 2, 2, 8, 128)
    picked = jnp.stack([lax.dynamic_index_in_dim(came, s, 0, False) for s in (first, second)])
    rows = picked.astype(F32)
    squares = jnp.sum(rows * rows, axis=(1, 4, 5))
    squares = squares + other_core(squares)
    inverse_rms = lax.rsqrt(squares / 8192 + NORM_EPS)[:, None, :, :, None, None]
    unit = rows * inverse_rms
    spread_gain = gain[None, :, None, None]
    normed = (unit * spread_gain).astype(BF16)

    block = normed.transpose(0, 2, 3, 1, 4, 5).reshape(1, 8, 4096)
    own = lax.all_to_all(jnp.broadcast_to(block, (64, 8, 4096)), CHIPS, 0, 0, tiled=True).reshape(512, 4096)
    other = other_core(own)
    own_cols = jnp.arange(4, dtype=jnp.int32) * 2 + core
    other_cols = jnp.arange(4, dtype=jnp.int32) * 2 + 1 - core
    cols = jnp.concatenate([own_cols, other_cols])
    logits, lse = logits_call(cols, own, other, head)

    parts = lax.all_to_all(jnp.broadcast_to(lse.reshape(1, 4, 128), (128, 4, 128)), AXES, 0, 0, tiled=True)
    both = jnp.where(zh == 0, jnp.stack([token_info, other_info]), jnp.stack([other_info, token_info]))
    by_row = jnp.broadcast_to(
        both.reshape(2, 2, 64, 2).transpose(1, 2, 0, 3)[:, :, None], (2, 64, 2, 2, 2)
    )
    row_weights = weights[None, :, None, None] * by_row[1].astype(F32)
    dlogits = dlogits_call(
        (device * 512).reshape(1), logits, parts.reshape(128, 512), by_row[0].reshape(1, 512), row_weights.reshape(1, 512)
    )

    sent = back_call(other_cols, dlogits, head)
    got = other_core(sent)
    kept = back_call(own_cols, dlogits, head)
    head_grad = head_call(cols, dlogits, own, other)
    chip_sum = (kept.astype(F32) + got.astype(F32)).astype(BF16).reshape(64, 8, 4096)
    terms = lax.all_to_all(chip_sum, CHIPS, 0, 0, tiled=True)
    grad = jnp.sum(terms.astype(F32), axis=0).reshape(2, 2, 2, 4, 8, 128).transpose(0, 3, 1, 2, 4, 5)

    gated = grad * spread_gain
    inner = jnp.sum(gated * unit, axis=(1, 4, 5))
    inner = inner + other_core(inner)
    exit_grad = inverse_rms * (gated - unit * (inner / 8192)[:, None, :, :, None, None])
    gain_part = jnp.sum(grad * unit, axis=(0, 2, 3))
    high = gain_part.astype(BF16)
    low = (gain_part - high.astype(F32)).astype(BF16)
    ids = section_ids[:, None, None, None, None, None]
    placed = jnp.where(ids == first, exit_grad[0], jnp.where(ids == second, exit_grad[1], 0.0)).astype(BF16)
    gains = jnp.broadcast_to(jnp.stack([high, low], axis=1)[None, :, None], (16, 4, 2, 2, 8, 128))
    slots = jnp.concatenate([placed, gains], axis=3).reshape(128, 32, 128)
    came = lax.all_to_all(slots, AXES, 0, 0, tiled=True).reshape(4, 2, 2, 4, 2, 4, 8, 128)
    exits = came[:, :, :, :, :, :2].transpose(0, 1, 3, 4, 5, 2, 6, 7).reshape(128, 2048)
    gain_grad = jnp.sum(came[:, :, :, :, :, 2:].astype(F32), axis=(0, 1, 3, 4, 5)).reshape(2048)
    residual_grad = (exits.astype(F32) + from_next[0].astype(F32)).astype(BF16)[None]
    return head_grad, residual_grad, gain_grad


def back_one(y, z, c, x):
    section = (y * 2 + z % 2) * 2 + c - 1
    return None if section < 0 else (section // 4, z // 2 * 2 + section // 2 % 2, section % 2, x)


def solution(mesh):
    fine = Mesh(mesh.devices.reshape(SIZES), AXES)
    in_specs = (
        P(PIPE, "zh", "x"),
        P(PIPE, "zh", "x"),
        P("x"),
        P(AXES, None),
        P("zh"),
        P("zh"),
        P(),
    )
    out_specs = (P(AXES, None), P(PIPE, "zh", "x"), P("x"))
    return jax.shard_map(local, mesh=fine, in_specs=in_specs, out_specs=out_specs, check_vma=False)
```

time: 767 us -> 248 us (0.32)
  waiting for transfers between devices: 462 us -> 82.5 us
  blocking collectives: 225 us -> 56.3 us
  matrix products: 43.2 us -> 0 us
  starting transfers between devices: 5.31 us -> 40.5 us
  Pallas kernels: 0 us -> 30.5 us
  local copies, waits for them, and re-layouts: 5.68 us -> 16.1 us
    reduce_scatter x1 -> x0, waiting for transfers between devices: 187 us -> none  [local(): lax.psum_scatter(jnp.concatenate(results, axis=0), ('tensor', 'dp'), scat...]
    all_gather x3 -> x0, waiting for transfers between devices: 162 us -> none  [the longest x1 71.2 us: local(): gathered = lax.all_gather(chosen, 'tensor', axis=2, tiled=True)]
    psum x4 -> x0, blocking collectives: 150 us -> none  [the longest x1 68.8 us: local(): gain_grad = lax.psum(jnp.sum(grad_in * unit_rows, axis=0), ('pipe', 'dp'))]
    psum x1 -> x0, waiting for transfers between devices: 112 us -> none  [local(): every_exit = lax.psum(own_part.reshape(E_ON, tok_rows, slice_width), 'pipe')]
    all_to_all x0 -> x4, waiting for transfers between devices: none -> 75.1 us  [the longest x1 52.1 us: local(): terms = lax.all_to_all(chip_sum, CHIPS, 0, 0, tiled=True)]
    pmax x1 -> x0, blocking collectives: 65.7 us -> none  [local(): row_top = lax.pmax(local_top, ('pipe', 'tensor', 'dp'))]
    all_to_all x0 -> x1, blocking collectives: none -> 56.3 us  [local(): lax.all_to_all(jnp.broadcast_to(block, (64, 8, 4096)), CHIPS, 0, 0, tiled...]
    dot_general x10 -> x0, matrix products: 43.2 us -> none  [the longest x8 23.2 us: local(): jnp.dot(chosen_rows, head_cols, preferred_element_type=jnp.float32)]
  transfers between devices with their start and end apart: 6 -> 13, of which waited for: 5 -> 8; matrix products, arithmetic and copies ran while one was open for 2% -> 5% of each run, Pallas kernels for 0% -> 6%
where the time goes in v1:
time: 248 us; the launch traced here: 246 us
  waiting for transfers between devices  82.5 us (33%)
  blocking collectives  56.3 us (23%)
  starting transfers between devices  40.5 us (16%)
  Pallas kernels  30.5 us (12%)
  local copies, waits for them, and re-layouts  16.1 us (6%)
  other arithmetic  14.3 us (6%)
  between operations  6.25 us (3%)
    all_to_all x1, blocking collectives, local(): lax.all_to_all(jnp.broadcast_to(block, (64, 8, 4096)), CHIPS, 0, 0, tiled...  56.3 us
    all_to_all x1, waiting for transfers between devices, local(): terms = lax.all_to_all(chip_sum, CHIPS, 0, 0, tiled=True)  52.1 us
    ppermute x9, starting transfers between devices, move(): return lax.ppermute(block, AXES, route(step))  12.3 us
    pallas_call x1, Pallas kernels, head_call(): pl.pallas_call(head_kernel, grid_spec=pltpu.PrefetchScalarGridSpec(num_sc...  11.7 us
    all_to_all x1, starting transfers between devices, local(): lax.all_to_all(slots, AXES, 0, 0, tiled=True).reshape(16, 4, 2, 2, 8, 128)  10.8 us
    all_to_all x1, waiting for transfers between devices, local(): lax.all_to_all(jnp.broadcast_to(lse.reshape(1, 4, 128), (128, 4, 128)), A...  10.5 us
    pallas_call x1, Pallas kernels, logits_call(): pl.pallas_call(logits_kernel, grid_spec=pltpu.PrefetchScalarGridSpec(num_...  10.2 us
    unnamed x18, local copies, waits for them, and re-layouts  8.67 us
  transfers between devices with their start and end apart: 13, of which 8 were waited for; matrix products, arithmetic and copies ran while one was open for 5% of the time, Pallas kernels for 6%

profile of v1, /device:TPU:1, one launch (start us, length us, event | category | flops | bytes accessed | tf_op | source)
XLA Modules:
  0.0 246.5 jit_solution(13488010048776984459)
XLA Ops:
  1.3 3.3 %collective-permute-start.1 = (f32[1,8,128]{2,1,0:T(8,128)S(1)}, f32[1,8,128]{2,1,0:T(8,128)S(1)}, u32[]{:S(2)}, u32[]{:S(2)}) collective-permute-start(f32[1,8,128]{2,1,0:T(8,128)S(1)} %constant_dynamic-slice_fusion.1), channel_id=1, source_target_pairs={{0,6},{1,7},{2,0},{3,1},{4,2},{5,3},{6,4},{7,5},{8,14},{9,15},{10,... | collective-permute-start | bytes 12296 | tf_op jit(solution)/shard_map/ppermute | solution.py:33
  7.8 10.8 %all-to-all-start = ((bf16[128,16,128]{2,1,0:T(8,128)(2,1)}), bf16[128,16,128]{2,1,0:T(8,128)(2,1)S(1)}, u32[]{:S(2)}, u32[]{:S(2)}) async-start(bf16[128,16,128]{2,1,0:T(8,128)(2,1)} %bitcast.2), calls=%async_computation | async-start | bytes 1048576 | tf_op jit(solution)/shard_map/all_to_all | solution.py:181
  25.4 7.3 %all-to-all-done = bf16[128,16,128]{2,1,0:T(8,128)(2,1)S(1)} async-done(((bf16[128,16,128]{2,1,0:T(8,128)(2,1)}), bf16[128,16,128]{2,1,0:T(8,128)(2,1)S(1)}, u32[]{:S(2)}, u32[]{:S(2)}) %all-to-all-start) | async-done | bytes 524320 | tf_op jit(solution)/shard_map/all_to_all | solution.py:181
  34.8 56.3 %all_to_all.25 = bf16[64,8,4096]{2,1,0:T(8,128)(2,1)} all-to-all(bf16[64,8,4096]{2,1,0:T(8,128)(2,1)S(1)} %broadcast_in_dim.74), channel_id=1, replica_groups=mesh['y'=4,'zl'=2,'c'=2,'x'=4,'zh'=2] {'y','zl','x','zh'}, dimensions={0} | all-to-all | bytes 8388608 | tf_op jit(solution)/shard_map/all_to_all | solution.py:192
  91.1 1.7 collective-permute-start.4
  97.2 2.7 %collective-permute-done.4.other = bf16[512,4096]{1,0:T(8,128)(2,1)} collective-permute-done((bf16[512,4096]{1,0:T(8,128)(2,1)}, bf16[512,4096]{1,0:T(8,128)(2,1)}, u32[]{:S(2)}, u32[]{:S(2)}) %collective-permute-start.4) | collective-permute-done | bytes 4194336 | tf_op jit(solution)/shard_map/ppermute | solution.py:33
  99.9 3.4 %copy-done = bf16[512,8192]{1,0:T(8,128)(2,1)S(1)} copy-done((bf16[512,8192]{1,0:T(8,128)(2,1)S(1)}, bf16[512,8192]{1,0:T(8,128)(2,1)}, u32[]{:S(2)}) %copy-start) | copy-done | bytes 8388632
  103.3 10.2 %shard_map.94 = (f32[512,512]{1,0:T(8,128)S(1)}, f32[1,512]{1,0:T(1,128)S(1)}) custom-call(s32[8]{0:T(128)S(1)} %pad_add_fusion.1.cols, bf16[512,4096]{1,0:T(8,128)(2,1)} %bitcast.6.own, bf16[512,4096]{1,0:T(8,128)(2,1)} %collective-permute-done.4.other, bf16[512,8192]{1,0:T(8,128)(2,1)S(1)} %copy-done), custom_call_target="tpu_custom_call" | custom-call | tf_op jit(solution)/shard_map/pallas_call | solution.py:64
  114.2 4.2 %all-to-all-start.2 = ((f32[128,4,128]{2,1,0:T(4,128)}), f32[128,4,128]{2,1,0:T(4,128)S(1)}, u32[]{:S(2)}, u32[]{:S(2)}) async-start(f32[128,4,128]{2,1,0:T(4,128)} %broadcast_in_dim.76), calls=%async_computation.2 | async-start | bytes 524288 | tf_op jit(solution)/shard_map/all_to_all | solution.py:199
  119.2 10.5 %all-to-all-done.2 = f32[128,4,128]{2,1,0:T(4,128)S(1)} async-done(((f32[128,4,128]{2,1,0:T(4,128)}), f32[128,4,128]{2,1,0:T(4,128)S(1)}, u32[]{:S(2)}, u32[]{:S(2)}) %all-to-all-start.2) | async-done | bytes 262176 | tf_op jit(solution)/shard_map/all_to_all | solution.py:199
  130.1 3.4 %copy-done.1 = bf16[512,8192]{1,0:T(8,128)(2,1)S(1)} copy-done((bf16[512,8192]{1,0:T(8,128)(2,1)S(1)}, bf16[512,8192]{1,0:T(8,128)(2,1)}, u32[]{:S(2)}) %copy-start.1) | copy-done | bytes 8388632
  133.5 4.2 %shard_map.98 = bf16[512,4096]{1,0:T(8,128)(2,1)S(1)} custom-call(s32[4]{0:T(128)S(1)} %get-tuple-element.19.cols, bf16[512,512]{1,0:T(8,128)(2,1)S(1)} %shard_map.95.dlogits, bf16[512,8192]{1,0:T(8,128)(2,1)S(1)} %copy-done.1), custom_call_target="tpu_custom_call" | custom-call | flops 2147483648 | bytes 9437184 | tf_op jit(solution)/shard_map/pallas_call | solution.py:115
  138.0 4.2 %shard_map.97 = bf16[512,4096]{1,0:T(8,128)(2,1)S(1)} custom-call(s32[4]{0:T(128)S(1)} %get-tuple-element.20.cols, bf16[512,512]{1,0:T(8,128)(2,1)S(1)} %shard_map.95.dlogits, bf16[512,8192]{1,0:T(8,128)(2,1)S(1)} %copy-done.1), custom_call_target="tpu_custom_call" | custom-call | flops 2147483648 | bytes 9437184 | tf_op jit(solution)/shard_map/pallas_call | solution.py:115
  142.2 2.7 %collective-permute-done.6 = bf16[512,4096]{1,0:T(8,128)(2,1)S(1)} collective-permute-done((bf16[512,4096]{1,0:T(8,128)(2,1)S(1)}, bf16[512,4096]{1,0:T(8,128)(2,1)S(1)}, u32[]{:S(2)}, u32[]{:S(2)}) %collective-permute-start.6) | collective-permute-done | bytes 4194336 | tf_op jit(solution)/shard_map/ppermute | solution.py:33
  144.9 3.6 %fusion = bf16[64,8,4096]{2,1,0:T(8,128)(2,1)} fusion(bf16[512,4096]{1,0:T(8,128)(2,1)S(1)} %collective-permute-done.6, bf16[512,4096]{1,0:T(8,128)(2,1)S(1)} %shard_map.97), kind=kLoop, calls=%fused_computation.2 | loop fusion | flops 8388608 | bytes 12582912 | tf_op jit(solution)/shard_map/reshape | solution.py:213
  148.5 5.9 %all-to-all-start.3 = ((bf16[64,8,4096]{2,1,0:T(8,128)(2,1)}), bf16[64,8,4096]{2,1,0:T(8,128)(2,1)}, u32[]{:S(2)}, u32[]{:S(2)}) async-start(bf16[64,8,4096]{2,1,0:T(8,128)(2,1)} %fusion), calls=%async_computation.3 | async-start | bytes 8388608 | tf_op jit(solution)/shard_map/all_to_all | solution.py:214
  155.7 52.1 %all-to-all-done.3 = bf16[64,8,4096]{2,1,0:T(8,128)(2,1)} async-done(((bf16[64,8,4096]{2,1,0:T(8,128)(2,1)}), bf16[64,8,4096]{2,1,0:T(8,128)(2,1)}, u32[]{:S(2)}, u32[]{:S(2)}) %all-to-all-start.3) | async-done | bytes 4194336 | tf_op jit(solution)/shard_map/all_to_all | solution.py:214
  207.8 2.8 %convert_reduce_fusion = f32[8,4096]{1,0:T(8,128)S(1)} fusion(bf16[64,8,4096]{2,1,0:T(8,128)(2,1)} %all-to-all-done.3), kind=kLoop, calls=%fused_computation | loop fusion | flops 4161536 | bytes 4325376 | tf_op jit(solution)/shard_map/reduce_sum | solution.py:215
  210.8 1.8 collective-permute-start.7
  215.0 7.3 %all-to-all-start.4 = ((bf16[128,32,128]{2,1,0:T(8,128)(2,1)}), bf16[128,32,128]{2,1,0:T(8,128)(2,1)S(1)}, u32[]{:S(2)}, u32[]{:S(2)}) async-start(bf16[128,32,128]{2,1,0:T(8,128)(2,1)} %bitcast.20), calls=%async_computation.4 | async-start | bytes 2097152 | tf_op jit(solution)/shard_map/all_to_all | solution.py:228
  222.3 3.0 %collective-permute-start.8 = (bf16[1,128,2048]{2,1,0:T(8,128)(2,1)}, bf16[1,128,2048]{2,1,0:T(8,128)(2,1)S(1)}, u32[]{:S(2)}, u32[]{:S(2)}) collective-permute-start(bf16[1,128,2048]{2,1,0:T(8,128)(2,1)} %param.8), channel_id=1, source_target_pairs={{8,0},{9,1},{10,2},{11,3},{12,4},{13,5},{14,6},{15,7},{16,8},{17,9... | collective-permute-start | bytes 1572872 | tf_op jit(solution)/shard_map/ppermute | solution.py:33
  225.3 11.7 %shard_map.96 = bf16[512,8192]{1,0:T(8,128)(2,1)} custom-call(s32[8]{0:T(128)S(1)} %pad_add_fusion.1.cols, bf16[512,512]{1,0:T(8,128)(2,1)S(1)} %shard_map.95.dlogits, bf16[512,4096]{1,0:T(8,128)(2,1)} %bitcast.6.own, bf16[512,4096]{1,0:T(8,128)(2,1)} %collective-permute-done.4.other), custom_call_target="tpu_custom_call" | custom-call | flops 4294967296 | bytes 17825792 | tf_op jit(solution)/shard_map/pallas_call | solution.py:144
  237.0 5.2 %all-to-all-done.4 = bf16[128,32,128]{2,1,0:T(8,128)(2,1)S(1)} async-done(((bf16[128,32,128]{2,1,0:T(8,128)(2,1)}), bf16[128,32,128]{2,1,0:T(8,128)(2,1)S(1)}, u32[]{:S(2)}, u32[]{:S(2)}) %all-to-all-start.4) | async-done | bytes 1048608 | tf_op jit(solution)/shard_map/all_to_all | solution.py:228
  243.4 1.4 reshape.172
  (75 shorter events, 20.6 us)
Async XLA Ops:
  1.3 22.7 %collective-permute-start.1 = (f32[1,8,128]{2,1,0:T(8,128)S(1)}, f32[1,8,128]{2,1,0:T(8,128)S(1)}, u32[]{:S(2)}, u32[]{:S(2)}) collective-permute-start(f32[1,8,128]{2,1,0:T(8,128)S(1)} %constant_dynamic-slice_fusion.1), channel_id=1, source_target_pairs={{0,6},{1,7},{2,0},{3,1},{4,2},{5,3},{6,4},{7,5},{8,14},{9,15},{10,... | collective-permute-start | bytes 12296 | tf_op jit(solution)/shard_map/ppermute | solution.py:33
  4.6 19.4 %collective-permute-start.2 = (f32[1,8,128]{2,1,0:T(8,128)S(1)}, f32[1,8,128]{2,1,0:T(8,128)S(1)}, u32[]{:S(2)}, u32[]{:S(2)}) collective-permute-start(f32[1,8,128]{2,1,0:T(8,128)S(1)} %constant_dynamic-slice_fusion.1), channel_id=1, source_target_pairs={{0,4},{1,5},{2,6},{3,7},{4,0},{5,1},{6,2},{7,3},{8,12},{9,13},{10,... | collective-permute-start | bytes 12296 | tf_op jit(solution)/shard_map/ppermute | solution.py:33
  5.2 18.9 %collective-permute-start.3 = (f32[1,8,128]{2,1,0:T(8,128)S(1)}, f32[1,8,128]{2,1,0:T(8,128)S(1)}, u32[]{:S(2)}, u32[]{:S(2)}) collective-permute-start(f32[1,8,128]{2,1,0:T(8,128)S(1)} %constant_dynamic-slice_fusion.1), channel_id=1, source_target_pairs={{0,2},{1,3},{2,4},{3,5},{4,6},{5,7},{6,0},{7,1},{8,10},{9,11},{10,... | collective-permute-start | bytes 12296 | tf_op jit(solution)/shard_map/ppermute | solution.py:33
  7.8 24.9 %all-to-all-start = ((bf16[128,16,128]{2,1,0:T(8,128)(2,1)}), bf16[128,16,128]{2,1,0:T(8,128)(2,1)S(1)}, u32[]{:S(2)}, u32[]{:S(2)}) async-start(bf16[128,16,128]{2,1,0:T(8,128)(2,1)} %bitcast.2), calls=%async_computation | async-start | bytes 1048576 | tf_op jit(solution)/shard_map/all_to_all | solution.py:181
  32.9 1.2 collective-permute-start
  34.8 58.0 %copy-start.2 = (s32[128]{0:T(128)S(1)}, s32[128]{0:T(128)}, u32[]{:S(2)}) copy-start(s32[128]{0:T(128)} %param.12) | copy-start | bytes 1540
  34.8 58.0 %copy-start.3 = (s32[128]{0:T(128)S(1)}, s32[128]{0:T(128)}, u32[]{:S(2)}) copy-start(s32[128]{0:T(128)} %param.11) | copy-start | bytes 1540
  91.1 8.9 %collective-permute-start.4 = (bf16[512,4096]{1,0:T(8,128)(2,1)}, bf16[512,4096]{1,0:T(8,128)(2,1)}, u32[]{:S(2)}, u32[]{:S(2)}) collective-permute-start(bf16[512,4096]{1,0:T(8,128)(2,1)} %bitcast.6.own), channel_id=1, source_target_pairs={{0,8},{1,9},{2,10},{3,11},{4,12},{5,13},{6,14},{7,15},{8,0},{9,1},... | collective-permute-start | bytes 12582920 | tf_op jit(solution)/shard_map/ppermute | solution.py:33
  92.8 4.1 %collective-permute-start.5 = (s32[2,128]{1,0:T(2,128)S(1)}, s32[2,128]{1,0:T(2,128)S(1)}, u32[]{:S(2)}, u32[]{:S(2)}) collective-permute-start(s32[2,128]{1,0:T(2,128)S(1)} %pad_add_fusion), channel_id=1, source_target_pairs={{0,1},{1,0},{2,3},{3,2},{4,5},{5,4},{6,7},{7,6},{8,9},{9,8},{10,11... | collective-permute-start | bytes 3080 | tf_op jit(solution)/shard_map/ppermute | solution.py:33
  99.9 3.4 %copy-start = (bf16[512,8192]{1,0:T(8,128)(2,1)S(1)}, bf16[512,8192]{1,0:T(8,128)(2,1)}, u32[]{:S(2)}) copy-start(bf16[512,8192]{1,0:T(8,128)(2,1)} %head.5) | copy-start | bytes 25165828
  114.2 15.5 %all-to-all-start.2 = ((f32[128,4,128]{2,1,0:T(4,128)}), f32[128,4,128]{2,1,0:T(4,128)S(1)}, u32[]{:S(2)}, u32[]{:S(2)}) async-start(f32[128,4,128]{2,1,0:T(4,128)} %broadcast_in_dim.76), calls=%async_computation.2 | async-start | bytes 524288 | tf_op jit(solution)/shard_map/all_to_all | solution.py:199
  130.1 3.4 %copy-start.1 = (bf16[512,8192]{1,0:T(8,128)(2,1)S(1)}, bf16[512,8192]{1,0:T(8,128)(2,1)}, u32[]{:S(2)}) copy-start(bf16[512,8192]{1,0:T(8,128)(2,1)} %head.5) | copy-start | bytes 25165828
  137.7 7.2 %collective-permute-start.6 = (bf16[512,4096]{1,0:T(8,128)(2,1)S(1)}, bf16[512,4096]{1,0:T(8,128)(2,1)S(1)}, u32[]{:S(2)}, u32[]{:S(2)}) collective-permute-start(bf16[512,4096]{1,0:T(8,128)(2,1)S(1)} %shard_map.98), channel_id=1, source_target_pairs={{0,8},{1,9},{2,10},{3,11},{4,12},{5,13},{6,14},{7,15},{8,0},{9,1},... | collective-permute-start | bytes 12582920 | tf_op jit(solution)/shard_map/ppermute | solution.py:33
  148.5 59.2 %all-to-all-start.3 = ((bf16[64,8,4096]{2,1,0:T(8,128)(2,1)}), bf16[64,8,4096]{2,1,0:T(8,128)(2,1)}, u32[]{:S(2)}, u32[]{:S(2)}) async-start(bf16[64,8,4096]{2,1,0:T(8,128)(2,1)} %fusion), calls=%async_computation.3 | async-start | bytes 8388608 | tf_op jit(solution)/shard_map/all_to_all | solution.py:214
  210.8 2.6 %collective-permute-start.7 = (f32[2,2,2]{2,1,0:T(2,128)S(1)}, f32[2,2,2]{2,1,0:T(2,128)S(1)}, u32[]{:S(2)}, u32[]{:S(2)}) collective-permute-start(f32[2,2,2]{2,1,0:T(2,128)S(1)} %get-tuple-element.7), channel_id=1, source_target_pairs={{0,8},{1,9},{2,10},{3,11},{4,12},{5,13},{6,14},{7,15},{8,0},{9,1},... | collective-permute-start | bytes 104 | tf_op jit(solution)/shard_map/ppermute | solution.py:33
  215.0 27.2 %all-to-all-start.4 = ((bf16[128,32,128]{2,1,0:T(8,128)(2,1)}), bf16[128,32,128]{2,1,0:T(8,128)(2,1)S(1)}, u32[]{:S(2)}, u32[]{:S(2)}) async-start(bf16[128,32,128]{2,1,0:T(8,128)(2,1)} %bitcast.20), calls=%async_computation.4 | async-start | bytes 2097152 | tf_op jit(solution)/shard_map/all_to_all | solution.py:228
  222.3 23.2 %collective-permute-start.8 = (bf16[1,128,2048]{2,1,0:T(8,128)(2,1)}, bf16[1,128,2048]{2,1,0:T(8,128)(2,1)S(1)}, u32[]{:S(2)}, u32[]{:S(2)}) collective-permute-start(bf16[1,128,2048]{2,1,0:T(8,128)(2,1)} %param.8), channel_id=1, source_target_pairs={{8,0},{9,1},{10,2},{11,3},{12,4},{13,5},{14,6},{15,7},{16,8},{17,9... | collective-permute-start | bytes 1572872 | tf_op jit(solution)/shard_map/ppermute | solution.py:33

commit v2 on v0

v2 whole, which is shorter than its diff:
```python
import functools

import jax
import jax.numpy as jnp
import numpy as np
from jax import lax
from jax.experimental import pallas as pl
from jax.experimental.pallas import tpu as pltpu
from jax.sharding import Mesh, PartitionSpec as P

NORM_EPS = 1e-05
AXES = ("y", "zl", "c", "x", "zh")
SIZES = (4, 2, 2, 4, 2)
CHIPS = ("x", "y", "zl", "zh")
PIPE = ("y", "zl", "c")
F32, BF16 = jnp.float32, jnp.bfloat16
NT = (((1,), (1,)), ((), ()))
LIMIT = 16 << 20
COLOURS = [(x + 2 * y + 3 * (2 * zh + zl)) % 4 for x in range(4) for y in range(4) for zl in range(2) for zh in range(2)]


def route(step):
    pairs = []
    for source in range(128):
        y, zl, c, x, zh = (int(i) for i in np.unravel_index(source, SIZES))
        there = step(y, 2 * zh + zl, c, x)
        if there is not None:
            y, z, c, x = there[0] % 4, there[1] % 4, there[2] % 2, there[3] % 4
            pairs.append((source, int(np.ravel_multi_index((y, z % 2, c, x, z // 2), SIZES))))
    return pairs


def move(block, step):
    return lax.ppermute(block, AXES, route(step))


def other_core(block):
    return move(block, lambda y, z, c, x: (y, z, 1 - c, x))


def to_colour(block, away):
    if away == 1:
        return move(block, lambda y, z, c, x: (y, z - 1, c, x) if c else (y, z, c, x + 1))
    if away == 3:
        return move(block, lambda y, z, c, x: (y, z + 1, c, x) if c else (y, z, c, x - 1))
    return move(block, lambda y, z, c, x: (y - 1 if c else y + 1, z, c, x))


def back_one(y, z, c, x):
    section = (y * 2 + z % 2) * 2 + c - 1
    return None if section < 0 else (section // 4, z // 2 * 2 + section // 2 % 2, section % 2, x)


def call(kernel, scalars, operands, outs, flops=0, moved=1 << 20):
    vmem = pl.BlockSpec(memory_space=pltpu.VMEM)
    smem = [] if scalars is None else [pl.BlockSpec(memory_space=pltpu.SMEM)]
    held = [pltpu.with_memory_space_constraint(o, pltpu.VMEM) for o in operands]
    return pl.pallas_call(
        kernel,
        in_specs=smem + [vmem] * len(operands),
        out_specs=[vmem] * len(outs),
        out_shape=[(jax.ShapeDtypeStruct if place else pltpu.VMEM)(shape, kind) for shape, kind, *place in outs],
        cost_estimate=pl.CostEstimate(flops=flops, bytes_accessed=moved, transcendentals=0),
        compiler_params=pltpu.CompilerParams(vmem_limit_bytes=LIMIT),
    )(*([] if scalars is None else [scalars]), *held)


def columns(tint, t, away):
    return pl.ds(pl.multiple_of(t * 2048 + tint[away] * 512, 512), 512)


def slots_kernel(rows, out):
    wide = rows[...].astype(F32)
    squares = jnp.sum(wide * wide, axis=1, keepdims=True)
    high = squares.astype(BF16).astype(F32)
    middle = (squares - high).astype(BF16).astype(F32)
    low = squares - high - middle
    lane = lax.broadcasted_iota(jnp.int32, (16, 128), 1)
    extra = jnp.where(lane == 0, high, jnp.where(lane == 1, middle, jnp.where(lane == 2, low, 0.0))).astype(BF16)
    for chip, colour in enumerate(COLOURS):
        out[chip, :, :512] = rows[:, colour * 512 : (colour + 1) * 512]
        out[chip, :, 512:] = extra


def slots_call(rows):
    return call(slots_kernel, None, [rows], [((64, 16, 640), BF16, True)])[0]


def norm_kernel(came, gain, own, inverse_rms):
    for group in range(16):
        span = slice(group * 16, (group + 1) * 16)
        squares = sum(came[t * 16 + group, :, 512:].astype(F32) for t in range(4))
        inverse = lax.rsqrt(jnp.sum(squares, axis=1, keepdims=True) / 8192 + NORM_EPS)
        inverse_rms[span, :] = jnp.broadcast_to(inverse, (16, 128))
        for t in range(4):
            unit = came[t * 16 + group, :, :512].astype(F32) * inverse
            own[t, span, :] = (unit * gain[t : t + 1, :]).astype(BF16)


def norm_call(came, gain):
    return call(norm_kernel, None, [came, gain], [((4, 256, 512), BF16), ((256, 128), F32, True)], moved=2 << 20)


def add_up(tint, aways, head, blocks, total):
    def part(t):
        return sum(
            lax.dot_general(head[:, columns(tint, t, away)], block[t], NT, preferred_element_type=F32)
            for away, block in zip(aways, blocks)
        )

    total[...] = part(0)

    @pl.loop(1, 4)
    def _(t):
        total[...] += part(t)


def logits_kernel(aways, tint, head, *refs):
    add_up(tint, aways, head, refs[:-1], refs[-1])


def logits_call(tint, head, aways, blocks):
    flops = 2 * 512 * 256 * 2048 * len(aways)
    kernel = functools.partial(logits_kernel, aways)
    return call(kernel, tint, [head, *blocks], [((512, 256), F32)], flops, len(aways) << 21)[0]


def last_kernel(tint, head, block_1, block_2, block_3, early, ours, theirs, logits, lse, total):
    add_up(tint, (1, 2, 3), head, (block_1, block_2, block_3), total)
    logits[:, :256] = early[...] + ours[...]
    logits[:, 256:] = theirs[...] + total[...]
    values = logits[...]
    top = jnp.max(values, axis=0, keepdims=True)
    sums = top + jnp.log(jnp.sum(jnp.exp(values - top), axis=0, keepdims=True))
    quarters = [sums[:, i * 128 : (i + 1) * 128] for i in range(4)]
    in_order = jnp.concatenate(quarters, axis=0)
    swapped = jnp.concatenate(quarters[2:] + quarters[:2], axis=0)
    lse[...] = jnp.broadcast_to(jnp.where(tint[4] == 0, in_order, swapped)[None], (128, 4, 128))


def last_call(tint, head, blocks, early, ours, theirs):
    outs = [((512, 512), F32), ((128, 4, 128), F32, True), ((512, 256), F32)]
    return call(last_kernel, tint, [head, *blocks, early, ours, theirs], outs, 6 * 512 * 256 * 2048, 9 << 20)[:2]


def dlogits_kernel(place, logits, parts, labels, weights, turned, dlogits):
    lse = parts[...]
    top = jnp.max(lse, axis=0)
    log_total = top + jnp.log(jnp.sum(jnp.exp(lse - top[None]), axis=0))
    quarters = [log_total[i : i + 1] for i in range(4)]
    in_order = jnp.concatenate(quarters, axis=1)
    swapped = jnp.concatenate(quarters[2:] + quarters[:2], axis=1)
    probs = jnp.exp(logits[...] - jnp.where(place[1] == 0, in_order, swapped))
    ids = place[0] * 512 + lax.broadcasted_iota(jnp.int32, (512, 512), 0)
    hot = jnp.where(ids == labels[...], 1.0, 0.0)
    values = (weights[...] * (probs - hot)).astype(BF16)
    turned[...] = values
    dlogits[...] = values.T


def dlogits_call(place, logits, parts, labels, weights):
    outs = [((512, 512), BF16)] * 2
    return call(dlogits_kernel, place, [logits, parts, labels, weights], outs, moved=3 << 20)


def fetch_kernel(after, source, out, sem):
    copy = pltpu.make_async_copy(source, out, sem)
    copy.start()
    copy.wait()


def fetch(source, after):
    return pl.pallas_call(
        fetch_kernel,
        in_specs=[pl.BlockSpec(memory_space=pl.ANY)] * 2,
        out_specs=pl.BlockSpec(memory_space=pltpu.VMEM),
        out_shape=pltpu.VMEM(source.shape, source.dtype),
        scratch_shapes=[pltpu.SemaphoreType.DMA],
        cost_estimate=pl.CostEstimate(flops=0, bytes_accessed=8 << 20, transcendentals=0),
        compiler_params=pltpu.CompilerParams(vmem_limit_bytes=LIMIT),
    )(after, source)


def back_kernel(away, tint, dlogits, head, own, other):
    @pl.loop(0, 4)
    def _(t):
        value = jnp.dot(dlogits[...], head[:, columns(tint, t, away)], preferred_element_type=F32)
        own[t] = value[:256]
        other[t] = value[256:].astype(BF16)


def back_call(tint, dlogits, head, away):
    kernel = functools.partial(back_kernel, away)
    outs = [((4, 256, 512), F32), ((4, 256, 512), BF16)]
    return call(kernel, tint, [dlogits, head], outs, 2 * 512 * 512 * 2048, 4 << 20)


def head_kernel(tint, turned, *refs):
    out = refs[-1]
    for away in range(4):
        own, other = refs[away], refs[4 + away]
        value = jnp.dot(turned[:, :256], own[0], preferred_element_type=F32)
        value += jnp.dot(turned[:, 256:], other[0], preferred_element_type=F32)
        out[:, pl.ds(pl.multiple_of(tint[away] * 512, 512), 512)] = value.astype(BF16)


def head_call(tint, turned, own, other):
    block = pl.BlockSpec((1, 256, 512), lambda t, tint: (t, 0, 0))
    return pl.pallas_call(
        head_kernel,
        grid_spec=pltpu.PrefetchScalarGridSpec(
            num_scalar_prefetch=1,
            grid=(4,),
            in_specs=[pl.BlockSpec((512, 512), lambda t, tint: (0, 0))] + [block] * 8,
            out_specs=pl.BlockSpec((512, 2048), lambda t, tint: (0, t)),
        ),
        out_shape=jax.ShapeDtypeStruct((512, 8192), BF16),
        cost_estimate=pl.CostEstimate(flops=2 * 512 * 512 * 8192, bytes_accessed=17 << 20, transcendentals=0),
        compiler_params=pltpu.CompilerParams(vmem_limit_bytes=LIMIT),
    )(tint, turned, *own, *other)


def tail_kernel(terms, rows, inverse_rms, gain, gated, unit, inner, gain_part):
    sums = [None] * 4
    for chip, colour in enumerate(COLOURS):
        term = terms[chip].astype(F32)
        sums[colour] = term if sums[colour] is None else sums[colour] + term
    inverse = inverse_rms[:, :1]
    total = jnp.zeros((16, 1), F32)
    for colour, grad in enumerate(sums):
        span = slice(colour * 512, (colour + 1) * 512)
        ours = rows[:, span].astype(F32) * inverse
        scaled = grad * gain[:, span]
        unit[:, span] = ours
        gated[:, span] = scaled
        total += jnp.sum(scaled * ours, axis=1, keepdims=True)
        part = jnp.sum(grad * ours, axis=0, keepdims=True)
        for i in range(2):
            gain_part[colour * 2 + i : colour * 2 + i + 1, :] = part[:, i * 256 : (i + 1) * 256]
    inner[...] = jnp.broadcast_to(total, (16, 128))


def tail_call(terms, rows, inverse_rms, gain):
    outs = [((16, 2048), F32), ((16, 2048), F32), ((16, 128), F32), ((8, 256), F32)]
    return call(tail_kernel, None, [terms, rows, inverse_rms, gain], outs, moved=2 << 20)


def exit_kernel(chosen, gated, unit, inverse_rms, inner, inner_1, inner_2, inner_3, gain, gain_1, out):
    total = (inner[...] + inner_1[...] + inner_2[...] + inner_3[...])[:, :1] / 8192
    grad = inverse_rms[:, :1] * (gated[...] - unit[...] * total)
    sums = gain[...] + gain_1[...]
    high = sums.astype(BF16).astype(F32)
    low = sums - high
    for section in range(16):
        value = jnp.where(chosen[0] == section, grad[:8], jnp.where(chosen[1] == section, grad[8:], 0.0))
        out[section] = jnp.concatenate([value, high, low], axis=1).astype(BF16)


def exit_call(chosen, *operands):
    return call(exit_kernel, chosen, operands, [((16, 8, 2560), BF16, True)])[0]


def local(hidden, section_cotangent, norm_gain, head, labels, loss_mask, exit_on):
    core, x, y, zl, zh = (lax.axis_index(a) for a in ("c", "x", "y", "zl", "zh"))
    device = lax.axis_index(AXES).astype(jnp.int32)
    colour = (x + 2 * y + 3 * (2 * zh + zl)) % 4
    aways = (colour + jnp.arange(4, dtype=jnp.int32)) % 4
    tint = jnp.concatenate([aways, core.reshape(1)]).astype(jnp.int32)

    came = lax.all_to_all(hidden.reshape(16, 8, 2048), PIPE, 0, 0, tiled=True)
    section_ids = jnp.arange(16, dtype=jnp.int32)
    first = jnp.min(jnp.where(exit_on == 1, section_ids, 16))
    second = jnp.max(jnp.where(exit_on == 1, section_ids, -1))
    chosen = jnp.stack([first, second])
    scores = (chosen + 1).astype(F32)
    weights = scores / jnp.sum(scores)

    turns = [norm_gain] + [move(norm_gain, lambda y, z, c, x, k=k: (y, z, c, x + k)) for k in (1, 2, 3)]
    ring = jnp.stack(turns[::-1] * 2)
    gain = lax.dynamic_slice(ring, ((3 - x) % 4, colour * 512), (4, 512))
    came, gain = lax.optimization_barrier((came, gain))
    rows = jnp.concatenate([lax.dynamic_index_in_dim(came, s, 0, False) for s in (first, second)])
    token_info = jnp.stack([labels, loss_mask])
    other_info = move(token_info, lambda y, z, c, x: (y, z + 2, c, x))
    both = jnp.where(zh == 0, jnp.stack([token_info, other_info]), jnp.stack([other_info, token_info]))
    by_row = jnp.broadcast_to(
        both.reshape(2, 2, 4, 2, 2, 8).transpose(4, 1, 2, 3, 0, 5)[:, :, :, :, :, None], (2, 2, 4, 2, 2, 2, 8)
    )
    by_row = jnp.where(core == 0, by_row, by_row[::-1])
    row_labels = by_row[:, 0].reshape(1, 512)
    row_weights = (weights[:, None] * by_row[:, 1].astype(F32)).reshape(1, 512)

    quarter = lax.all_to_all(slots_call(rows), CHIPS, 0, 0, tiled=True)
    quarter, row_labels, row_weights = lax.optimization_barrier((quarter, row_labels, row_weights))
    own, inverse_rms = norm_call(quarter, gain)

    blocks = [own, to_colour(own, 3), to_colour(own, 2), to_colour(own, 1)]
    first_mate = other_core(own)
    early = logits_call(tint, head, (0,), blocks[:1])
    blocks[1], blocks[2], blocks[3], early = lax.optimization_barrier((*blocks[1:], early))
    mates = [first_mate] + [other_core(b) for b in blocks[1:]]
    theirs = logits_call(tint, head, (0,), mates[:1])
    ours = logits_call(tint, head, (1, 2, 3), blocks[1:])
    logits, lse = last_call(tint, head, mates[1:], early, ours, theirs)
    parts = lax.all_to_all(lse, AXES, 0, 0, tiled=True)
    near = fetch(head, lse)
    parts, near = lax.optimization_barrier((parts, near))
    turned, dlogits = dlogits_call(jnp.stack([device, core]), logits, parts, row_labels, row_weights)

    halves = [back_call(tint, dlogits, near, away) for away in (1, 2, 3)]
    sums = [(ours + other_core(theirs).astype(F32)).astype(BF16) for ours, theirs in halves]
    arrived = [to_colour(s, away) for s, away in zip(sums, (1, 2, 3))]
    late, _ = lax.optimization_barrier((dlogits, sums[2]))
    ours, theirs = back_call(tint, late, near, 0)
    quarter = ours + other_core(theirs).astype(F32) + sum(a.astype(F32) for a in arrived)
    terms = lax.all_to_all(quarter.astype(BF16).reshape(64, 16, 512), CHIPS, 0, 0, tiled=True)
    head_grad = head_call(tint, turned, blocks, mates)
    terms, head_grad = lax.optimization_barrier((terms, head_grad))

    place = (y * 2 + zl) * 2 + zh
    inverse_here = lax.dynamic_slice_in_dim(inverse_rms, place * 16, 16, 0)
    gated, unit, inner, gain_part = tail_call(terms, rows, inverse_here, norm_gain.reshape(1, 2048))
    inners = [inner] + [move(inner, lambda y, z, c, x, k=k: (y, z, c, x + k)) for k in (1, 2, 3)]
    gain_other = move(gain_part, lambda y, z, c, x: (y, z + 2, c, x))
    placed = exit_call(chosen, gated, unit, inverse_here, *inners, gain_part, gain_other)
    came = lax.all_to_all(placed, PIPE, 0, 0, tiled=True)
    gain_grad = jnp.sum(came[:, :, 2048:].astype(F32).reshape(16, 8, 2, 256), axis=(0, 2)).reshape(2048)
    from_next = move(section_cotangent, back_one)
    residual_grad = (came[:, :, :2048].reshape(1, 128, 2048).astype(F32) + from_next.astype(F32)).astype(BF16)
    return head_grad, residual_grad, gain_grad


def solution(mesh):
    fine = Mesh(mesh.devices.reshape(SIZES), AXES)
    in_specs = (
        P(PIPE, "zh", "x"),
        P(PIPE, "zh", "x"),
        P("x"),
        P(AXES, None),
        P("zh"),
        P("zh"),
        P(),
    )
    out_specs = (P(AXES, None), P(PIPE, "zh", "x"), P("x"))
    return jax.shard_map(local, mesh=fine, in_specs=in_specs, out_specs=out_specs, check_vma=False)
```

time: 767 us -> 191 us (0.25)
  waiting for transfers between devices: 462 us -> 49.3 us
  blocking collectives: 225 us -> 0 us
  starting transfers between devices: 5.31 us -> 67.1 us
  matrix products: 43.2 us -> 0 us
  Pallas kernels: 0 us -> 33.2 us
  local copies, waits for them, and re-layouts: 5.68 us -> 27.4 us
  between operations: 13.9 us -> 5.02 us
    reduce_scatter x1 -> x0, waiting for transfers between devices: 187 us -> none  [local(): lax.psum_scatter(jnp.concatenate(results, axis=0), ('tensor', 'dp'), scat...]
    all_gather x3 -> x0, waiting for transfers between devices: 162 us -> none  [the longest x1 71.2 us: local(): gathered = lax.all_gather(chosen, 'tensor', axis=2, tiled=True)]
    psum x4 -> x0, blocking collectives: 150 us -> none  [the longest x1 68.8 us: local(): gain_grad = lax.psum(jnp.sum(grad_in * unit_rows, axis=0), ('pipe', 'dp'))]
    psum x1 -> x0, waiting for transfers between devices: 112 us -> none  [local(): every_exit = lax.psum(own_part.reshape(E_ON, tok_rows, slice_width), 'pipe')]
    pmax x1 -> x0, blocking collectives: 65.7 us -> none  [local(): row_top = lax.pmax(local_top, ('pipe', 'tensor', 'dp'))]
    dot_general x10 -> x0, matrix products: 43.2 us -> none  [the longest x8 23.2 us: local(): jnp.dot(chosen_rows, head_cols, preferred_element_type=jnp.float32)]
    all_to_all x0 -> x5, starting transfers between devices: none -> 39.4 us  [the longest x1 9.99 us: local(): quarter = lax.all_to_all(slots_call(rows), CHIPS, 0, 0, tiled=True)]
    pallas_call x0 -> x15, Pallas kernels: none -> 33.2 us  [the longest x13 25.7 us: call(): pl.pallas_call(kernel, in_specs=smem + [vmem] * len(operands), out_specs=...]
  transfers between devices with their start and end apart: 6 -> 28, of which waited for: 5 -> 10; matrix products, arithmetic and copies ran while one was open for 2% -> 4% of each run, Pallas kernels for 0% -> 11%
where the time goes in v2:
time: 191 us; the launch traced here: 190 us
  starting transfers between devices  67.1 us (35%)
  waiting for transfers between devices  49.3 us (26%)
  Pallas kernels  33.2 us (17%)
  local copies, waits for them, and re-layouts  27.4 us (14%)
  other arithmetic  8 us (4%)
  between operations  5.02 us (3%)
    ppermute x23, starting transfers between devices, move(): return lax.ppermute(block, AXES, route(step))  27.7 us
    pallas_call x13, Pallas kernels, call(): pl.pallas_call(kernel, in_specs=smem + [vmem] * len(operands), out_specs=...  25.7 us
    unnamed x54, local copies, waits for them, and re-layouts  25 us
    ppermute x23, waiting for transfers between devices, move(): return lax.ppermute(block, AXES, route(step))  21 us
    all_to_all x1, waiting for transfers between devices, local(): quarter = lax.all_to_all(slots_call(rows), CHIPS, 0, 0, tiled=True)  13.9 us
    all_to_all x1, starting transfers between devices, local(): quarter = lax.all_to_all(slots_call(rows), CHIPS, 0, 0, tiled=True)  9.99 us
    all_to_all x1, starting transfers between devices, local(): came = lax.all_to_all(placed, PIPE, 0, 0, tiled=True)  9.13 us
    all_to_all x1, waiting for transfers between devices, local(): came = lax.all_to_all(placed, PIPE, 0, 0, tiled=True)  8.8 us
  transfers between devices with their start and end apart: 28, of which 10 were waited for; matrix products, arithmetic and copies ran while one was open for 4% of the time, Pallas kernels for 11%

profile of v2, /device:TPU:1, one launch (start us, length us, event | category | flops | bytes accessed | tf_op | source)
XLA Modules:
  0.0 190.1 jit_solution(3046689156540111489)
XLA Ops:
  0.6 7.4 %all-to-all-start = ((bf16[16,8,2048]{2,1,0:T(8,128)(2,1)}), bf16[16,8,2048]{2,1,0:T(8,128)(2,1)S(1)}, u32[]{:S(2)}, u32[]{:S(2)}) async-start(bf16[16,8,2048]{2,1,0:T(8,128)(2,1)} %bitcast.36), calls=%async_computation | async-start | bytes 1048576 | tf_op jit(solution)/shard_map/all_to_all | solution.py:270
  8.0 2.5 %collective-permute-start = (f32[2048]{0:T(1024)}, f32[2048]{0:T(1024)S(1)}, u32[]{:S(2)}, u32[]{:S(2)}) collective-permute-start(f32[2048]{0:T(1024)} %param.9), channel_id=1, source_target_pairs={{0,6},{1,7},{2,0},{3,1},{4,2},{5,3},{6,4},{7,5},{8,14},{9,15},{10,... | collective-permute-start | bytes 24584 | tf_op jit(solution)/shard_map/ppermute | solution.py:34
  19.1 10.0 %all-to-all-start.1 = ((bf16[64,16,640]{2,1,0:T(8,128)(2,1)}), bf16[64,16,640]{2,1,0:T(8,128)(2,1)S(1)}, u32[]{:S(2)}, u32[]{:S(2)}) async-start(bf16[64,16,640]{2,1,0:T(8,128)(2,1)} %shard_map.94), calls=%async_computation.1 | async-start | bytes 2621440 | tf_op jit(solution)/shard_map/all_to_all | solution.py:293
  29.1 2.6 %collective-permute-start.3 = (s32[2,128]{1,0:T(2,128)S(1)}, s32[2,128]{1,0:T(2,128)S(1)}, u32[]{:S(2)}, u32[]{:S(2)}) collective-permute-start(s32[2,128]{1,0:T(2,128)S(1)} %pad_add_fusion), channel_id=1, source_target_pairs={{0,1},{1,0},{2,3},{3,2},{4,5},{5,4},{6,7},{7,6},{8,9},{9,8},{10,11... | collective-permute-start | bytes 3080 | tf_op jit(solution)/shard_map/ppermute | solution.py:34
  35.2 13.9 %all-to-all-done.1.came = bf16[64,16,640]{2,1,0:T(8,128)(2,1)S(1)} async-done(((bf16[64,16,640]{2,1,0:T(8,128)(2,1)}), bf16[64,16,640]{2,1,0:T(8,128)(2,1)S(1)}, u32[]{:S(2)}, u32[]{:S(2)}) %all-to-all-start.1) | async-done | bytes 1310752 | tf_op jit(solution)/shard_map/all_to_all | solution.py:293
  54.7 3.4 %copy-done = bf16[512,8192]{1,0:T(8,128)(2,1)S(1)} copy-done((bf16[512,8192]{1,0:T(8,128)(2,1)S(1)}, bf16[512,8192]{1,0:T(8,128)(2,1)}, u32[]{:S(2)}) %copy-start) | copy-done | bytes 8388632
  60.0 5.3 %collective-permute-done.4.refs_0_.refs_1_ = bf16[4,256,512]{2,1,0:T(8,128)(2,1)S(1)} collective-permute-done((bf16[4,256,512]{2,1,0:T(8,128)(2,1)S(1)}, bf16[4,256,512]{2,1,0:T(8,128)(2,1)S(1)}, u32[]{:S(2)}, u32[]{:S(2)}) %collective-permute-start.4) | collective-permute-done | bytes 1048608 | tf_op jit(solution)/shard_map/ppermute | solution.py:34
  65.3 4.4 %collective-permute-start.7 = (bf16[4,256,512]{2,1,0:T(8,128)(2,1)S(1)}, bf16[4,256,512]{2,1,0:T(8,128)(2,1)S(1)}, u32[]{:S(2)}, u32[]{:S(2)}) collective-permute-start(bf16[4,256,512]{2,1,0:T(8,128)(2,1)S(1)} %collective-permute-done.4.refs_0_.refs_1_), channel_id=1, source_target_pairs={{0,8},{1,9},{2,10},{3,11},{4,12},{5,13},{6,14},{7,15},{8,0},{9,1},... | collective-permute-start | bytes 3145736 | tf_op jit(solution)/shard_map/ppermute | solution.py:34
  72.1 3.0 %shard_map.97.ours = f32[512,256]{1,0:T(8,128)S(1)} custom-call(s32[5]{0:T(128)S(1)} %pad_add_fusion.1.tint, bf16[512,8192]{1,0:T(8,128)(2,1)S(1)} %copy-done.1, bf16[4,256,512]{2,1,0:T(8,128)(2,1)S(1)} %collective-permute-done.4.refs_0_.refs_1_, bf16[4,256,512]{2,1,0:T(8,128)(2,1)S(1)} %collective-permute-done.5.refs_1_.refs_2_, ...), custom_call_target="tpu_custom_call" | custom-call | flops 1610612736 | bytes 6291456 | tf_op jit(solution)/shard_map/pallas_call | solution.py:58
  75.1 4.1 %shard_map.99 = (f32[512,512]{1,0:T(8,128)S(1)}, f32[128,4,128]{2,1,0:T(4,128)}, f32[512,256]{1,0:T(8,128)}) custom-call(s32[5]{0:T(128)S(1)} %pad_add_fusion.1.tint, bf16[512,8192]{1,0:T(8,128)(2,1)S(1)} %copy-done.1, bf16[4,256,512]{2,1,0:T(8,128)(2,1)S(1)} %collective-permute-done.7.block_1.refs_5_, ...), custom_call_target="tpu_custom_call" | custom-call | flops 1610612736 | bytes 9437184 | tf_op jit(solution)/shard_map/pallas_call | solution.py:58
  80.2 5.1 %all-to-all-start.2 = ((f32[128,4,128]{2,1,0:T(4,128)}), f32[128,4,128]{2,1,0:T(4,128)S(1)}, u32[]{:S(2)}, u32[]{:S(2)}) async-start(f32[128,4,128]{2,1,0:T(4,128)} %get-tuple-element.44.after), calls=%async_computation.2 | async-start | bytes 524288 | tf_op jit(solution)/shard_map/all_to_all | solution.py:305
  85.4 3.4 %copy-done.2 = bf16[512,8192]{1,0:T(8,128)(2,1)S(1)} copy-done((bf16[512,8192]{1,0:T(8,128)(2,1)S(1)}, bf16[512,8192]{1,0:T(8,128)(2,1)}, u32[]{:S(2)}) %copy-start.2) | copy-done | bytes 8388632
  89.3 3.4 %copy-done.3 = bf16[512,8192]{1,0:T(8,128)(2,1)} copy-done((bf16[512,8192]{1,0:T(8,128)(2,1)}, bf16[512,8192]{1,0:T(8,128)(2,1)S(1)}, u32[]{:S(2)}) %copy-start.3) | copy-done | bytes 8388632
  92.7 3.9 %all-to-all-done.2.parts = f32[128,4,128]{2,1,0:T(4,128)S(1)} async-done(((f32[128,4,128]{2,1,0:T(4,128)}), f32[128,4,128]{2,1,0:T(4,128)S(1)}, u32[]{:S(2)}, u32[]{:S(2)}) %all-to-all-start.2) | async-done | bytes 262176 | tf_op jit(solution)/shard_map/all_to_all | solution.py:305
  99.7 3.4 %copy-done.4 = bf16[512,8192]{1,0:T(8,128)(2,1)S(1)} copy-done((bf16[512,8192]{1,0:T(8,128)(2,1)S(1)}, bf16[512,8192]{1,0:T(8,128)(2,1)}, u32[]{:S(2)}) %copy-start.4) | copy-done | bytes 8388632
  108.4 2.3 %shard_map.104 = (f32[4,256,512]{2,1,0:T(8,128)S(1)}, bf16[4,256,512]{2,1,0:T(8,128)(2,1)S(1)}) custom-call(s32[5]{0:T(128)S(1)} %pad_add_fusion.1.tint, bf16[512,512]{1,0:T(8,128)(2,1)S(1)} %get-tuple-element.52.dlogits, bf16[512,8192]{1,0:T(8,128)(2,1)S(1)} %copy-done.4), custom_call_target="tpu_custom_call" | custom-call | flops 1073741824 | bytes 4194304 | tf_op jit(solution)/shard_map/pallas_call | solution.py:58
  115.9 2.3 %shard_map.103 = (f32[4,256,512]{2,1,0:T(8,128)S(1)}, bf16[4,256,512]{2,1,0:T(8,128)(2,1)S(1)}) custom-call(s32[5]{0:T(128)S(1)} %pad_add_fusion.1.tint, bf16[512,512]{1,0:T(8,128)(2,1)S(1)} %get-tuple-element.52.dlogits, bf16[512,8192]{1,0:T(8,128)(2,1)S(1)} %bitcast.31), custom_call_target="tpu_custom_call" | custom-call | flops 1073741824 | bytes 4194304 | tf_op jit(solution)/shard_map/pallas_call | solution.py:58
  118.3 8.5 %collective-permute-done.17 = bf16[4,256,512]{2,1,0:T(8,128)(2,1)S(1)} collective-permute-done((bf16[4,256,512]{2,1,0:T(8,128)(2,1)S(1)}, bf16[4,256,512]{2,1,0:T(8,128)(2,1)S(1)}, u32[]{:S(2)}, u32[]{:S(2)}) %collective-permute-start.17) | collective-permute-done | bytes 1048608 | tf_op jit(solution)/shard_map/ppermute | solution.py:34
  129.7 7.8 %all-to-all-start.3 = ((bf16[64,16,512]{2,1,0:T(8,128)(2,1)}), bf16[64,16,512]{2,1,0:T(8,128)(2,1)}, u32[]{:S(2)}, u32[]{:S(2)}) async-start(bf16[64,16,512]{2,1,0:T(8,128)(2,1)} %bitcast.35), calls=%async_computation.3 | async-start | bytes 2097152 | tf_op jit(solution)/shard_map/all_to_all | solution.py:316
  145.5 7.0 %shard_map.106 = bf16[512,8192]{1,0:T(8,128)(2,1)} custom-call(s32[5]{0:T(128)S(1)} %pad_add_fusion.1.tint, bf16[512,512]{1,0:T(8,128)(2,1)S(1)} %copy-done.18, bf16[4,256,512]{2,1,0:T(8,128)(2,1)S(1)} %get-tuple-element.38.refs_0_, bf16[4,256,512]{2,1,0:T(8,128)(2,1)S(1)} %collective-permute-done.4.refs_0_.refs_1_, ...), custom_call_target="tpu_custom_call" | custom-call | flops 4294967296 | bytes 17825792 | tf_op jit(solution)/shard_map/pallas_call | solution.py:209
  158.7 2.6 %collective-permute-start.21 = (f32[8,256]{1,0:T(8,128)S(1)}, f32[8,256]{1,0:T(8,128)S(1)}, u32[]{:S(2)}, u32[]{:S(2)}) collective-permute-start(f32[8,256]{1,0:T(8,128)S(1)} %get-tuple-element.66.gain), channel_id=1, source_target_pairs={{0,1},{1,0},{2,3},{3,2},{4,5},{5,4},{6,7},{7,6},{8,9},{9,8},{10,11... | collective-permute-start | bytes 24584 | tf_op jit(solution)/shard_map/ppermute | solution.py:34
  164.3 9.1 %all-to-all-start.4 = ((bf16[16,8,2560]{2,1,0:T(8,128)(2,1)}), bf16[16,8,2560]{2,1,0:T(8,128)(2,1)S(1)}, u32[]{:S(2)}, u32[]{:S(2)}) async-start(bf16[16,8,2560]{2,1,0:T(8,128)(2,1)} %shard_map.108), calls=%async_computation.4 | async-start | bytes 1310720 | tf_op jit(solution)/shard_map/all_to_all | solution.py:326
  175.5 8.8 %all-to-all-done.4 = bf16[16,8,2560]{2,1,0:T(8,128)(2,1)S(1)} async-done(((bf16[16,8,2560]{2,1,0:T(8,128)(2,1)}), bf16[16,8,2560]{2,1,0:T(8,128)(2,1)S(1)}, u32[]{:S(2)}, u32[]{:S(2)}) %all-to-all-start.4) | async-done | bytes 655392 | tf_op jit(solution)/shard_map/all_to_all | solution.py:326
  184.9 4.2 %collective-permute-done.22 = bf16[1,128,2048]{2,1,0:T(8,128)(2,1)S(1)} collective-permute-done((bf16[1,128,2048]{2,1,0:T(8,128)(2,1)S(1)}, bf16[1,128,2048]{2,1,0:T(8,128)(2,1)S(1)}, u32[]{:S(2)}, u32[]{:S(2)}) %collective-permute-start.22) | collective-permute-done | bytes 524320 | tf_op jit(solution)/shard_map/ppermute | solution.py:34
  (135 shorter events, 56.8 us)
Async XLA Ops:
  0.6 17.2 %all-to-all-start = ((bf16[16,8,2048]{2,1,0:T(8,128)(2,1)}), bf16[16,8,2048]{2,1,0:T(8,128)(2,1)S(1)}, u32[]{:S(2)}, u32[]{:S(2)}) async-start(bf16[16,8,2048]{2,1,0:T(8,128)(2,1)} %bitcast.36), calls=%async_computation | async-start | bytes 1048576 | tf_op jit(solution)/shard_map/all_to_all | solution.py:270
  8.0 8.8 %collective-permute-start = (f32[2048]{0:T(1024)}, f32[2048]{0:T(1024)S(1)}, u32[]{:S(2)}, u32[]{:S(2)}) collective-permute-start(f32[2048]{0:T(1024)} %param.9), channel_id=1, source_target_pairs={{0,6},{1,7},{2,0},{3,1},{4,2},{5,3},{6,4},{7,5},{8,14},{9,15},{10,... | collective-permute-start | bytes 24584 | tf_op jit(solution)/shard_map/ppermute | solution.py:34
  10.5 6.3 %collective-permute-start.1 = (f32[2048]{0:T(1024)}, f32[2048]{0:T(1024)S(1)}, u32[]{:S(2)}, u32[]{:S(2)}) collective-permute-start(f32[2048]{0:T(1024)} %param.9), channel_id=1, source_target_pairs={{0,4},{1,5},{2,6},{3,7},{4,0},{5,1},{6,2},{7,3},{8,12},{9,13},{10,... | collective-permute-start | bytes 24584 | tf_op jit(solution)/shard_map/ppermute | solution.py:34
  11.0 5.8 %collective-permute-start.2 = (f32[2048]{0:T(1024)}, f32[2048]{0:T(1024)S(1)}, u32[]{:S(2)}, u32[]{:S(2)}) collective-permute-start(f32[2048]{0:T(1024)} %param.9), channel_id=1, source_target_pairs={{0,2},{1,3},{2,4},{3,5},{4,6},{5,7},{6,0},{7,1},{8,10},{9,11},{10,... | collective-permute-start | bytes 24584 | tf_op jit(solution)/shard_map/ppermute | solution.py:34
  19.1 30.0 %all-to-all-start.1 = ((bf16[64,16,640]{2,1,0:T(8,128)(2,1)}), bf16[64,16,640]{2,1,0:T(8,128)(2,1)S(1)}, u32[]{:S(2)}, u32[]{:S(2)}) async-start(bf16[64,16,640]{2,1,0:T(8,128)(2,1)} %shard_map.94), calls=%async_computation.1 | async-start | bytes 2621440 | tf_op jit(solution)/shard_map/all_to_all | solution.py:293
  29.1 5.7 %collective-permute-start.3 = (s32[2,128]{1,0:T(2,128)S(1)}, s32[2,128]{1,0:T(2,128)S(1)}, u32[]{:S(2)}, u32[]{:S(2)}) collective-permute-start(s32[2,128]{1,0:T(2,128)S(1)} %pad_add_fusion), channel_id=1, source_target_pairs={{0,1},{1,0},{2,3},{3,2},{4,5},{5,4},{6,7},{7,6},{8,9},{9,8},{10,11... | collective-permute-start | bytes 3080 | tf_op jit(solution)/shard_map/ppermute | solution.py:34
  50.1 15.2 %collective-permute-start.4 = (bf16[4,256,512]{2,1,0:T(8,128)(2,1)S(1)}, bf16[4,256,512]{2,1,0:T(8,128)(2,1)S(1)}, u32[]{:S(2)}, u32[]{:S(2)}) collective-permute-start(bf16[4,256,512]{2,1,0:T(8,128)(2,1)S(1)} %get-tuple-element.38.refs_0_), channel_id=1, source_target_pairs={{0,6},{1,7},{2,0},{3,1},{4,2},{5,3},{6,4},{7,5},{8,24},{9,25},{10,... | collective-permute-start | bytes 3145736 | tf_op jit(solution)/shard_map/ppermute | solution.py:34
  50.2 15.1 %collective-permute-start.5 = (bf16[4,256,512]{2,1,0:T(8,128)(2,1)S(1)}, bf16[4,256,512]{2,1,0:T(8,128)(2,1)S(1)}, u32[]{:S(2)}, u32[]{:S(2)}) collective-permute-start(bf16[4,256,512]{2,1,0:T(8,128)(2,1)S(1)} %get-tuple-element.38.refs_0_), channel_id=1, source_target_pairs={{0,32},{1,33},{2,34},{3,35},{4,36},{5,37},{6,38},{7,39},{8,104},{9... | collective-permute-start | bytes 3145736 | tf_op jit(solution)/shard_map/ppermute | solution.py:34
  50.8 14.5 %collective-permute-start.6 = (bf16[4,256,512]{2,1,0:T(8,128)(2,1)S(1)}, bf16[4,256,512]{2,1,0:T(8,128)(2,1)S(1)}, u32[]{:S(2)}, u32[]{:S(2)}) collective-permute-start(bf16[4,256,512]{2,1,0:T(8,128)(2,1)S(1)} %get-tuple-element.38.refs_0_), channel_id=1, source_target_pairs={{0,2},{1,3},{2,4},{3,5},{4,6},{5,7},{6,0},{7,1},{8,25},{9,24},{10,... | collective-permute-start | bytes 3145736 | tf_op jit(solution)/shard_map/ppermute | solution.py:34
  52.8 17.4 %collective-permute-start.10 = (bf16[4,256,512]{2,1,0:T(8,128)(2,1)S(1)}, bf16[4,256,512]{2,1,0:T(8,128)(2,1)S(1)}, u32[]{:S(2)}, u32[]{:S(2)}) collective-permute-start(bf16[4,256,512]{2,1,0:T(8,128)(2,1)S(1)} %get-tuple-element.38.refs_0_), channel_id=1, source_target_pairs={{0,8},{1,9},{2,10},{3,11},{4,12},{5,13},{6,14},{7,15},{8,0},{9,1},... | collective-permute-start | bytes 3145736 | tf_op jit(solution)/shard_map/ppermute | solution.py:34
  65.3 9.8 %collective-permute-start.7 = (bf16[4,256,512]{2,1,0:T(8,128)(2,1)S(1)}, bf16[4,256,512]{2,1,0:T(8,128)(2,1)S(1)}, u32[]{:S(2)}, u32[]{:S(2)}) collective-permute-start(bf16[4,256,512]{2,1,0:T(8,128)(2,1)S(1)} %collective-permute-done.4.refs_0_.refs_1_), channel_id=1, source_target_pairs={{0,8},{1,9},{2,10},{3,11},{4,12},{5,13},{6,14},{7,15},{8,0},{9,1},... | collective-permute-start | bytes 3145736 | tf_op jit(solution)/shard_map/ppermute | solution.py:34
  69.7 5.4 %collective-permute-start.8 = (bf16[4,256,512]{2,1,0:T(8,128)(2,1)S(1)}, bf16[4,256,512]{2,1,0:T(8,128)(2,1)S(1)}, u32[]{:S(2)}, u32[]{:S(2)}) collective-permute-start(bf16[4,256,512]{2,1,0:T(8,128)(2,1)S(1)} %collective-permute-done.5.refs_1_.refs_2_), channel_id=1, source_target_pairs={{0,8},{1,9},{2,10},{3,11},{4,12},{5,13},{6,14},{7,15},{8,0},{9,1},... | collective-permute-start | bytes 3145736 | tf_op jit(solution)/shard_map/ppermute | solution.py:34
  69.8 5.3 %collective-permute-start.9 = (bf16[4,256,512]{2,1,0:T(8,128)(2,1)S(1)}, bf16[4,256,512]{2,1,0:T(8,128)(2,1)S(1)}, u32[]{:S(2)}, u32[]{:S(2)}) collective-permute-start(bf16[4,256,512]{2,1,0:T(8,128)(2,1)S(1)} %collective-permute-done.6.refs_2_.refs_3_), channel_id=1, source_target_pairs={{0,8},{1,9},{2,10},{3,11},{4,12},{5,13},{6,14},{7,15},{8,0},{9,1},... | collective-permute-start | bytes 3145736 | tf_op jit(solution)/shard_map/ppermute | solution.py:34
  80.2 16.4 %all-to-all-start.2 = ((f32[128,4,128]{2,1,0:T(4,128)}), f32[128,4,128]{2,1,0:T(4,128)S(1)}, u32[]{:S(2)}, u32[]{:S(2)}) async-start(f32[128,4,128]{2,1,0:T(4,128)} %get-tuple-element.44.after), calls=%async_computation.2 | async-start | bytes 524288 | tf_op jit(solution)/shard_map/all_to_all | solution.py:305
  105.4 5.8 %collective-permute-start.11 = (bf16[4,256,512]{2,1,0:T(8,128)(2,1)S(1)}, bf16[4,256,512]{2,1,0:T(8,128)(2,1)S(1)}, u32[]{:S(2)}, u32[]{:S(2)}) collective-permute-start(bf16[4,256,512]{2,1,0:T(8,128)(2,1)S(1)} %get-tuple-element.51), channel_id=1, source_target_pairs={{0,8},{1,9},{2,10},{3,11},{4,12},{5,13},{6,14},{7,15},{8,0},{9,1},... | collective-permute-start | bytes 3145736 | tf_op jit(solution)/shard_map/ppermute | solution.py:34
  111.6 15.2 %collective-permute-start.17 = (bf16[4,256,512]{2,1,0:T(8,128)(2,1)S(1)}, bf16[4,256,512]{2,1,0:T(8,128)(2,1)S(1)}, u32[]{:S(2)}, u32[]{:S(2)}) collective-permute-start(bf16[4,256,512]{2,1,0:T(8,128)(2,1)S(1)} %add_convert_fusion.3), channel_id=1, source_target_pairs={{0,6},{1,7},{2,0},{3,1},{4,2},{5,3},{6,4},{7,5},{8,24},{9,25},{10,... | collective-permute-start | bytes 3145736 | tf_op jit(solution)/shard_map/ppermute | solution.py:34
  112.6 14.2 %collective-permute-start.16 = (bf16[4,256,512]{2,1,0:T(8,128)(2,1)S(1)}, bf16[4,256,512]{2,1,0:T(8,128)(2,1)S(1)}, u32[]{:S(2)}, u32[]{:S(2)}) collective-permute-start(bf16[4,256,512]{2,1,0:T(8,128)(2,1)S(1)} %add_convert_fusion.1), channel_id=1, source_target_pairs={{0,32},{1,33},{2,34},{3,35},{4,36},{5,37},{6,38},{7,39},{8,104},{9... | collective-permute-start | bytes 3145736 | tf_op jit(solution)/shard_map/ppermute | solution.py:34
  114.0 14.0 %collective-permute-start.14 = (bf16[4,256,512]{2,1,0:T(8,128)(2,1)S(1)}, bf16[4,256,512]{2,1,0:T(8,128)(2,1)S(1)}, u32[]{:S(2)}, u32[]{:S(2)}) collective-permute-start(bf16[4,256,512]{2,1,0:T(8,128)(2,1)S(1)} %add_convert_fusion.2), channel_id=1, source_target_pairs={{0,2},{1,3},{2,4},{3,5},{4,6},{5,7},{6,0},{7,1},{8,25},{9,24},{10,... | collective-permute-start | bytes 3145736 | tf_op jit(solution)/shard_map/ppermute | solution.py:34
  118.2 9.8 %collective-permute-start.12 = (bf16[4,256,512]{2,1,0:T(8,128)(2,1)S(1)}, bf16[4,256,512]{2,1,0:T(8,128)(2,1)S(1)}, u32[]{:S(2)}, u32[]{:S(2)}) collective-permute-start(bf16[4,256,512]{2,1,0:T(8,128)(2,1)S(1)} %get-tuple-element.54), channel_id=1, source_target_pairs={{0,8},{1,9},{2,10},{3,11},{4,12},{5,13},{6,14},{7,15},{8,0},{9,1},... | collective-permute-start | bytes 3145736 | tf_op jit(solution)/shard_map/ppermute | solution.py:34
  129.7 24.5 %all-to-all-start.3 = ((bf16[64,16,512]{2,1,0:T(8,128)(2,1)}), bf16[64,16,512]{2,1,0:T(8,128)(2,1)}, u32[]{:S(2)}, u32[]{:S(2)}) async-start(bf16[64,16,512]{2,1,0:T(8,128)(2,1)} %bitcast.35), calls=%async_computation.3 | async-start | bytes 2097152 | tf_op jit(solution)/shard_map/all_to_all | solution.py:316
  155.7 5.6 %collective-permute-start.18 = (f32[16,128]{1,0:T(8,128)S(1)}, f32[16,128]{1,0:T(8,128)S(1)}, u32[]{:S(2)}, u32[]{:S(2)}) collective-permute-start(f32[16,128]{1,0:T(8,128)S(1)} %get-tuple-element.65.inner), channel_id=1, source_target_pairs={{0,2},{1,3},{2,4},{3,5},{4,6},{5,7},{6,0},{7,1},{8,10},{9,11},{10,... | collective-permute-start | bytes 24584 | tf_op jit(solution)/shard_map/ppermute | solution.py:34
  156.2 5.1 %collective-permute-start.19 = (f32[16,128]{1,0:T(8,128)S(1)}, f32[16,128]{1,0:T(8,128)S(1)}, u32[]{:S(2)}, u32[]{:S(2)}) collective-permute-start(f32[16,128]{1,0:T(8,128)S(1)} %get-tuple-element.65.inner), channel_id=1, source_target_pairs={{0,4},{1,5},{2,6},{3,7},{4,0},{5,1},{6,2},{7,3},{8,12},{9,13},{10,... | collective-permute-start | bytes 24584 | tf_op jit(solution)/shard_map/ppermute | solution.py:34
  164.3 20.0 %all-to-all-start.4 = ((bf16[16,8,2560]{2,1,0:T(8,128)(2,1)}), bf16[16,8,2560]{2,1,0:T(8,128)(2,1)S(1)}, u32[]{:S(2)}, u32[]{:S(2)}) async-start(bf16[16,8,2560]{2,1,0:T(8,128)(2,1)} %shard_map.108), calls=%async_computation.4 | async-start | bytes 1310720 | tf_op jit(solution)/shard_map/all_to_all | solution.py:326
  173.4 15.7 %collective-permute-start.22 = (bf16[1,128,2048]{2,1,0:T(8,128)(2,1)S(1)}, bf16[1,128,2048]{2,1,0:T(8,128)(2,1)S(1)}, u32[]{:S(2)}, u32[]{:S(2)}) collective-permute-start(bf16[1,128,2048]{2,1,0:T(8,128)(2,1)S(1)} %copy-done.23), channel_id=1, source_target_pairs={{8,0},{9,1},{10,2},{11,3},{12,4},{13,5},{14,6},{15,7},{16,8},{17,9... | collective-permute-start | bytes 1572872 | tf_op jit(solution)/shard_map/ppermute | solution.py:34
  (30 other events, 136.6 us)

commit v3 on v2

--- a/solution.py
+++ b/solution.py
@@ -101,10 +101,47 @@
     return call(norm_kernel, None, [came, gain], [((4, 256, 512), BF16), ((256, 128), F32, True)], moved=2 << 20)
 
 
-def add_up(tint, aways, head, blocks, total):
+def near_columns(t, away):
+    return away * 4 + t
+
+
+def fetch_columns(head, near, sems, tint, aways):
+    copies = []
+    for away in aways:
+        for t in range(4):
+            at = near_columns(t, away)
+            copies.append(pltpu.make_async_copy(head.at[:, columns(tint, t, away)], near.at[at], sems.at[at]))
+            copies[-1].start()
+    return copies
+
+
+def early_kernel(tint, head, block, near, total, sems):
+    copies = fetch_columns(head, near, sems, tint, range(4))
+    for t in range(4):
+        copies[t].wait()
+        part = lax.dot_general(near[near_columns(t, 0)], block[t], NT, preferred_element_type=F32)
+        total[...] = part if t == 0 else total[...] + part
+    for copy in copies[4:]:
+        copy.wait()
+
+
+def early_call(tint, head, block):
+    vmem = pl.BlockSpec(memory_space=pltpu.VMEM)
+    return pl.pallas_call(
+        early_kernel,
+        in_specs=[pl.BlockSpec(memory_space=pltpu.SMEM), pl.BlockSpec(memory_space=pl.ANY), vmem],
+        out_specs=[vmem] * 2,
+        out_shape=[pltpu.VMEM((16, 512, 512), BF16), pltpu.VMEM((512, 256), F32)],
+        scratch_shapes=[pltpu.SemaphoreType.DMA((16,))],
+        cost_estimate=pl.CostEstimate(flops=2 * 512 * 256 * 2048, bytes_accessed=9 << 20, transcendentals=0),
+        compiler_params=pltpu.CompilerParams(vmem_limit_bytes=LIMIT),
+    )(tint, head, pltpu.with_memory_space_constraint(block, pltpu.VMEM))
+
+
+def add_up(aways, near, blocks, total):
     def part(t):
         return sum(
-            lax.dot_general(head[:, columns(tint, t, away)], block[t], NT, preferred_element_type=F32)
+            lax.dot_general(near[near_columns(t, away)], block[t], NT, preferred_element_type=F32)
             for away, block in zip(aways, blocks)
         )
 
@@ -115,18 +152,18 @@
         total[...] += part(t)
 
 
-def logits_kernel(aways, tint, head, *refs):
-    add_up(tint, aways, head, refs[:-1], refs[-1])
-
-
-def logits_call(tint, head, aways, blocks):
+def logits_kernel(aways, near, *refs):
+    add_up(aways, near, refs[:-1], refs[-1])
+
+
+def logits_call(near, aways, blocks):
     flops = 2 * 512 * 256 * 2048 * len(aways)
     kernel = functools.partial(logits_kernel, aways)
-    return call(kernel, tint, [head, *blocks], [((512, 256), F32)], flops, len(aways) << 21)[0]
-
-
-def last_kernel(tint, head, block_1, block_2, block_3, early, ours, theirs, logits, lse, total):
-    add_up(tint, (1, 2, 3), head, (block_1, block_2, block_3), total)
+    return call(kernel, None, [near, *blocks], [((512, 256), F32)], flops, len(aways) << 21)[0]
+
+
+def last_kernel(core, near, block_1, block_2, block_3, early, ours, theirs, logits, lse, total):
+    add_up((1, 2, 3), near, (block_1, block_2, block_3), total)
     logits[:, :256] = early[...] + ours[...]
     logits[:, 256:] = theirs[...] + total[...]
     values = logits[...]
@@ -135,64 +172,74 @@
     quarters = [sums[:, i * 128 : (i + 1) * 128] for i in range(4)]
     in_order = jnp.concatenate(quarters, axis=0)
     swapped = jnp.concatenate(quarters[2:] + quarters[:2], axis=0)
-    lse[...] = jnp.broadcast_to(jnp.where(tint[4] == 0, in_order, swapped)[None], (128, 4, 128))
-
-
-def last_call(tint, head, blocks, early, ours, theirs):
-    outs = [((512, 512), F32), ((128, 4, 128), F32, True), ((512, 256), F32)]
-    return call(last_kernel, tint, [head, *blocks, early, ours, theirs], outs, 6 * 512 * 256 * 2048, 9 << 20)[:2]
-
-
-def dlogits_kernel(place, logits, parts, labels, weights, turned, dlogits):
+    lse[...] = jnp.broadcast_to(jnp.where(core[4] == 0, in_order, swapped)[None], (128, 4, 128))
+
+
+def last_call(tint, near, blocks, early, ours, theirs):
+    outs = [((512, 512), F32, True), ((128, 4, 128), F32, True), ((512, 256), F32)]
+    return call(last_kernel, tint, [near, *blocks, early, ours, theirs], outs, 6 * 512 * 256 * 2048, 9 << 20)[:2]
+
+
+def turn_kernel(info, logits, head, parts, labels, weights, turned, dlogits, inner, near, own, other, held, sems):
+    first = pltpu.make_async_copy(logits, held, sems.at[16])
+    first.start()
+    copies = fetch_columns(head, near, sems, info, (1, 2, 3, 0))
     lse = parts[...]
     top = jnp.max(lse, axis=0)
     log_total = top + jnp.log(jnp.sum(jnp.exp(lse - top[None]), axis=0))
     quarters = [log_total[i : i + 1] for i in range(4)]
     in_order = jnp.concatenate(quarters, axis=1)
     swapped = jnp.concatenate(quarters[2:] + quarters[:2], axis=1)
-    probs = jnp.exp(logits[...] - jnp.where(place[1] == 0, in_order, swapped))
-    ids = place[0] * 512 + lax.broadcasted_iota(jnp.int32, (512, 512), 0)
+    log_total = jnp.where(info[4] == 0, in_order, swapped)
+    first.wait()
+    probs = jnp.exp(held[...] - log_total)
+    ids = info[5] * 512 + lax.broadcasted_iota(jnp.int32, (512, 512), 0)
     hot = jnp.where(ids == labels[...], 1.0, 0.0)
     values = (weights[...] * (probs - hot)).astype(BF16)
     turned[...] = values
     dlogits[...] = values.T
-
-
-def dlogits_call(place, logits, parts, labels, weights):
-    outs = [((512, 512), BF16)] * 2
-    return call(dlogits_kernel, place, [logits, parts, labels, weights], outs, moved=3 << 20)
-
-
-def fetch_kernel(after, source, out, sem):
-    copy = pltpu.make_async_copy(source, out, sem)
-    copy.start()
-    copy.wait()
-
-
-def fetch(source, after):
+    inner[...] = jnp.sum(values.astype(F32) * held[...], axis=0, keepdims=True)
+    for t in range(4):
+        copies[t].wait()
+        value = jnp.dot(dlogits[...], near[near_columns(t, 1)], preferred_element_type=F32)
+        own[t] = value[:256]
+        other[t] = value[256:].astype(BF16)
+    for copy in copies[4:]:
+        copy.wait()
+
+
+def turn_call(info, logits, head, parts, labels, weights):
+    vmem, anywhere = pl.BlockSpec(memory_space=pltpu.VMEM), pl.BlockSpec(memory_space=pl.ANY)
     return pl.pallas_call(
-        fetch_kernel,
-        in_specs=[pl.BlockSpec(memory_space=pl.ANY)] * 2,
-        out_specs=pl.BlockSpec(memory_space=pltpu.VMEM),
-        out_shape=pltpu.VMEM(source.shape, source.dtype),
-        scratch_shapes=[pltpu.SemaphoreType.DMA],
-        cost_estimate=pl.CostEstimate(flops=0, bytes_accessed=8 << 20, transcendentals=0),
+        turn_kernel,
+        in_specs=[pl.BlockSpec(memory_space=pltpu.SMEM), anywhere, anywhere, vmem, vmem, vmem],
+        out_specs=[vmem] * 6,
+        out_shape=[
+            jax.ShapeDtypeStruct((512, 512), BF16),
+            pltpu.VMEM((512, 512), BF16),
+            jax.ShapeDtypeStruct((1, 512), F32),
+            pltpu.VMEM((16, 512, 512), BF16),
+            pltpu.VMEM((4, 256, 512), F32),
+            pltpu.VMEM((4, 256, 512), BF16),
+        ],
+        scratch_shapes=[pltpu.VMEM((512, 512), F32), pltpu.SemaphoreType.DMA((17,))],
+        cost_estimate=pl.CostEstimate(flops=2 * 512 * 512 * 2048, bytes_accessed=9 << 20, transcendentals=0),
         compiler_params=pltpu.CompilerParams(vmem_limit_bytes=LIMIT),
-    )(after, source)
-
-
-def back_kernel(away, tint, dlogits, head, own, other):
+    )(info, logits, head, parts, labels, weights)
+
+
+def back_kernel(away, dlogits, near, own, other):
     @pl.loop(0, 4)
     def _(t):
-        value = jnp.dot(dlogits[...], head[:, columns(tint, t, away)], preferred_element_type=F32)
+        value = jnp.dot(dlogits[...], near[near_columns(t, away)], preferred_element_type=F32)
         own[t] = value[:256]
         other[t] = value[256:].astype(BF16)
 
 
-def back_call(tint, dlogits, head, away):
+def back_call(dlogits, near, away):
     kernel = functools.partial(back_kernel, away)
     outs = [((4, 256, 512), F32), ((4, 256, 512), BF16)]
-    return call(kernel, tint, [dlogits, head], outs, 2 * 512 * 512 * 2048, 4 << 20)
+    return call(kernel, None, [dlogits, near], outs, 2 * 512 * 512 * 2048, 4 << 20)
 
 
 def head_kernel(tint, turned, *refs):
@@ -220,44 +267,57 @@
     )(tint, turned, *own, *other)
 
 
-def tail_kernel(terms, rows, inverse_rms, gain, gated, unit, inner, gain_part):
+def three_parts(value):
+    high = value.astype(BF16).astype(F32)
+    middle = (value - high).astype(BF16).astype(F32)
+    return high, middle, value - high - middle
+
+
+def join_kernel(came, inverse_rms, ours, swapped, one, two, three, inner, out):
+    products = [part[i : i + 1] for part in three_parts(inner[...]) for i in range(2)]
+    for t in range(4):
+        gain = jnp.zeros((1, 512), F32)
+        for group in range(16):
+            span = slice(group * 16, (group + 1) * 16)
+            total = ours[t, span] + swapped[t, span].astype(F32)
+            total += one[t, span].astype(F32) + two[t, span].astype(F32) + three[t, span].astype(F32)
+            out[t * 16 + group, :, :512] = total.astype(BF16)
+            unit = came[t * 16 + group, :, :512].astype(F32) * inverse_rms[span, :1]
+            gain += jnp.sum(total * unit, axis=0, keepdims=True)
+        parts = [part[:, i * 128 : (i + 1) * 128] for part in three_parts(gain)[:2] for i in range(4)]
+        extra = jnp.concatenate(parts + products + [jnp.zeros((2, 128), F32)], axis=0).astype(BF16)
+        for group in range(16):
+            out[t * 16 + group, :, 512:] = extra
+
+
+def join_call(*operands):
+    return call(join_kernel, None, operands, [((64, 16, 640), BF16, True)], moved=6 << 20)[0]
+
+
+def tail_kernel(info, terms, rows, inverse_rms, gain, placed, gain_grad):
     sums = [None] * 4
     for chip, colour in enumerate(COLOURS):
         term = terms[chip].astype(F32)
         sums[colour] = term if sums[colour] is None else sums[colour] + term
+    products = sum(s[8:14, 512:] for s in sums)
+    lane = lax.broadcasted_iota(jnp.int32, (16, 128), 1)
+    row = info[2] * 16 + lax.broadcasted_iota(jnp.int32, (16, 128), 0)
+    here = [jnp.where(lane + 128 * (i % 2) == row, products[i : i + 1], 0.0) for i in range(6)]
+    inner = jnp.sum(sum(here), axis=1, keepdims=True) / 8192
     inverse = inverse_rms[:, :1]
-    total = jnp.zeros((16, 1), F32)
-    for colour, grad in enumerate(sums):
+    for colour, total in enumerate(sums):
         span = slice(colour * 512, (colour + 1) * 512)
-        ours = rows[:, span].astype(F32) * inverse
-        scaled = grad * gain[:, span]
-        unit[:, span] = ours
-        gated[:, span] = scaled
-        total += jnp.sum(scaled * ours, axis=1, keepdims=True)
-        part = jnp.sum(grad * ours, axis=0, keepdims=True)
-        for i in range(2):
-            gain_part[colour * 2 + i : colour * 2 + i + 1, :] = part[:, i * 256 : (i + 1) * 256]
-    inner[...] = jnp.broadcast_to(total, (16, 128))
-
-
-def tail_call(terms, rows, inverse_rms, gain):
-    outs = [((16, 2048), F32), ((16, 2048), F32), ((16, 128), F32), ((8, 256), F32)]
-    return call(tail_kernel, None, [terms, rows, inverse_rms, gain], outs, moved=2 << 20)
-
-
-def exit_kernel(chosen, gated, unit, inverse_rms, inner, inner_1, inner_2, inner_3, gain, gain_1, out):
-    total = (inner[...] + inner_1[...] + inner_2[...] + inner_3[...])[:, :1] / 8192
-    grad = inverse_rms[:, :1] * (gated[...] - unit[...] * total)
-    sums = gain[...] + gain_1[...]
-    high = sums.astype(BF16).astype(F32)
-    low = sums - high
-    for section in range(16):
-        value = jnp.where(chosen[0] == section, grad[:8], jnp.where(chosen[1] == section, grad[8:], 0.0))
-        out[section] = jnp.concatenate([value, high, low], axis=1).astype(BF16)
-
-
-def exit_call(chosen, *operands):
-    return call(exit_kernel, chosen, operands, [((16, 8, 2560), BF16, True)])[0]
+        gain_grad[colour * 4 : (colour + 1) * 4, :] = total[:4, 512:] + total[4:8, 512:]
+        unit = rows[:, span].astype(F32) * inverse
+        exit_grad = inverse * (total[:, :512] * gain[:, span] - unit * inner)
+        for section in range(16):
+            value = jnp.where(info[0] == section, exit_grad[:8], jnp.where(info[1] == section, exit_grad[8:], 0.0))
+            placed[section, :, span] = value.astype(BF16)
+
+
+def tail_call(info, *operands):
+    outs = [((16, 8, 2048), BF16, True), ((16, 128), F32)]
+    return call(tail_kernel, info, operands, outs, moved=2 << 20)
 
 
 def local(hidden, section_cotangent, norm_gain, head, labels, loss_mask, exit_on):
@@ -265,7 +325,7 @@
     device = lax.axis_index(AXES).astype(jnp.int32)
     colour = (x + 2 * y + 3 * (2 * zh + zl)) % 4
     aways = (colour + jnp.arange(4, dtype=jnp.int32)) % 4
-    tint = jnp.concatenate([aways, core.reshape(1)]).astype(jnp.int32)
+    tint = jnp.concatenate([aways, core.reshape(1), device.reshape(1)]).astype(jnp.int32)
 
     came = lax.all_to_all(hidden.reshape(16, 8, 2048), PIPE, 0, 0, tiled=True)
     section_ids = jnp.arange(16, dtype=jnp.int32)
@@ -296,37 +356,34 @@
 
     blocks = [own, to_colour(own, 3), to_colour(own, 2), to_colour(own, 1)]
     first_mate = other_core(own)
-    early = logits_call(tint, head, (0,), blocks[:1])
-    blocks[1], blocks[2], blocks[3], early = lax.optimization_barrier((*blocks[1:], early))
+    near, early = early_call(tint, head, own)
+    theirs = logits_call(near, (0,), [first_mate])
+    blocks[1], blocks[2], blocks[3], early, theirs = lax.optimization_barrier((*blocks[1:], early, theirs))
     mates = [first_mate] + [other_core(b) for b in blocks[1:]]
-    theirs = logits_call(tint, head, (0,), mates[:1])
-    ours = logits_call(tint, head, (1, 2, 3), blocks[1:])
-    logits, lse = last_call(tint, head, mates[1:], early, ours, theirs)
+    ours = logits_call(near, (1, 2, 3), blocks[1:])
+    logits, lse = last_call(tint, near, mates[1:], early, ours, theirs)
     parts = lax.all_to_all(lse, AXES, 0, 0, tiled=True)
-    near = fetch(head, lse)
-    parts, near = lax.optimization_barrier((parts, near))
-    turned, dlogits = dlogits_call(jnp.stack([device, core]), logits, parts, row_labels, row_weights)
-
-    halves = [back_call(tint, dlogits, near, away) for away in (1, 2, 3)]
+    turned, dlogits, inner, near, *first_half = turn_call(tint, logits, head, parts, row_labels, row_weights)
+
+    halves = [first_half] + [back_call(dlogits, near, away) for away in (2, 3)]
     sums = [(ours + other_core(theirs).astype(F32)).astype(BF16) for ours, theirs in halves]
     arrived = [to_colour(s, away) for s, away in zip(sums, (1, 2, 3))]
-    late, _ = lax.optimization_barrier((dlogits, sums[2]))
-    ours, theirs = back_call(tint, late, near, 0)
-    quarter = ours + other_core(theirs).astype(F32) + sum(a.astype(F32) for a in arrived)
-    terms = lax.all_to_all(quarter.astype(BF16).reshape(64, 16, 512), CHIPS, 0, 0, tiled=True)
+    late, inner, _ = lax.optimization_barrier((dlogits, inner, sums[2]))
+    ours, theirs = back_call(late, near, 0)
+    inner = inner.reshape(2, 2, 128)
+    inner = inner[0] + other_core(inner[1])
+    slots = join_call(quarter, inverse_rms, ours, other_core(theirs), *arrived, inner)
+    terms = lax.all_to_all(slots, CHIPS, 0, 0, tiled=True)
     head_grad = head_call(tint, turned, blocks, mates)
-    terms, head_grad = lax.optimization_barrier((terms, head_grad))
-
     place = (y * 2 + zl) * 2 + zh
     inverse_here = lax.dynamic_slice_in_dim(inverse_rms, place * 16, 16, 0)
-    gated, unit, inner, gain_part = tail_call(terms, rows, inverse_here, norm_gain.reshape(1, 2048))
-    inners = [inner] + [move(inner, lambda y, z, c, x, k=k: (y, z, c, x + k)) for k in (1, 2, 3)]
-    gain_other = move(gain_part, lambda y, z, c, x: (y, z + 2, c, x))
-    placed = exit_call(chosen, gated, unit, inverse_here, *inners, gain_part, gain_other)
+    terms, head_grad, inverse_here = lax.optimization_barrier((terms, head_grad, inverse_here))
+    info = jnp.concatenate([chosen, place.reshape(1)]).astype(jnp.int32)
+    placed, gain_grad = tail_call(info, terms, rows, inverse_here, norm_gain.reshape(1, 2048))
     came = lax.all_to_all(placed, PIPE, 0, 0, tiled=True)
-    gain_grad = jnp.sum(came[:, :, 2048:].astype(F32).reshape(16, 8, 2, 256), axis=(0, 2)).reshape(2048)
+    gain_grad = (gain_grad + other_core(gain_grad)).reshape(2048)
     from_next = move(section_cotangent, back_one)
-    residual_grad = (came[:, :, :2048].reshape(1, 128, 2048).astype(F32) + from_next.astype(F32)).astype(BF16)
+    residual_grad = (came.reshape(1, 128, 2048).astype(F32) + from_next.astype(F32)).astype(BF16)
     return head_grad, residual_grad, gain_grad
 
 

time: 191 us -> 173 us (0.906)
  blocking collectives: 0 us -> 16.4 us
  local copies, waits for them, and re-layouts: 27.4 us -> 11.2 us
  starting transfers between devices: 67.1 us -> 53.8 us
  waiting for transfers between devices: 49.3 us -> 38.1 us
  Pallas kernels: 33.2 us -> 36.9 us
  other arithmetic: 8 us -> 10.5 us
    all_to_all x0 -> x1, blocking collectives: none -> 16.4 us  [local(): parts = lax.all_to_all(lse, AXES, 0, 0, tiled=True)]
    unnamed x54 -> x33, local copies, waits for them, and re-layouts: 25 us -> 8.8 us
    all_to_all x2 -> x1, starting transfers between devices: 12.9 us -> 5 us  [local(): terms = lax.all_to_all(slots, CHIPS, 0, 0, tiled=True)]
    pallas_call x1 -> x2, Pallas kernels: 0.57 us -> 8.06 us  [the longest x1 4.49 us: turn_call(): pl.pallas_call(turn_kernel, in_specs=[pl.BlockSpec(memory_space=pltpu.SME...]
    all_to_all x2 -> x1, waiting for transfers between devices: 5.63 us -> 0.01 us  [local(): terms = lax.all_to_all(slots, CHIPS, 0, 0, tiled=True)]
    pallas_call x13 -> x10, Pallas kernels: 25.7 us -> 20.3 us  [call(): pl.pallas_call(kernel, in_specs=smem + [vmem] * len(operands), out_specs=...]
    ppermute x23 -> x21, waiting for transfers between devices: 21 us -> 17.7 us  [move(): return lax.ppermute(block, AXES, route(step))]
    all_to_all x1, starting transfers between devices: 9.13 us -> 5.86 us  [local(): came = lax.all_to_all(placed, PIPE, 0, 0, tiled=True)]
  transfers between devices with their start and end apart: 28 -> 25, of which waited for: 10 -> 10; matrix products, arithmetic and copies ran while one was open for 4% -> 6% of each run, Pallas kernels for 11% -> 13%
where the time goes in v3:
time: 173 us; the launch traced here: 172 us
  starting transfers between devices  53.8 us (31%)
  waiting for transfers between devices  38.1 us (22%)
  Pallas kernels  36.9 us (21%)
  blocking collectives  16.4 us (9%)
  local copies, waits for them, and re-layouts  11.2 us (6%)
  other arithmetic  10.5 us (6%)
  between operations  4.89 us (3%)
    ppermute x21, starting transfers between devices, move(): return lax.ppermute(block, AXES, route(step))  25.6 us
    pallas_call x10, Pallas kernels, call(): pl.pallas_call(kernel, in_specs=smem + [vmem] * len(operands), out_specs=...  20.3 us
    ppermute x21, waiting for transfers between devices, move(): return lax.ppermute(block, AXES, route(step))  17.7 us
    all_to_all x1, blocking collectives, local(): parts = lax.all_to_all(lse, AXES, 0, 0, tiled=True)  16.4 us
    all_to_all x1, waiting for transfers between devices, local(): quarter = lax.all_to_all(slots_call(rows), CHIPS, 0, 0, tiled=True)  12.6 us
    all_to_all x1, starting transfers between devices, local(): quarter = lax.all_to_all(slots_call(rows), CHIPS, 0, 0, tiled=True)  9.99 us
    unnamed x33, local copies, waits for them, and re-layouts  8.8 us
    pallas_call x1, Pallas kernels, head_call(): pl.pallas_call(head_kernel, grid_spec=pltpu.PrefetchScalarGridSpec(num_sc...  8.54 us
  transfers between devices with their start and end apart: 25, of which 10 were waited for; matrix products, arithmetic and copies ran while one was open for 6% of the time, Pallas kernels for 13%

profile of v3, /device:TPU:1, one launch (start us, length us, event | category | flops | bytes accessed | tf_op | source)
XLA Modules:
  0.0 171.9 jit_solution(7832960896974225830)
XLA Ops:
  0.6 7.4 %all-to-all-start = ((bf16[16,8,2048]{2,1,0:T(8,128)(2,1)}), bf16[16,8,2048]{2,1,0:T(8,128)(2,1)S(1)}, u32[]{:S(2)}, u32[]{:S(2)}) async-start(bf16[16,8,2048]{2,1,0:T(8,128)(2,1)} %bitcast.34), calls=%async_computation | async-start | bytes 1048576 | tf_op jit(solution)/shard_map/all_to_all | solution.py:330
  8.0 2.5 %collective-permute-start = (f32[2048]{0:T(1024)}, f32[2048]{0:T(1024)S(1)}, u32[]{:S(2)}, u32[]{:S(2)}) collective-permute-start(f32[2048]{0:T(1024)} %param.9), channel_id=1, source_target_pairs={{0,6},{1,7},{2,0},{3,1},{4,2},{5,3},{6,4},{7,5},{8,14},{9,15},{10,... | collective-permute-start | bytes 24584 | tf_op jit(solution)/shard_map/ppermute | solution.py:34
  19.1 10.0 %all-to-all-start.1 = ((bf16[64,16,640]{2,1,0:T(8,128)(2,1)}), bf16[64,16,640]{2,1,0:T(8,128)(2,1)S(1)}, u32[]{:S(2)}, u32[]{:S(2)}) async-start(bf16[64,16,640]{2,1,0:T(8,128)(2,1)} %shard_map.94), calls=%async_computation.1 | async-start | bytes 2621440 | tf_op jit(solution)/shard_map/all_to_all | solution.py:353
  29.1 2.6 %collective-permute-start.3 = (s32[2,128]{1,0:T(2,128)S(1)}, s32[2,128]{1,0:T(2,128)S(1)}, u32[]{:S(2)}, u32[]{:S(2)}) collective-permute-start(s32[2,128]{1,0:T(2,128)S(1)} %pad_add_fusion), channel_id=1, source_target_pairs={{0,1},{1,0},{2,3},{3,2},{4,5},{5,4},{6,7},{7,6},{8,9},{9,8},{10,11... | collective-permute-start | bytes 3080 | tf_op jit(solution)/shard_map/ppermute | solution.py:34
  31.9 2.0 %fusion.6 = f32[]{:T(128)} fusion(s32[1]{0:T(128)} %bitcast.11, s32[1]{0:T(128)} %bitcast.10), kind=kLoop, calls=%fused_computation.30 | loop fusion | flops 7 | bytes 12 | tf_op jit(solution)/shard_map/reduce_sum | solution.py:336
  33.9 2.0 %broadcast_divide_fusion = f32[2]{0:T(128)S(1)} fusion(f32[]{:T(128)} %fusion.6, s32[1]{0:T(128)} %bitcast.11, s32[1]{0:T(128)} %bitcast.10), kind=kLoop, calls=%fused_computation.29 | loop fusion | flops 8 | bytes 20 | tf_op jit(solution)/shard_map/div | solution.py:336
  36.6 12.6 %all-to-all-done.1.came = bf16[64,16,640]{2,1,0:T(8,128)(2,1)S(1)} async-done(((bf16[64,16,640]{2,1,0:T(8,128)(2,1)}), bf16[64,16,640]{2,1,0:T(8,128)(2,1)S(1)}, u32[]{:S(2)}, u32[]{:S(2)}) %all-to-all-start.1) | async-done | bytes 1310752 | tf_op jit(solution)/shard_map/all_to_all | solution.py:353
  50.2 2.5 %collective-permute-start.7 = (bf16[4,256,512]{2,1,0:T(8,128)(2,1)S(1)}, bf16[4,256,512]{2,1,0:T(8,128)(2,1)S(1)}, u32[]{:S(2)}, u32[]{:S(2)}) collective-permute-start(bf16[4,256,512]{2,1,0:T(8,128)(2,1)S(1)} %get-tuple-element.42.block.refs_0_), channel_id=1, source_target_pairs={{0,8},{1,9},{2,10},{3,11},{4,12},{5,13},{6,14},{7,15},{8,0},{9,1},... | collective-permute-start | bytes 3145736 | tf_op jit(solution)/shard_map/ppermute | solution.py:34
  53.3 2.4 %collective-permute-start.6 = (bf16[4,256,512]{2,1,0:T(8,128)(2,1)S(1)}, bf16[4,256,512]{2,1,0:T(8,128)(2,1)}, u32[]{:S(2)}, u32[]{:S(2)}) collective-permute-start(bf16[4,256,512]{2,1,0:T(8,128)(2,1)S(1)} %get-tuple-element.42.block.refs_0_), channel_id=1, source_target_pairs={{0,2},{1,3},{2,4},{3,5},{4,6},{5,7},{6,0},{7,1},{8,25},{9,24},{10,... | collective-permute-start | bytes 3145736 | tf_op jit(solution)/shard_map/ppermute | solution.py:34
  55.8 3.4 %copy-done = bf16[512,8192]{1,0:T(8,128)(2,1)S(1)} copy-done((bf16[512,8192]{1,0:T(8,128)(2,1)S(1)}, bf16[512,8192]{1,0:T(8,128)(2,1)}, u32[]{:S(2)}) %copy-start) | copy-done | bytes 8388632
  59.2 3.6 %shard_map.96 = (bf16[16,512,512]{2,1,0:T(8,128)(2,1)S(1)}, f32[512,256]{1,0:T(8,128)S(1)}) custom-call(s32[6]{0:T(128)S(1)} %pad_add_fusion.1.tint.core.info, bf16[512,8192]{1,0:T(8,128)(2,1)S(1)} %copy-done, bf16[4,256,512]{2,1,0:T(8,128)(2,1)S(1)} %get-tuple-element.42.block.refs_0_), custom_call_target="tpu_custom_call" | custom-call | flops 536870912 | bytes 9437184 | tf_op jit(solution)/shard_map/pallas_call | solution.py:130
  64.1 3.8 %collective-permute-done.4.refs_0_.refs_1_ = bf16[4,256,512]{2,1,0:T(8,128)(2,1)} collective-permute-done((bf16[4,256,512]{2,1,0:T(8,128)(2,1)S(1)}, bf16[4,256,512]{2,1,0:T(8,128)(2,1)}, u32[]{:S(2)}, u32[]{:S(2)}) %collective-permute-start.4) | collective-permute-done | bytes 1048608 | tf_op jit(solution)/shard_map/ppermute | solution.py:34
  70.3 4.4 %shard_map.98.ours = f32[512,256]{1,0:T(8,128)S(1)} custom-call(bf16[16,512,512]{2,1,0:T(8,128)(2,1)S(1)} %get-tuple-element.43.near, bf16[4,256,512]{2,1,0:T(8,128)(2,1)} %collective-permute-done.4.refs_0_.refs_1_, bf16[4,256,512]{2,1,0:T(8,128)(2,1)} %collective-permute-done.5.refs_1_.refs_2_, bf16[4,256,512]{2,1,0:T(8,128)(2,1)} %collective-permute-done.6.refs_2_.refs_3_), custom_call_target="tpu_custom_call" | custom-call | flops 1610612736 | bytes 6291456 | tf_op jit(solution)/shard_map/pallas_call | solution.py:58
  75.3 3.8 %shard_map.99 = (f32[512,512]{1,0:T(8,128)S(1)}, f32[128,4,128]{2,1,0:T(4,128)S(1)}, f32[512,256]{1,0:T(8,128)}) custom-call(s32[6]{0:T(128)S(1)} %pad_add_fusion.1.tint.core.info, bf16[16,512,512]{2,1,0:T(8,128)(2,1)S(1)} %get-tuple-element.43.near, bf16[4,256,512]{2,1,0:T(8,128)(2,1)S(1)} %collective-permute-done.8.block_1.refs_5_, ...), custom_call_target="tpu_custom_call" | custom-call | flops 1610612736 | bytes 9437184 | tf_op jit(solution)/shard_map/pallas_call | solution.py:58
  79.2 16.4 %all_to_all.25.parts = f32[128,4,128]{2,1,0:T(4,128)S(1)} all-to-all(f32[128,4,128]{2,1,0:T(4,128)S(1)} %get-tuple-element.51), channel_id=1, replica_groups=mesh['y'=4,'zl'=2,'c'=2,'x'=4,'zh'=2] {'y','zl','c','x','zh'}, dimensions={0} | all-to-all | bytes 524288 | tf_op jit(solution)/shard_map/all_to_all | solution.py:365
  95.5 4.5 %shard_map.100 = (bf16[512,512]{1,0:T(8,128)(2,1)S(1)}, bf16[512,512]{1,0:T(8,128)(2,1)S(1)}, f32[1,512]{1,0:T(1,128)S(1)}, bf16[16,512,512]{2,1,0:T(8,128)(2,1)...) custom-call(s32[6]{0:T(128)S(1)} %pad_add_fusion.1.tint.core.info, ...), custom_call_target="tpu_custom_call" | custom-call | flops 1073741824 | bytes 9437184 | tf_op jit(solution)/shard_map/pallas_call | solution.py:213
  112.9 8.5 %collective-permute-done.14.one = bf16[4,256,512]{2,1,0:T(8,128)(2,1)S(1)} collective-permute-done((bf16[4,256,512]{2,1,0:T(8,128)(2,1)S(1)}, bf16[4,256,512]{2,1,0:T(8,128)(2,1)S(1)}, u32[]{:S(2)}, u32[]{:S(2)}) %collective-permute-start.14) | collective-permute-done | bytes 1048608 | tf_op jit(solution)/shard_map/ppermute | solution.py:34
  124.3 2.3 %shard_map.104 = bf16[64,16,640]{2,1,0:T(8,128)(2,1)} custom-call(bf16[64,16,640]{2,1,0:T(8,128)(2,1)S(1)} %all-to-all-done.1.came, f32[256,128]{1,0:T(8,128)S(1)} %copy-done.10, f32[4,256,512]{2,1,0:T(8,128)S(1)} %get-tuple-element.60.ours, bf16[4,256,512]{2,1,0:T(8,128)(2,1)S(1)} %collective-permute-done.12.swapped, ...), custom_call_target="tpu_custom_call" | custom-call | bytes 6291456 | tf_op jit(solution)/shard_map/pallas_call | solution.py:58
  126.6 5.0 %all-to-all-start.3 = ((bf16[64,16,640]{2,1,0:T(8,128)(2,1)}), bf16[64,16,640]{2,1,0:T(8,128)(2,1)S(1)}, u32[]{:S(2)}, u32[]{:S(2)}) async-start(bf16[64,16,640]{2,1,0:T(8,128)(2,1)} %shard_map.104), calls=%async_computation.3 | async-start | bytes 2621440 | tf_op jit(solution)/shard_map/all_to_all | solution.py:376
  131.6 5.8 %collective-permute-start.19 = (bf16[1,128,2048]{2,1,0:T(8,128)(2,1)}, bf16[1,128,2048]{2,1,0:T(8,128)(2,1)}, u32[]{:S(2)}, u32[]{:S(2)}) collective-permute-start(bf16[1,128,2048]{2,1,0:T(8,128)(2,1)} %param.8), channel_id=1, source_target_pairs={{8,0},{9,1},{10,2},{11,3},{12,4},{13,5},{14,6},{15,7},{16,8},{17,9... | collective-permute-start | bytes 1572872 | tf_op jit(solution)/shard_map/ppermute | solution.py:34
  144.2 8.5 %shard_map.105 = bf16[512,8192]{1,0:T(8,128)(2,1)} custom-call(s32[6]{0:T(128)S(1)} %pad_add_fusion.1.tint.core.info, bf16[512,512]{1,0:T(8,128)(2,1)S(1)} %copy-done.8, bf16[4,256,512]{2,1,0:T(8,128)(2,1)S(1)} %get-tuple-element.42.block.refs_0_, bf16[4,256,512]{2,1,0:T(8,128)(2,1)} %collective-permute-done.4.refs_0_.refs_1_, ...), custom_call_target="tpu_custom_call" | custom-call | flops 4294967296 | bytes 17825792 | tf_op jit(solution)/shard_map/pallas_call | solution.py:256
  154.4 5.9 %all-to-all-start.4 = ((bf16[16,8,2048]{2,1,0:T(8,128)(2,1)}), bf16[16,8,2048]{2,1,0:T(8,128)(2,1)S(1)}, u32[]{:S(2)}, u32[]{:S(2)}) async-start(bf16[16,8,2048]{2,1,0:T(8,128)(2,1)} %get-tuple-element.71), calls=%async_computation.4 | async-start | bytes 1048576 | tf_op jit(solution)/shard_map/all_to_all | solution.py:383
  162.0 7.9 %all-to-all-done.4 = bf16[16,8,2048]{2,1,0:T(8,128)(2,1)S(1)} async-done(((bf16[16,8,2048]{2,1,0:T(8,128)(2,1)}), bf16[16,8,2048]{2,1,0:T(8,128)(2,1)S(1)}, u32[]{:S(2)}, u32[]{:S(2)}) %all-to-all-start.4) | async-done | bytes 524320 | tf_op jit(solution)/shard_map/all_to_all | solution.py:383
  169.9 2.0 %fusion = bf16[1,128,2048]{2,1,0:T(8,128)(2,1)} fusion(bf16[1,128,2048]{2,1,0:T(8,128)(2,1)} %collective-permute-done.19, bf16[16,8,2048]{2,1,0:T(8,128)(2,1)S(1)} %all-to-all-done.4), kind=kLoop, calls=%fused_computation.4 | loop fusion | flops 1048576 | bytes 1572864 | tf_op jit(solution)/shard_map/convert_element_type | solution.py:386
  (107 shorter events, 37.5 us)
Async XLA Ops:
  0.6 17.2 %all-to-all-start = ((bf16[16,8,2048]{2,1,0:T(8,128)(2,1)}), bf16[16,8,2048]{2,1,0:T(8,128)(2,1)S(1)}, u32[]{:S(2)}, u32[]{:S(2)}) async-start(bf16[16,8,2048]{2,1,0:T(8,128)(2,1)} %bitcast.34), calls=%async_computation | async-start | bytes 1048576 | tf_op jit(solution)/shard_map/all_to_all | solution.py:330
  8.0 8.9 %collective-permute-start = (f32[2048]{0:T(1024)}, f32[2048]{0:T(1024)S(1)}, u32[]{:S(2)}, u32[]{:S(2)}) collective-permute-start(f32[2048]{0:T(1024)} %param.9), channel_id=1, source_target_pairs={{0,6},{1,7},{2,0},{3,1},{4,2},{5,3},{6,4},{7,5},{8,14},{9,15},{10,... | collective-permute-start | bytes 24584 | tf_op jit(solution)/shard_map/ppermute | solution.py:34
  10.5 6.4 %collective-permute-start.1 = (f32[2048]{0:T(1024)}, f32[2048]{0:T(1024)S(1)}, u32[]{:S(2)}, u32[]{:S(2)}) collective-permute-start(f32[2048]{0:T(1024)} %param.9), channel_id=1, source_target_pairs={{0,4},{1,5},{2,6},{3,7},{4,0},{5,1},{6,2},{7,3},{8,12},{9,13},{10,... | collective-permute-start | bytes 24584 | tf_op jit(solution)/shard_map/ppermute | solution.py:34
  11.0 5.9 %collective-permute-start.2 = (f32[2048]{0:T(1024)}, f32[2048]{0:T(1024)S(1)}, u32[]{:S(2)}, u32[]{:S(2)}) collective-permute-start(f32[2048]{0:T(1024)} %param.9), channel_id=1, source_target_pairs={{0,2},{1,3},{2,4},{3,5},{4,6},{5,7},{6,0},{7,1},{8,10},{9,11},{10,... | collective-permute-start | bytes 24584 | tf_op jit(solution)/shard_map/ppermute | solution.py:34
  19.1 30.0 %all-to-all-start.1 = ((bf16[64,16,640]{2,1,0:T(8,128)(2,1)}), bf16[64,16,640]{2,1,0:T(8,128)(2,1)S(1)}, u32[]{:S(2)}, u32[]{:S(2)}) async-start(bf16[64,16,640]{2,1,0:T(8,128)(2,1)} %shard_map.94), calls=%async_computation.1 | async-start | bytes 2621440 | tf_op jit(solution)/shard_map/all_to_all | solution.py:353
  29.1 7.0 %collective-permute-start.3 = (s32[2,128]{1,0:T(2,128)S(1)}, s32[2,128]{1,0:T(2,128)S(1)}, u32[]{:S(2)}, u32[]{:S(2)}) collective-permute-start(s32[2,128]{1,0:T(2,128)S(1)} %pad_add_fusion), channel_id=1, source_target_pairs={{0,1},{1,0},{2,3},{3,2},{4,5},{5,4},{6,7},{7,6},{8,9},{9,8},{10,11... | collective-permute-start | bytes 3080 | tf_op jit(solution)/shard_map/ppermute | solution.py:34
  50.2 12.6 %collective-permute-start.7 = (bf16[4,256,512]{2,1,0:T(8,128)(2,1)S(1)}, bf16[4,256,512]{2,1,0:T(8,128)(2,1)S(1)}, u32[]{:S(2)}, u32[]{:S(2)}) collective-permute-start(bf16[4,256,512]{2,1,0:T(8,128)(2,1)S(1)} %get-tuple-element.42.block.refs_0_), channel_id=1, source_target_pairs={{0,8},{1,9},{2,10},{3,11},{4,12},{5,13},{6,14},{7,15},{8,0},{9,1},... | collective-permute-start | bytes 3145736 | tf_op jit(solution)/shard_map/ppermute | solution.py:34
  52.6 15.3 %collective-permute-start.4 = (bf16[4,256,512]{2,1,0:T(8,128)(2,1)S(1)}, bf16[4,256,512]{2,1,0:T(8,128)(2,1)}, u32[]{:S(2)}, u32[]{:S(2)}) collective-permute-start(bf16[4,256,512]{2,1,0:T(8,128)(2,1)S(1)} %get-tuple-element.42.block.refs_0_), channel_id=1, source_target_pairs={{0,6},{1,7},{2,0},{3,1},{4,2},{5,3},{6,4},{7,5},{8,24},{9,25},{10,... | collective-permute-start | bytes 3145736 | tf_op jit(solution)/shard_map/ppermute | solution.py:34
  53.0 14.9 %collective-permute-start.5 = (bf16[4,256,512]{2,1,0:T(8,128)(2,1)S(1)}, bf16[4,256,512]{2,1,0:T(8,128)(2,1)}, u32[]{:S(2)}, u32[]{:S(2)}) collective-permute-start(bf16[4,256,512]{2,1,0:T(8,128)(2,1)S(1)} %get-tuple-element.42.block.refs_0_), channel_id=1, source_target_pairs={{0,32},{1,33},{2,34},{3,35},{4,36},{5,37},{6,38},{7,39},{8,104},{9... | collective-permute-start | bytes 3145736 | tf_op jit(solution)/shard_map/ppermute | solution.py:34
  53.3 14.6 %collective-permute-start.6 = (bf16[4,256,512]{2,1,0:T(8,128)(2,1)S(1)}, bf16[4,256,512]{2,1,0:T(8,128)(2,1)}, u32[]{:S(2)}, u32[]{:S(2)}) collective-permute-start(bf16[4,256,512]{2,1,0:T(8,128)(2,1)S(1)} %get-tuple-element.42.block.refs_0_), channel_id=1, source_target_pairs={{0,2},{1,3},{2,4},{3,5},{4,6},{5,7},{6,0},{7,1},{8,25},{9,24},{10,... | collective-permute-start | bytes 3145736 | tf_op jit(solution)/shard_map/ppermute | solution.py:34
  67.9 6.9 %collective-permute-start.8 = (bf16[4,256,512]{2,1,0:T(8,128)(2,1)}, bf16[4,256,512]{2,1,0:T(8,128)(2,1)S(1)}, u32[]{:S(2)}, u32[]{:S(2)}) collective-permute-start(bf16[4,256,512]{2,1,0:T(8,128)(2,1)} %collective-permute-done.4.refs_0_.refs_1_), channel_id=1, source_target_pairs={{0,8},{1,9},{2,10},{3,11},{4,12},{5,13},{6,14},{7,15},{8,0},{9,1},... | collective-permute-start | bytes 3145736 | tf_op jit(solution)/shard_map/ppermute | solution.py:34
  69.8 5.0 %collective-permute-start.9 = (bf16[4,256,512]{2,1,0:T(8,128)(2,1)}, bf16[4,256,512]{2,1,0:T(8,128)(2,1)S(1)}, u32[]{:S(2)}, u32[]{:S(2)}) collective-permute-start(bf16[4,256,512]{2,1,0:T(8,128)(2,1)} %collective-permute-done.5.refs_1_.refs_2_), channel_id=1, source_target_pairs={{0,8},{1,9},{2,10},{3,11},{4,12},{5,13},{6,14},{7,15},{8,0},{9,1},... | collective-permute-start | bytes 3145736 | tf_op jit(solution)/shard_map/ppermute | solution.py:34
  69.8 5.5 %collective-permute-start.10 = (bf16[4,256,512]{2,1,0:T(8,128)(2,1)}, bf16[4,256,512]{2,1,0:T(8,128)(2,1)S(1)}, u32[]{:S(2)}, u32[]{:S(2)}) collective-permute-start(bf16[4,256,512]{2,1,0:T(8,128)(2,1)} %collective-permute-done.6.refs_2_.refs_3_), channel_id=1, source_target_pairs={{0,8},{1,9},{2,10},{3,11},{4,12},{5,13},{6,14},{7,15},{8,0},{9,1},... | collective-permute-start | bytes 3145736 | tf_op jit(solution)/shard_map/ppermute | solution.py:34
  101.8 2.7 %collective-permute-start.11 = (bf16[4,256,512]{2,1,0:T(8,128)(2,1)S(1)}, bf16[4,256,512]{2,1,0:T(8,128)(2,1)S(1)}, u32[]{:S(2)}, u32[]{:S(2)}) collective-permute-start(bf16[4,256,512]{2,1,0:T(8,128)(2,1)S(1)} %get-tuple-element.58), channel_id=1, source_target_pairs={{0,8},{1,9},{2,10},{3,11},{4,12},{5,13},{6,14},{7,15},{8,0},{9,1},... | collective-permute-start | bytes 3145736 | tf_op jit(solution)/shard_map/ppermute | solution.py:34
  102.1 4.9 %collective-permute-start.13 = (bf16[4,256,512]{2,1,0:T(8,128)(2,1)S(1)}, bf16[4,256,512]{2,1,0:T(8,128)(2,1)S(1)}, u32[]{:S(2)}, u32[]{:S(2)}) collective-permute-start(bf16[4,256,512]{2,1,0:T(8,128)(2,1)S(1)} %get-tuple-element.63), channel_id=1, source_target_pairs={{0,8},{1,9},{2,10},{3,11},{4,12},{5,13},{6,14},{7,15},{8,0},{9,1},... | collective-permute-start | bytes 3145736 | tf_op jit(solution)/shard_map/ppermute | solution.py:34
  104.2 4.1 %collective-permute-start.15 = (bf16[4,256,512]{2,1,0:T(8,128)(2,1)S(1)}, bf16[4,256,512]{2,1,0:T(8,128)(2,1)S(1)}, u32[]{:S(2)}, u32[]{:S(2)}) collective-permute-start(bf16[4,256,512]{2,1,0:T(8,128)(2,1)S(1)} %get-tuple-element.65), channel_id=1, source_target_pairs={{0,8},{1,9},{2,10},{3,11},{4,12},{5,13},{6,14},{7,15},{8,0},{9,1},... | collective-permute-start | bytes 3145736 | tf_op jit(solution)/shard_map/ppermute | solution.py:34
  106.7 6.2 %collective-permute-start.12 = (bf16[4,256,512]{2,1,0:T(8,128)(2,1)S(1)}, bf16[4,256,512]{2,1,0:T(8,128)(2,1)S(1)}, u32[]{:S(2)}, u32[]{:S(2)}) collective-permute-start(bf16[4,256,512]{2,1,0:T(8,128)(2,1)S(1)} %get-tuple-element.61), channel_id=1, source_target_pairs={{0,8},{1,9},{2,10},{3,11},{4,12},{5,13},{6,14},{7,15},{8,0},{9,1},... | collective-permute-start | bytes 3145736 | tf_op jit(solution)/shard_map/ppermute | solution.py:34
  107.4 14.0 %collective-permute-start.14 = (bf16[4,256,512]{2,1,0:T(8,128)(2,1)S(1)}, bf16[4,256,512]{2,1,0:T(8,128)(2,1)S(1)}, u32[]{:S(2)}, u32[]{:S(2)}) collective-permute-start(bf16[4,256,512]{2,1,0:T(8,128)(2,1)S(1)} %add_convert_fusion.1), channel_id=1, source_target_pairs={{0,2},{1,3},{2,4},{3,5},{4,6},{5,7},{6,0},{7,1},{8,25},{9,24},{10,... | collective-permute-start | bytes 3145736 | tf_op jit(solution)/shard_map/ppermute | solution.py:34
  108.7 14.0 %collective-permute-start.16 = (bf16[4,256,512]{2,1,0:T(8,128)(2,1)S(1)}, bf16[4,256,512]{2,1,0:T(8,128)(2,1)S(1)}, u32[]{:S(2)}, u32[]{:S(2)}) collective-permute-start(bf16[4,256,512]{2,1,0:T(8,128)(2,1)S(1)} %add_convert_fusion), channel_id=1, source_target_pairs={{0,32},{1,33},{2,34},{3,35},{4,36},{5,37},{6,38},{7,39},{8,104},{9... | collective-permute-start | bytes 3145736 | tf_op jit(solution)/shard_map/ppermute | solution.py:34
  109.2 15.1 %collective-permute-start.17 = (bf16[4,256,512]{2,1,0:T(8,128)(2,1)S(1)}, bf16[4,256,512]{2,1,0:T(8,128)(2,1)S(1)}, u32[]{:S(2)}, u32[]{:S(2)}) collective-permute-start(bf16[4,256,512]{2,1,0:T(8,128)(2,1)S(1)} %add_convert_fusion.2), channel_id=1, source_target_pairs={{0,6},{1,7},{2,0},{3,1},{4,2},{5,3},{6,4},{7,5},{8,24},{9,25},{10,... | collective-permute-start | bytes 3145736 | tf_op jit(solution)/shard_map/ppermute | solution.py:34
  110.1 2.7 %collective-permute-start.18 = (f32[2,128]{1,0:T(2,128)S(1)}, f32[2,128]{1,0:T(2,128)S(1)}, u32[]{:S(2)}, u32[]{:S(2)}) collective-permute-start(f32[2,128]{1,0:T(2,128)S(1)} %bitcast.44), channel_id=1, source_target_pairs={{0,8},{1,9},{2,10},{3,11},{4,12},{5,13},{6,14},{7,15},{8,0},{9,1},... | collective-permute-start | bytes 3080 | tf_op jit(solution)/shard_map/ppermute | solution.py:34
  126.6 26.2 %all-to-all-start.3 = ((bf16[64,16,640]{2,1,0:T(8,128)(2,1)}), bf16[64,16,640]{2,1,0:T(8,128)(2,1)S(1)}, u32[]{:S(2)}, u32[]{:S(2)}) async-start(bf16[64,16,640]{2,1,0:T(8,128)(2,1)} %shard_map.104), calls=%async_computation.3 | async-start | bytes 2621440 | tf_op jit(solution)/shard_map/all_to_all | solution.py:376
  131.6 30.4 %collective-permute-start.19 = (bf16[1,128,2048]{2,1,0:T(8,128)(2,1)}, bf16[1,128,2048]{2,1,0:T(8,128)(2,1)}, u32[]{:S(2)}, u32[]{:S(2)}) collective-permute-start(bf16[1,128,2048]{2,1,0:T(8,128)(2,1)} %param.8), channel_id=1, source_target_pairs={{8,0},{9,1},{10,2},{11,3},{12,4},{13,5},{14,6},{15,7},{16,8},{17,9... | collective-permute-start | bytes 1572872 | tf_op jit(solution)/shard_map/ppermute | solution.py:34
  154.4 15.5 %all-to-all-start.4 = ((bf16[16,8,2048]{2,1,0:T(8,128)(2,1)}), bf16[16,8,2048]{2,1,0:T(8,128)(2,1)S(1)}, u32[]{:S(2)}, u32[]{:S(2)}) async-start(bf16[16,8,2048]{2,1,0:T(8,128)(2,1)} %get-tuple-element.71), calls=%async_computation.4 | async-start | bytes 1048576 | tf_op jit(solution)/shard_map/all_to_all | solution.py:383
  (17 other events, 117.3 us)

commit v4 on v3

--- a/solution.py
+++ b/solution.py
@@ -69,36 +69,46 @@
     return pl.ds(pl.multiple_of(t * 2048 + tint[away] * 512, 512), 512)
 
 
+def diagonal():
+    return lax.broadcasted_iota(jnp.int32, (16, 128), 0) == lax.broadcasted_iota(jnp.int32, (16, 128), 1)
+
+
 def slots_kernel(rows, out):
     wide = rows[...].astype(F32)
     squares = jnp.sum(wide * wide, axis=1, keepdims=True)
-    high = squares.astype(BF16).astype(F32)
-    middle = (squares - high).astype(BF16).astype(F32)
-    low = squares - high - middle
-    lane = lax.broadcasted_iota(jnp.int32, (16, 128), 1)
-    extra = jnp.where(lane == 0, high, jnp.where(lane == 1, middle, jnp.where(lane == 2, low, 0.0))).astype(BF16)
+    along = jnp.sum(jnp.where(diagonal(), squares, 0.0), axis=0, keepdims=True)
+    extra = jnp.concatenate([*three_parts(along), jnp.zeros((5, 128), F32)], axis=0).astype(BF16)
     for chip, colour in enumerate(COLOURS):
-        out[chip, :, :512] = rows[:, colour * 512 : (colour + 1) * 512]
-        out[chip, :, 512:] = extra
+        for i in range(4):
+            start = colour * 512 + i * 128
+            out[chip, i * 16 : (i + 1) * 16, :] = rows[:, start : start + 128]
+        out[chip, 64:, :] = extra
 
 
 def slots_call(rows):
-    return call(slots_kernel, None, [rows], [((64, 16, 640), BF16, True)])[0]
-
-
-def norm_kernel(came, gain, own, inverse_rms):
+    return call(slots_kernel, None, [rows], [((64, 72, 128), BF16, True)])[0]
+
+
+def inverse_of(came, group):
+    squares = sum(came[t * 16 + group, 64:, :].astype(F32) for t in range(4))
+    along = jnp.sum(squares, axis=0, keepdims=True)
+    squares = jnp.sum(jnp.where(diagonal(), along, 0.0), axis=1, keepdims=True)
+    return lax.rsqrt(squares / 8192 + NORM_EPS)
+
+
+def norm_kernel(came, gain, own):
     for group in range(16):
         span = slice(group * 16, (group + 1) * 16)
-        squares = sum(came[t * 16 + group, :, 512:].astype(F32) for t in range(4))
-        inverse = lax.rsqrt(jnp.sum(squares, axis=1, keepdims=True) / 8192 + NORM_EPS)
-        inverse_rms[span, :] = jnp.broadcast_to(inverse, (16, 128))
+        inverse = inverse_of(came, group)
         for t in range(4):
-            unit = came[t * 16 + group, :, :512].astype(F32) * inverse
-            own[t, span, :] = (unit * gain[t : t + 1, :]).astype(BF16)
+            for i in range(4):
+                unit = came[t * 16 + group, i * 16 : (i + 1) * 16, :].astype(F32) * inverse
+                lanes = slice(i * 128, (i + 1) * 128)
+                own[t, span, lanes] = (unit * gain[t : t + 1, lanes]).astype(BF16)
 
 
 def norm_call(came, gain):
-    return call(norm_kernel, None, [came, gain], [((4, 256, 512), BF16), ((256, 128), F32, True)], moved=2 << 20)
+    return call(norm_kernel, None, [came, gain], [((4, 256, 512), BF16)], moved=2 << 20)[0]
 
 
 def near_columns(t, away):
@@ -273,7 +283,9 @@
     return high, middle, value - high - middle
 
 
-def join_kernel(came, inverse_rms, ours, swapped, one, two, three, inner, out):
+def join_kernel(came, ours, swapped, one, two, three, inner, out, inverse_rms):
+    for group in range(16):
+        inverse_rms[group * 16 : (group + 1) * 16, :] = jnp.broadcast_to(inverse_of(came, group), (16, 128))
     products = [part[i : i + 1] for part in three_parts(inner[...]) for i in range(2)]
     for t in range(4):
         gain = jnp.zeros((1, 512), F32)
@@ -282,7 +294,8 @@
             total = ours[t, span] + swapped[t, span].astype(F32)
             total += one[t, span].astype(F32) + two[t, span].astype(F32) + three[t, span].astype(F32)
             out[t * 16 + group, :, :512] = total.astype(BF16)
-            unit = came[t * 16 + group, :, :512].astype(F32) * inverse_rms[span, :1]
+            pieces = [came[t * 16 + group, i * 16 : (i + 1) * 16, :] for i in range(4)]
+            unit = jnp.concatenate(pieces, axis=1).astype(F32) * inverse_rms[span, :1]
             gain += jnp.sum(total * unit, axis=0, keepdims=True)
         parts = [part[:, i * 128 : (i + 1) * 128] for part in three_parts(gain)[:2] for i in range(4)]
         extra = jnp.concatenate(parts + products + [jnp.zeros((2, 128), F32)], axis=0).astype(BF16)
@@ -291,7 +304,8 @@
 
 
 def join_call(*operands):
-    return call(join_kernel, None, operands, [((64, 16, 640), BF16, True)], moved=6 << 20)[0]
+    outs = [((64, 16, 640), BF16, True), ((256, 128), F32)]
+    return call(join_kernel, None, operands, outs, moved=6 << 20)
 
 
 def tail_kernel(info, terms, rows, inverse_rms, gain, placed, gain_grad):
@@ -320,6 +334,14 @@
     return call(tail_kernel, info, operands, outs, moved=2 << 20)
 
 
+def hold_kernel(source, out):
+    out[...] = source[...]
+
+
+def add_kernel(exits, from_next, out):
+    out[...] = (exits[...].astype(F32) + from_next[...].astype(F32)).astype(BF16)
+
+
 def local(hidden, section_cotangent, norm_gain, head, labels, loss_mask, exit_on):
     core, x, y, zl, zh = (lax.axis_index(a) for a in ("c", "x", "y", "zl", "zh"))
     device = lax.axis_index(AXES).astype(jnp.int32)
@@ -352,7 +374,7 @@
 
     quarter = lax.all_to_all(slots_call(rows), CHIPS, 0, 0, tiled=True)
     quarter, row_labels, row_weights = lax.optimization_barrier((quarter, row_labels, row_weights))
-    own, inverse_rms = norm_call(quarter, gain)
+    own = norm_call(quarter, gain)
 
     blocks = [own, to_colour(own, 3), to_colour(own, 2), to_colour(own, 1)]
     first_mate = other_core(own)
@@ -368,11 +390,12 @@
     halves = [first_half] + [back_call(dlogits, near, away) for away in (2, 3)]
     sums = [(ours + other_core(theirs).astype(F32)).astype(BF16) for ours, theirs in halves]
     arrived = [to_colour(s, away) for s, away in zip(sums, (1, 2, 3))]
-    late, inner, _ = lax.optimization_barrier((dlogits, inner, sums[2]))
-    ours, theirs = back_call(late, near, 0)
+    inner, _ = lax.optimization_barrier((inner, sums[2]))
     inner = inner.reshape(2, 2, 128)
     inner = inner[0] + other_core(inner[1])
-    slots = join_call(quarter, inverse_rms, ours, other_core(theirs), *arrived, inner)
+    late, inner = lax.optimization_barrier((dlogits, inner))
+    ours, theirs = back_call(late, near, 0)
+    slots, inverse_rms = join_call(quarter, ours, other_core(theirs), *arrived, inner)
     terms = lax.all_to_all(slots, CHIPS, 0, 0, tiled=True)
     head_grad = head_call(tint, turned, blocks, mates)
     place = (y * 2 + zl) * 2 + zh
@@ -383,7 +406,8 @@
     came = lax.all_to_all(placed, PIPE, 0, 0, tiled=True)
     gain_grad = (gain_grad + other_core(gain_grad)).reshape(2048)
     from_next = move(section_cotangent, back_one)
-    residual_grad = (came.reshape(1, 128, 2048).astype(F32) + from_next.astype(F32)).astype(BF16)
+    from_next = call(hold_kernel, None, [from_next[0]], [((128, 2048), BF16)])[0]
+    residual_grad = call(add_kernel, None, [came.reshape(128, 2048), from_next], [((128, 2048), BF16, True)])[0][None]
     return head_grad, residual_grad, gain_grad
 
 

time: 173 us -> 169 us (0.977)
  waiting for transfers between devices: 38.1 us -> 35 us
  other arithmetic: 10.5 us -> 8.03 us
  local copies, waits for them, and re-layouts: 11.2 us -> 13 us
    ppermute x21, waiting for transfers between devices: 17.7 us -> 15.6 us  [move(): return lax.ppermute(block, AXES, route(step))]
    ppermute x21, starting transfers between devices: 25.6 us -> 23.6 us  [move(): return lax.ppermute(block, AXES, route(step))]
    convert_element_type x1 -> x0, other arithmetic: 1.96 us -> none  [local(): (came.reshape(1, 128, 2048).astype(F32) + from_next.astype(F32)).astype(B...]
    unnamed x33 -> x41, local copies, waits for them, and re-layouts: 8.8 us -> 10.6 us
    pallas_call x10 -> x12, Pallas kernels: 20.3 us -> 21.4 us  [call(): pl.pallas_call(kernel, in_specs=smem + [vmem] * len(operands), out_specs=...]
  transfers between devices with their start and end apart: 25 -> 25, of which waited for: 10 -> 9; matrix products, arithmetic and copies ran while one was open for 6% -> 6% of each run, Pallas kernels for 13% -> 14%
where the time goes in v4:
time: 169 us; the launch traced here: 168 us
  starting transfers between devices  53.6 us (32%)
  Pallas kernels  38 us (22%)
  waiting for transfers between devices  35 us (21%)
  blocking collectives  16.3 us (10%)
  local copies, waits for them, and re-layouts  13 us (8%)
  other arithmetic  8.03 us (5%)
  between operations  4.46 us (3%)
    ppermute x21, starting transfers between devices, move(): return lax.ppermute(block, AXES, route(step))  23.6 us
    pallas_call x12, Pallas kernels, call(): pl.pallas_call(kernel, in_specs=smem + [vmem] * len(operands), out_specs=...  21.4 us
    all_to_all x1, blocking collectives, local(): parts = lax.all_to_all(lse, AXES, 0, 0, tiled=True)  16.3 us
    ppermute x21, waiting for transfers between devices, move(): return lax.ppermute(block, AXES, route(step))  15.6 us
    all_to_all x1, waiting for transfers between devices, local(): quarter = lax.all_to_all(slots_call(rows), CHIPS, 0, 0, tiled=True)  11.3 us
    unnamed x41, local copies, waits for them, and re-layouts  10.6 us
    all_to_all x1, starting transfers between devices, local(): quarter = lax.all_to_all(slots_call(rows), CHIPS, 0, 0, tiled=True)  9.78 us
    pallas_call x1, Pallas kernels, head_call(): pl.pallas_call(head_kernel, grid_spec=pltpu.PrefetchScalarGridSpec(num_sc...  8.53 us
  transfers between devices with their start and end apart: 25, of which 9 were waited for; matrix products, arithmetic and copies ran while one was open for 6% of the time, Pallas kernels for 14%

profile of v4, /device:TPU:1, one launch (start us, length us, event | category | flops | bytes accessed | tf_op | source)
XLA Modules:
  0.0 168.3 jit_solution(1191323658368146793)
XLA Ops:
  0.6 7.4 %all-to-all-start = ((bf16[16,8,2048]{2,1,0:T(8,128)(2,1)}), bf16[16,8,2048]{2,1,0:T(8,128)(2,1)S(1)}, u32[]{:S(2)}, u32[]{:S(2)}) async-start(bf16[16,8,2048]{2,1,0:T(8,128)(2,1)} %bitcast.36), calls=%async_computation | async-start | bytes 1048576 | tf_op jit(solution)/shard_map/all_to_all | solution.py:352
  8.0 2.6 %collective-permute-start = (f32[2048]{0:T(1024)}, f32[2048]{0:T(1024)S(1)}, u32[]{:S(2)}, u32[]{:S(2)}) collective-permute-start(f32[2048]{0:T(1024)} %param.9), channel_id=1, source_target_pairs={{0,6},{1,7},{2,0},{3,1},{4,2},{5,3},{6,4},{7,5},{8,14},{9,15},{10,... | collective-permute-start | bytes 24584 | tf_op jit(solution)/shard_map/ppermute | solution.py:34
  19.4 9.8 %all-to-all-start.1 = ((bf16[64,72,128]{2,1,0:T(8,128)(2,1)}), bf16[64,72,128]{2,1,0:T(8,128)(2,1)S(1)}, u32[]{:S(2)}, u32[]{:S(2)}) async-start(bf16[64,72,128]{2,1,0:T(8,128)(2,1)} %shard_map.94), calls=%async_computation.1 | async-start | bytes 2359296 | tf_op jit(solution)/shard_map/all_to_all | solution.py:375
  29.3 2.6 %collective-permute-start.3 = (s32[2,128]{1,0:T(2,128)S(1)}, s32[2,128]{1,0:T(2,128)S(1)}, u32[]{:S(2)}, u32[]{:S(2)}) collective-permute-start(s32[2,128]{1,0:T(2,128)S(1)} %pad_add_fusion), channel_id=1, source_target_pairs={{0,1},{1,0},{2,3},{3,2},{4,5},{5,4},{6,7},{7,6},{8,9},{9,8},{10,11... | collective-permute-start | bytes 3080 | tf_op jit(solution)/shard_map/ppermute | solution.py:34
  32.1 1.8 %fusion.5 = f32[]{:T(128)} fusion(s32[1]{0:T(128)} %bitcast.11, s32[1]{0:T(128)} %bitcast.10), kind=kLoop, calls=%fused_computation.28 | loop fusion | flops 7 | bytes 12 | tf_op jit(solution)/shard_map/reduce_sum | solution.py:358
  33.9 1.9 %broadcast_divide_fusion = f32[2]{0:T(128)S(1)} fusion(f32[]{:T(128)} %fusion.5, s32[1]{0:T(128)} %bitcast.11, s32[1]{0:T(128)} %bitcast.10), kind=kLoop, calls=%fused_computation.27 | loop fusion | flops 8 | bytes 20 | tf_op jit(solution)/shard_map/div | solution.py:358
  36.4 11.3 %all-to-all-done.1.came = bf16[64,72,128]{2,1,0:T(8,128)(2,1)S(1)} async-done(((bf16[64,72,128]{2,1,0:T(8,128)(2,1)}), bf16[64,72,128]{2,1,0:T(8,128)(2,1)S(1)}, u32[]{:S(2)}, u32[]{:S(2)}) %all-to-all-start.1) | async-done | bytes 1179680 | tf_op jit(solution)/shard_map/all_to_all | solution.py:375
  48.2 2.7 %collective-permute-start.7 = (bf16[4,256,512]{2,1,0:T(8,128)(2,1)S(1)}, bf16[4,256,512]{2,1,0:T(8,128)(2,1)S(1)}, u32[]{:S(2)}, u32[]{:S(2)}) collective-permute-start(bf16[4,256,512]{2,1,0:T(8,128)(2,1)S(1)} %shard_map.95.block.refs_0_), channel_id=1, source_target_pairs={{0,8},{1,9},{2,10},{3,11},{4,12},{5,13},{6,14},{7,15},{8,0},{9,1},... | collective-permute-start | bytes 3145736 | tf_op jit(solution)/shard_map/ppermute | solution.py:34
  51.5 2.4 %collective-permute-start.6 = (bf16[4,256,512]{2,1,0:T(8,128)(2,1)S(1)}, bf16[4,256,512]{2,1,0:T(8,128)(2,1)}, u32[]{:S(2)}, u32[]{:S(2)}) collective-permute-start(bf16[4,256,512]{2,1,0:T(8,128)(2,1)S(1)} %shard_map.95.block.refs_0_), channel_id=1, source_target_pairs={{0,2},{1,3},{2,4},{3,5},{4,6},{5,7},{6,0},{7,1},{8,25},{9,24},{10,... | collective-permute-start | bytes 3145736 | tf_op jit(solution)/shard_map/ppermute | solution.py:34
  54.0 3.4 %copy-done = bf16[512,8192]{1,0:T(8,128)(2,1)S(1)} copy-done((bf16[512,8192]{1,0:T(8,128)(2,1)S(1)}, bf16[512,8192]{1,0:T(8,128)(2,1)}, u32[]{:S(2)}) %copy-start) | copy-done | bytes 8388632
  57.4 3.6 %shard_map.96 = (bf16[16,512,512]{2,1,0:T(8,128)(2,1)S(1)}, f32[512,256]{1,0:T(8,128)S(1)}) custom-call(s32[6]{0:T(128)S(1)} %pad_add_fusion.1.tint.core.info, bf16[512,8192]{1,0:T(8,128)(2,1)S(1)} %copy-done, bf16[4,256,512]{2,1,0:T(8,128)(2,1)S(1)} %shard_map.95.block.refs_0_), custom_call_target="tpu_custom_call" | custom-call | flops 536870912 | bytes 9437184 | tf_op jit(solution)/shard_map/pallas_call | solution.py:140
  62.3 3.8 %collective-permute-done.4.refs_0_.refs_1_ = bf16[4,256,512]{2,1,0:T(8,128)(2,1)} collective-permute-done((bf16[4,256,512]{2,1,0:T(8,128)(2,1)S(1)}, bf16[4,256,512]{2,1,0:T(8,128)(2,1)}, u32[]{:S(2)}, u32[]{:S(2)}) %collective-permute-start.4) | collective-permute-done | bytes 1048608 | tf_op jit(solution)/shard_map/ppermute | solution.py:34
  66.1 2.0 %collective-permute-start.8 = (bf16[4,256,512]{2,1,0:T(8,128)(2,1)}, bf16[4,256,512]{2,1,0:T(8,128)(2,1)S(1)}, u32[]{:S(2)}, u32[]{:S(2)}) collective-permute-start(bf16[4,256,512]{2,1,0:T(8,128)(2,1)} %collective-permute-done.4.refs_0_.refs_1_), channel_id=1, source_target_pairs={{0,8},{1,9},{2,10},{3,11},{4,12},{5,13},{6,14},{7,15},{8,0},{9,1},... | collective-permute-start | bytes 3145736 | tf_op jit(solution)/shard_map/ppermute | solution.py:34
  68.6 4.4 %shard_map.98.ours = f32[512,256]{1,0:T(8,128)S(1)} custom-call(bf16[16,512,512]{2,1,0:T(8,128)(2,1)S(1)} %get-tuple-element.42.near, bf16[4,256,512]{2,1,0:T(8,128)(2,1)} %collective-permute-done.4.refs_0_.refs_1_, bf16[4,256,512]{2,1,0:T(8,128)(2,1)} %collective-permute-done.5.refs_1_.refs_2_, bf16[4,256,512]{2,1,0:T(8,128)(2,1)} %collective-permute-done.6.refs_2_.refs_3_), custom_call_target="tpu_custom_call" | custom-call | flops 1610612736 | bytes 6291456 | tf_op jit(solution)/shard_map/pallas_call | solution.py:58
  73.6 3.8 %shard_map.99 = (f32[512,512]{1,0:T(8,128)S(1)}, f32[128,4,128]{2,1,0:T(4,128)S(1)}, f32[512,256]{1,0:T(8,128)}) custom-call(s32[6]{0:T(128)S(1)} %pad_add_fusion.1.tint.core.info, bf16[16,512,512]{2,1,0:T(8,128)(2,1)S(1)} %get-tuple-element.42.near, bf16[4,256,512]{2,1,0:T(8,128)(2,1)S(1)} %collective-permute-done.8.block_1.refs_5_, ...), custom_call_target="tpu_custom_call" | custom-call | flops 1610612736 | bytes 9437184 | tf_op jit(solution)/shard_map/pallas_call | solution.py:58
  77.5 16.3 %all_to_all.25.parts = f32[128,4,128]{2,1,0:T(4,128)S(1)} all-to-all(f32[128,4,128]{2,1,0:T(4,128)S(1)} %get-tuple-element.50), channel_id=1, replica_groups=mesh['y'=4,'zl'=2,'c'=2,'x'=4,'zh'=2] {'y','zl','c','x','zh'}, dimensions={0} | all-to-all | bytes 524288 | tf_op jit(solution)/shard_map/all_to_all | solution.py:387
  93.8 4.5 %shard_map.100 = (bf16[512,512]{1,0:T(8,128)(2,1)S(1)}, bf16[512,512]{1,0:T(8,128)(2,1)S(1)}, f32[1,512]{1,0:T(1,128)S(1)}, bf16[16,512,512]{2,1,0:T(8,128)(2,1)...) custom-call(s32[6]{0:T(128)S(1)} %pad_add_fusion.1.tint.core.info, ...), custom_call_target="tpu_custom_call" | custom-call | flops 1073741824 | bytes 9437184 | tf_op jit(solution)/shard_map/pallas_call | solution.py:223
  98.3 1.8 %shard_map.101 = (f32[4,256,512]{2,1,0:T(8,128)S(1)}, bf16[4,256,512]{2,1,0:T(8,128)(2,1)S(1)}) custom-call(bf16[512,512]{1,0:T(8,128)(2,1)S(1)} %get-tuple-element.59.dlogits, bf16[16,512,512]{2,1,0:T(8,128)(2,1)S(1)} %get-tuple-element.55.near), custom_call_target="tpu_custom_call" | custom-call | flops 1073741824 | bytes 4194304 | tf_op jit(solution)/shard_map/pallas_call | solution.py:58
  109.5 10.0 %collective-permute-done.15.one = bf16[4,256,512]{2,1,0:T(8,128)(2,1)S(1)} collective-permute-done((bf16[4,256,512]{2,1,0:T(8,128)(2,1)S(1)}, bf16[4,256,512]{2,1,0:T(8,128)(2,1)S(1)}, u32[]{:S(2)}, u32[]{:S(2)}) %collective-permute-start.15) | collective-permute-done | bytes 1048608 | tf_op jit(solution)/shard_map/ppermute | solution.py:34
  123.8 5.8 %all-to-all-start.3 = ((bf16[64,16,640]{2,1,0:T(8,128)(2,1)}), bf16[64,16,640]{2,1,0:T(8,128)(2,1)S(1)}, u32[]{:S(2)}, u32[]{:S(2)}) async-start(bf16[64,16,640]{2,1,0:T(8,128)(2,1)} %copy-done.9), calls=%async_computation.3 | async-start | bytes 2621440 | tf_op jit(solution)/shard_map/all_to_all | solution.py:399
  129.6 4.1 %collective-permute-start.19 = (bf16[1,128,2048]{2,1,0:T(8,128)(2,1)}, bf16[1,128,2048]{2,1,0:T(8,128)(2,1)}, u32[]{:S(2)}, u32[]{:S(2)}) collective-permute-start(bf16[1,128,2048]{2,1,0:T(8,128)(2,1)} %param.8), channel_id=1, source_target_pairs={{8,0},{9,1},{10,2},{11,3},{12,4},{13,5},{14,6},{15,7},{16,8},{17,9... | collective-permute-start | bytes 1572872 | tf_op jit(solution)/shard_map/ppermute | solution.py:34
  139.6 8.5 %shard_map.105 = bf16[512,8192]{1,0:T(8,128)(2,1)} custom-call(s32[6]{0:T(128)S(1)} %pad_add_fusion.1.tint.core.info, bf16[512,512]{1,0:T(8,128)(2,1)S(1)} %copy-done.13, bf16[4,256,512]{2,1,0:T(8,128)(2,1)S(1)} %shard_map.95.block.refs_0_, bf16[4,256,512]{2,1,0:T(8,128)(2,1)} %collective-permute-done.4.refs_0_.refs_1_, ...), custom_call_target="tpu_custom_call" | custom-call | flops 4294967296 | bytes 17825792 | tf_op jit(solution)/shard_map/pallas_call | solution.py:266
  150.6 7.0 %all-to-all-start.4 = ((bf16[16,8,2048]{2,1,0:T(8,128)(2,1)}), bf16[16,8,2048]{2,1,0:T(8,128)(2,1)S(1)}, u32[]{:S(2)}, u32[]{:S(2)}) async-start(bf16[16,8,2048]{2,1,0:T(8,128)(2,1)} %get-tuple-element.73), calls=%async_computation.4 | async-start | bytes 1048576 | tf_op jit(solution)/shard_map/all_to_all | solution.py:406
  159.6 7.7 %all-to-all-done.4 = bf16[16,8,2048]{2,1,0:T(8,128)(2,1)S(1)} async-done(((bf16[16,8,2048]{2,1,0:T(8,128)(2,1)}), bf16[16,8,2048]{2,1,0:T(8,128)(2,1)S(1)}, u32[]{:S(2)}, u32[]{:S(2)}) %all-to-all-start.4) | async-done | bytes 524320 | tf_op jit(solution)/shard_map/all_to_all | solution.py:406
  (116 shorter events, 34.8 us)
Async XLA Ops:
  0.6 17.0 %all-to-all-start = ((bf16[16,8,2048]{2,1,0:T(8,128)(2,1)}), bf16[16,8,2048]{2,1,0:T(8,128)(2,1)S(1)}, u32[]{:S(2)}, u32[]{:S(2)}) async-start(bf16[16,8,2048]{2,1,0:T(8,128)(2,1)} %bitcast.36), calls=%async_computation | async-start | bytes 1048576 | tf_op jit(solution)/shard_map/all_to_all | solution.py:352
  8.0 8.4 %collective-permute-start = (f32[2048]{0:T(1024)}, f32[2048]{0:T(1024)S(1)}, u32[]{:S(2)}, u32[]{:S(2)}) collective-permute-start(f32[2048]{0:T(1024)} %param.9), channel_id=1, source_target_pairs={{0,6},{1,7},{2,0},{3,1},{4,2},{5,3},{6,4},{7,5},{8,14},{9,15},{10,... | collective-permute-start | bytes 24584 | tf_op jit(solution)/shard_map/ppermute | solution.py:34
  10.6 5.9 %collective-permute-start.1 = (f32[2048]{0:T(1024)}, f32[2048]{0:T(1024)S(1)}, u32[]{:S(2)}, u32[]{:S(2)}) collective-permute-start(f32[2048]{0:T(1024)} %param.9), channel_id=1, source_target_pairs={{0,4},{1,5},{2,6},{3,7},{4,0},{5,1},{6,2},{7,3},{8,12},{9,13},{10,... | collective-permute-start | bytes 24584 | tf_op jit(solution)/shard_map/ppermute | solution.py:34
  11.1 5.4 %collective-permute-start.2 = (f32[2048]{0:T(1024)}, f32[2048]{0:T(1024)S(1)}, u32[]{:S(2)}, u32[]{:S(2)}) collective-permute-start(f32[2048]{0:T(1024)} %param.9), channel_id=1, source_target_pairs={{0,2},{1,3},{2,4},{3,5},{4,6},{5,7},{6,0},{7,1},{8,10},{9,11},{10,... | collective-permute-start | bytes 24584 | tf_op jit(solution)/shard_map/ppermute | solution.py:34
  19.4 28.3 %all-to-all-start.1 = ((bf16[64,72,128]{2,1,0:T(8,128)(2,1)}), bf16[64,72,128]{2,1,0:T(8,128)(2,1)S(1)}, u32[]{:S(2)}, u32[]{:S(2)}) async-start(bf16[64,72,128]{2,1,0:T(8,128)(2,1)} %shard_map.94), calls=%async_computation.1 | async-start | bytes 2359296 | tf_op jit(solution)/shard_map/all_to_all | solution.py:375
  29.3 6.7 %collective-permute-start.3 = (s32[2,128]{1,0:T(2,128)S(1)}, s32[2,128]{1,0:T(2,128)S(1)}, u32[]{:S(2)}, u32[]{:S(2)}) collective-permute-start(s32[2,128]{1,0:T(2,128)S(1)} %pad_add_fusion), channel_id=1, source_target_pairs={{0,1},{1,0},{2,3},{3,2},{4,5},{5,4},{6,7},{7,6},{8,9},{9,8},{10,11... | collective-permute-start | bytes 3080 | tf_op jit(solution)/shard_map/ppermute | solution.py:34
  48.2 12.8 %collective-permute-start.7 = (bf16[4,256,512]{2,1,0:T(8,128)(2,1)S(1)}, bf16[4,256,512]{2,1,0:T(8,128)(2,1)S(1)}, u32[]{:S(2)}, u32[]{:S(2)}) collective-permute-start(bf16[4,256,512]{2,1,0:T(8,128)(2,1)S(1)} %shard_map.95.block.refs_0_), channel_id=1, source_target_pairs={{0,8},{1,9},{2,10},{3,11},{4,12},{5,13},{6,14},{7,15},{8,0},{9,1},... | collective-permute-start | bytes 3145736 | tf_op jit(solution)/shard_map/ppermute | solution.py:34
  50.9 15.3 %collective-permute-start.4 = (bf16[4,256,512]{2,1,0:T(8,128)(2,1)S(1)}, bf16[4,256,512]{2,1,0:T(8,128)(2,1)}, u32[]{:S(2)}, u32[]{:S(2)}) collective-permute-start(bf16[4,256,512]{2,1,0:T(8,128)(2,1)S(1)} %shard_map.95.block.refs_0_), channel_id=1, source_target_pairs={{0,6},{1,7},{2,0},{3,1},{4,2},{5,3},{6,4},{7,5},{8,24},{9,25},{10,... | collective-permute-start | bytes 3145736 | tf_op jit(solution)/shard_map/ppermute | solution.py:34
  51.2 15.0 %collective-permute-start.5 = (bf16[4,256,512]{2,1,0:T(8,128)(2,1)S(1)}, bf16[4,256,512]{2,1,0:T(8,128)(2,1)}, u32[]{:S(2)}, u32[]{:S(2)}) collective-permute-start(bf16[4,256,512]{2,1,0:T(8,128)(2,1)S(1)} %shard_map.95.block.refs_0_), channel_id=1, source_target_pairs={{0,32},{1,33},{2,34},{3,35},{4,36},{5,37},{6,38},{7,39},{8,104},{9... | collective-permute-start | bytes 3145736 | tf_op jit(solution)/shard_map/ppermute | solution.py:34
  51.5 14.6 %collective-permute-start.6 = (bf16[4,256,512]{2,1,0:T(8,128)(2,1)S(1)}, bf16[4,256,512]{2,1,0:T(8,128)(2,1)}, u32[]{:S(2)}, u32[]{:S(2)}) collective-permute-start(bf16[4,256,512]{2,1,0:T(8,128)(2,1)S(1)} %shard_map.95.block.refs_0_), channel_id=1, source_target_pairs={{0,2},{1,3},{2,4},{3,5},{4,6},{5,7},{6,0},{7,1},{8,25},{9,24},{10,... | collective-permute-start | bytes 3145736 | tf_op jit(solution)/shard_map/ppermute | solution.py:34
  66.1 7.0 %collective-permute-start.8 = (bf16[4,256,512]{2,1,0:T(8,128)(2,1)}, bf16[4,256,512]{2,1,0:T(8,128)(2,1)S(1)}, u32[]{:S(2)}, u32[]{:S(2)}) collective-permute-start(bf16[4,256,512]{2,1,0:T(8,128)(2,1)} %collective-permute-done.4.refs_0_.refs_1_), channel_id=1, source_target_pairs={{0,8},{1,9},{2,10},{3,11},{4,12},{5,13},{6,14},{7,15},{8,0},{9,1},... | collective-permute-start | bytes 3145736 | tf_op jit(solution)/shard_map/ppermute | solution.py:34
  68.1 5.0 %collective-permute-start.9 = (bf16[4,256,512]{2,1,0:T(8,128)(2,1)}, bf16[4,256,512]{2,1,0:T(8,128)(2,1)S(1)}, u32[]{:S(2)}, u32[]{:S(2)}) collective-permute-start(bf16[4,256,512]{2,1,0:T(8,128)(2,1)} %collective-permute-done.5.refs_1_.refs_2_), channel_id=1, source_target_pairs={{0,8},{1,9},{2,10},{3,11},{4,12},{5,13},{6,14},{7,15},{8,0},{9,1},... | collective-permute-start | bytes 3145736 | tf_op jit(solution)/shard_map/ppermute | solution.py:34
  68.1 5.5 %collective-permute-start.10 = (bf16[4,256,512]{2,1,0:T(8,128)(2,1)}, bf16[4,256,512]{2,1,0:T(8,128)(2,1)S(1)}, u32[]{:S(2)}, u32[]{:S(2)}) collective-permute-start(bf16[4,256,512]{2,1,0:T(8,128)(2,1)} %collective-permute-done.6.refs_2_.refs_3_), channel_id=1, source_target_pairs={{0,8},{1,9},{2,10},{3,11},{4,12},{5,13},{6,14},{7,15},{8,0},{9,1},... | collective-permute-start | bytes 3145736 | tf_op jit(solution)/shard_map/ppermute | solution.py:34
  100.0 2.7 %collective-permute-start.11 = (bf16[4,256,512]{2,1,0:T(8,128)(2,1)S(1)}, bf16[4,256,512]{2,1,0:T(8,128)(2,1)S(1)}, u32[]{:S(2)}, u32[]{:S(2)}) collective-permute-start(bf16[4,256,512]{2,1,0:T(8,128)(2,1)S(1)} %get-tuple-element.57), channel_id=1, source_target_pairs={{0,8},{1,9},{2,10},{3,11},{4,12},{5,13},{6,14},{7,15},{8,0},{9,1},... | collective-permute-start | bytes 3145736 | tf_op jit(solution)/shard_map/ppermute | solution.py:34
  100.4 4.7 %collective-permute-start.14 = (bf16[4,256,512]{2,1,0:T(8,128)(2,1)S(1)}, bf16[4,256,512]{2,1,0:T(8,128)(2,1)S(1)}, u32[]{:S(2)}, u32[]{:S(2)}) collective-permute-start(bf16[4,256,512]{2,1,0:T(8,128)(2,1)S(1)} %get-tuple-element.63), channel_id=1, source_target_pairs={{0,8},{1,9},{2,10},{3,11},{4,12},{5,13},{6,14},{7,15},{8,0},{9,1},... | collective-permute-start | bytes 3145736 | tf_op jit(solution)/shard_map/ppermute | solution.py:34
  102.4 3.9 %collective-permute-start.16 = (bf16[4,256,512]{2,1,0:T(8,128)(2,1)S(1)}, bf16[4,256,512]{2,1,0:T(8,128)(2,1)S(1)}, u32[]{:S(2)}, u32[]{:S(2)}) collective-permute-start(bf16[4,256,512]{2,1,0:T(8,128)(2,1)S(1)} %get-tuple-element.65), channel_id=1, source_target_pairs={{0,8},{1,9},{2,10},{3,11},{4,12},{5,13},{6,14},{7,15},{8,0},{9,1},... | collective-permute-start | bytes 3145736 | tf_op jit(solution)/shard_map/ppermute | solution.py:34
  103.2 17.6 %collective-permute-start.18 = (bf16[4,256,512]{2,1,0:T(8,128)(2,1)S(1)}, bf16[4,256,512]{2,1,0:T(8,128)(2,1)S(1)}, u32[]{:S(2)}, u32[]{:S(2)}) collective-permute-start(bf16[4,256,512]{2,1,0:T(8,128)(2,1)S(1)} %add_convert_fusion.2), channel_id=1, source_target_pairs={{0,6},{1,7},{2,0},{3,1},{4,2},{5,3},{6,4},{7,5},{8,24},{9,25},{10,... | collective-permute-start | bytes 3145736 | tf_op jit(solution)/shard_map/ppermute | solution.py:34
  103.8 3.8 %collective-permute-start.12 = (f32[2,128]{1,0:T(2,128)S(1)}, f32[2,128]{1,0:T(2,128)S(1)}, u32[]{:S(2)}, u32[]{:S(2)}) collective-permute-start(f32[2,128]{1,0:T(2,128)S(1)} %bitcast.46), channel_id=1, source_target_pairs={{0,8},{1,9},{2,10},{3,11},{4,12},{5,13},{6,14},{7,15},{8,0},{9,1},... | collective-permute-start | bytes 3080 | tf_op jit(solution)/shard_map/ppermute | solution.py:34
  105.4 14.0 %collective-permute-start.15 = (bf16[4,256,512]{2,1,0:T(8,128)(2,1)S(1)}, bf16[4,256,512]{2,1,0:T(8,128)(2,1)S(1)}, u32[]{:S(2)}, u32[]{:S(2)}) collective-permute-start(bf16[4,256,512]{2,1,0:T(8,128)(2,1)S(1)} %add_convert_fusion.1), channel_id=1, source_target_pairs={{0,2},{1,3},{2,4},{3,5},{4,6},{5,7},{6,0},{7,1},{8,25},{9,24},{10,... | collective-permute-start | bytes 3145736 | tf_op jit(solution)/shard_map/ppermute | solution.py:34
  106.7 14.0 %collective-permute-start.17 = (bf16[4,256,512]{2,1,0:T(8,128)(2,1)S(1)}, bf16[4,256,512]{2,1,0:T(8,128)(2,1)S(1)}, u32[]{:S(2)}, u32[]{:S(2)}) collective-permute-start(bf16[4,256,512]{2,1,0:T(8,128)(2,1)S(1)} %add_convert_fusion), channel_id=1, source_target_pairs={{0,32},{1,33},{2,34},{3,35},{4,36},{5,37},{6,38},{7,39},{8,104},{9... | collective-permute-start | bytes 3145736 | tf_op jit(solution)/shard_map/ppermute | solution.py:34
  109.4 11.4 %collective-permute-start.13 = (bf16[4,256,512]{2,1,0:T(8,128)(2,1)S(1)}, bf16[4,256,512]{2,1,0:T(8,128)(2,1)S(1)}, u32[]{:S(2)}, u32[]{:S(2)}) collective-permute-start(bf16[4,256,512]{2,1,0:T(8,128)(2,1)S(1)} %get-tuple-element.61), channel_id=1, source_target_pairs={{0,8},{1,9},{2,10},{3,11},{4,12},{5,13},{6,14},{7,15},{8,0},{9,1},... | collective-permute-start | bytes 3145736 | tf_op jit(solution)/shard_map/ppermute | solution.py:34
  123.8 25.2 %all-to-all-start.3 = ((bf16[64,16,640]{2,1,0:T(8,128)(2,1)}), bf16[64,16,640]{2,1,0:T(8,128)(2,1)S(1)}, u32[]{:S(2)}, u32[]{:S(2)}) async-start(bf16[64,16,640]{2,1,0:T(8,128)(2,1)} %copy-done.9), calls=%async_computation.3 | async-start | bytes 2621440 | tf_op jit(solution)/shard_map/all_to_all | solution.py:399
  129.6 28.3 %collective-permute-start.19 = (bf16[1,128,2048]{2,1,0:T(8,128)(2,1)}, bf16[1,128,2048]{2,1,0:T(8,128)(2,1)}, u32[]{:S(2)}, u32[]{:S(2)}) collective-permute-start(bf16[1,128,2048]{2,1,0:T(8,128)(2,1)} %param.8), channel_id=1, source_target_pairs={{8,0},{9,1},{10,2},{11,3},{12,4},{13,5},{14,6},{15,7},{16,8},{17,9... | collective-permute-start | bytes 1572872 | tf_op jit(solution)/shard_map/ppermute | solution.py:34
  150.6 16.7 %all-to-all-start.4 = ((bf16[16,8,2048]{2,1,0:T(8,128)(2,1)}), bf16[16,8,2048]{2,1,0:T(8,128)(2,1)S(1)}, u32[]{:S(2)}, u32[]{:S(2)}) async-start(bf16[16,8,2048]{2,1,0:T(8,128)(2,1)} %get-tuple-element.73), calls=%async_computation.4 | async-start | bytes 1048576 | tf_op jit(solution)/shard_map/all_to_all | solution.py:406
  (21 other events, 145.7 us)

commit v5 on v4

v5 whole, which is shorter than its diff:
```python
import functools

import jax
import jax.numpy as jnp
import numpy as np
from jax import lax
from jax.experimental import pallas as pl
from jax.experimental.pallas import tpu as pltpu
from jax.sharding import Mesh, PartitionSpec as P

NORM_EPS = 1e-05
AXES = ("y", "zl", "c", "x", "zh")
SIZES = (4, 2, 2, 4, 2)
CHIPS = ("x", "y", "zl", "zh")
PIPE = ("y", "zl", "c")
F32, BF16 = jnp.float32, jnp.bfloat16
NT = (((1,), (1,)), ((), ()))
LIMIT = 16 << 20
COLOURS = [(x + 2 * y + 3 * (2 * zh + zl)) % 4 for x in range(4) for y in range(4) for zl in range(2) for zh in range(2)]


def route(step):
    pairs = []
    for source in range(128):
        y, zl, c, x, zh = (int(i) for i in np.unravel_index(source, SIZES))
        there = step(y, 2 * zh + zl, c, x)
        if there is not None:
            y, z, c, x = there[0] % 4, there[1] % 4, there[2] % 2, there[3] % 4
            pairs.append((source, int(np.ravel_multi_index((y, z % 2, c, x, z // 2), SIZES))))
    return pairs


def move(block, step):
    return lax.ppermute(block, AXES, route(step))


def other_core(block):
    return move(block, lambda y, z, c, x: (y, z, 1 - c, x))


def to_colour(block, away):
    if away == 1:
        return move(block, lambda y, z, c, x: (y, z - 1, c, x) if c else (y, z, c, x + 1))
    if away == 3:
        return move(block, lambda y, z, c, x: (y, z + 1, c, x) if c else (y, z, c, x - 1))
    return move(block, lambda y, z, c, x: (y - 1 if c else y + 1, z, c, x))


def back_one(y, z, c, x):
    section = (y * 2 + z % 2) * 2 + c - 1
    return None if section < 0 else (section // 4, z // 2 * 2 + section // 2 % 2, section % 2, x)


def call(kernel, scalars, operands, outs, flops=0, moved=1 << 20):
    vmem = pl.BlockSpec(memory_space=pltpu.VMEM)
    smem = [] if scalars is None else [pl.BlockSpec(memory_space=pltpu.SMEM)]
    held = [pltpu.with_memory_space_constraint(o, pltpu.VMEM) for o in operands]
    return pl.pallas_call(
        kernel,
        in_specs=smem + [vmem] * len(operands),
        out_specs=[vmem] * len(outs),
        out_shape=[(jax.ShapeDtypeStruct if place else pltpu.VMEM)(shape, kind) for shape, kind, *place in outs],
        cost_estimate=pl.CostEstimate(flops=flops, bytes_accessed=moved, transcendentals=0),
        compiler_params=pltpu.CompilerParams(vmem_limit_bytes=LIMIT),
    )(*([] if scalars is None else [scalars]), *held)


def columns(tint, t, away):
    return pl.ds(pl.multiple_of(t * 2048 + tint[away] * 512, 512), 512)


def diagonal():
    return lax.broadcasted_iota(jnp.int32, (16, 128), 0) == lax.broadcasted_iota(jnp.int32, (16, 128), 1)


def slots_kernel(rows, out):
    wide = rows[...].astype(F32)
    squares = jnp.sum(wide * wide, axis=1, keepdims=True)
    along = jnp.sum(jnp.where(diagonal(), squares, 0.0), axis=0, keepdims=True)
    extra = jnp.concatenate([*three_parts(along), jnp.zeros((5, 128), F32)], axis=0).astype(BF16)
    for chip, colour in enumerate(COLOURS):
        for i in range(4):
            start = colour * 512 + i * 128
            out[chip, i * 16 : (i + 1) * 16, :] = rows[:, start : start + 128]
        out[chip, 64:, :] = extra


def slots_call(rows):
    return call(slots_kernel, None, [rows], [((64, 72, 128), BF16, True)])[0]


def inverse_of(came, group):
    squares = sum(came[t * 16 + group, 64:, :].astype(F32) for t in range(4))
    along = jnp.sum(squares, axis=0, keepdims=True)
    squares = jnp.sum(jnp.where(diagonal(), along, 0.0), axis=1, keepdims=True)
    return lax.rsqrt(squares / 8192 + NORM_EPS)


def norm_kernel(came, gain, own):
    for group in range(16):
        span = slice(group * 16, (group + 1) * 16)
        inverse = inverse_of(came, group)
        for t in range(4):
            for i in range(4):
                unit = came[t * 16 + group, i * 16 : (i + 1) * 16, :].astype(F32) * inverse
                lanes = slice(i * 128, (i + 1) * 128)
                own[t, span, lanes] = (unit * gain[t : t + 1, lanes]).astype(BF16)


def norm_call(came, gain):
    return call(norm_kernel, None, [came, gain], [((4, 256, 512), BF16)], moved=2 << 20)[0]


def near_columns(t, away):
    return away * 4 + t


def early_kernel(tint, head, head_2, block, total, near, sems):
    copies = []
    for away in range(4):
        for t in range(4):
            at = near_columns(t, away)
            copies.append(pltpu.make_async_copy(head_2.at[:, columns(tint, t, away)], near.at[at], sems.at[at]))
            copies[-1].start()
    for t in range(4):
        part = lax.dot_general(head[:, columns(tint, t, 0)], block[t], NT, preferred_element_type=F32)
        total[:512, :] = part if t == 0 else total[:512, :] + part
    for t in range(4):
        copies[t].wait()
        part = lax.dot_general(near[near_columns(t, 0)], block[t], NT, preferred_element_type=F32)
        total[512:, :] = part if t == 0 else total[512:, :] + part
    for copy in copies[4:]:
        copy.wait()


def early_call(tint, head, head_2, block):
    vmem, anywhere = pl.BlockSpec(memory_space=pltpu.VMEM), pl.BlockSpec(memory_space=pl.ANY)
    return pl.pallas_call(
        early_kernel,
        in_specs=[pl.BlockSpec(memory_space=pltpu.SMEM), vmem, anywhere, vmem],
        out_specs=[vmem] * 2,
        out_shape=[pltpu.VMEM((1024, 256), F32), pltpu.VMEM((16, 512, 512), BF16)],
        scratch_shapes=[pltpu.SemaphoreType.DMA((16,))],
        cost_estimate=pl.CostEstimate(flops=2 * 1024 * 256 * 2048, bytes_accessed=9 << 20, transcendentals=0),
        compiler_params=pltpu.CompilerParams(vmem_limit_bytes=LIMIT),
    )(
        tint,
        pltpu.with_memory_space_constraint(head, pltpu.VMEM),
        pltpu.with_memory_space_constraint(head_2, pltpu.HBM),
        pltpu.with_memory_space_constraint(block, pltpu.VMEM),
    )


def last_kernel(tint, head, near, block_1, block_2, block_3, early, logits, lse, total):
    def step(t, first):
        for i in range(2):
            part = None
            for away, block in ((1, block_1), (2, block_2), (3, block_3)):
                side = near[near_columns(t, away)] if i else head[:, columns(tint, t, away)]
                term = lax.dot_general(side, block[t], NT, preferred_element_type=F32)
                part = term if part is None else part + term
            span = slice(i * 512, (i + 1) * 512)
            total[span, :] = part if first else total[span, :] + part

    step(0, True)

    @pl.loop(1, 4)
    def _(t):
        step(t, False)

    values = early[...] + total[...]
    logits[...] = values
    top = jnp.max(values, axis=0, keepdims=True)
    sums = top + jnp.log(jnp.sum(jnp.exp(values - top), axis=0, keepdims=True))
    sums = jnp.concatenate([sums[:, :128], sums[:, 128:]], axis=0)
    lse[...] = jnp.broadcast_to(sums[None], (64, 2, 128))


def last_call(tint, heads, blocks, early):
    outs = [((1024, 256), F32, jax.ShapeDtypeStruct), ((64, 2, 128), F32, jax.ShapeDtypeStruct), ((1024, 256), F32)]
    return call(last_kernel, tint, [*heads, *blocks, early], outs, 6 * 1024 * 256 * 2048, 17 << 20)[:2]


def product(tint, dlogits, heads, away, out):
    @pl.loop(0, 4)
    def _(t):
        value = jnp.dot(dlogits[:, :512], heads[0][:, columns(tint, t, away)], preferred_element_type=F32)
        value += jnp.dot(dlogits[:, 512:], heads[1][near_columns(t, away)], preferred_element_type=F32)
        out[t] = value.astype(out.dtype)


def turn_kernel(tint, logits, head, head_2, parts, labels, weights, turned, dlogits, inner, out, held, sem):
    copy = pltpu.make_async_copy(logits, held, sem)
    copy.start()
    lse = parts[...]
    top = jnp.max(lse, axis=0)
    log_total = top + jnp.log(jnp.sum(jnp.exp(lse - top[None]), axis=0))
    log_total = jnp.concatenate([log_total[:1], log_total[1:]], axis=1)
    copy.wait()
    for i in range(2):
        span = slice(i * 512, (i + 1) * 512)
        probs = jnp.exp(held[span, :] - log_total)
        ids = tint[5 + i] * 512 + lax.broadcasted_iota(jnp.int32, (512, 256), 0)
        hot = jnp.where(ids == labels[...], 1.0, 0.0)
        values = (weights[...] * (probs - hot)).astype(BF16)
        turned[span, :] = values
        dlogits[:, span] = values.T
        part = jnp.sum(values.astype(F32) * held[span, :], axis=0, keepdims=True)
        inner[...] = part if i == 0 else inner[...] + part
    product(tint, dlogits, (head, head_2), 1, out)


def turn_call(tint, logits, heads, parts, labels, weights):
    vmem = pl.BlockSpec(memory_space=pltpu.VMEM)
    return pl.pallas_call(
        turn_kernel,
        in_specs=[pl.BlockSpec(memory_space=pltpu.SMEM), pl.BlockSpec(memory_space=pl.ANY)] + [vmem] * 5,
        out_specs=[vmem] * 4,
        out_shape=[
            pltpu.VMEM((1024, 256), BF16),
            pltpu.VMEM((256, 1024), BF16),
            jax.ShapeDtypeStruct((1, 256), F32),
            pltpu.VMEM((4, 256, 512), BF16),
        ],
        scratch_shapes=[pltpu.VMEM((1024, 256), F32), pltpu.SemaphoreType.DMA],
        cost_estimate=pl.CostEstimate(flops=2 * 1024 * 256 * 2048, bytes_accessed=5 << 20, transcendentals=0),
        compiler_params=pltpu.CompilerParams(vmem_limit_bytes=LIMIT),
    )(tint, logits, *[pltpu.with_memory_space_constraint(h, pltpu.VMEM) for h in heads], parts, labels, weights)


def back_kernel(away, tint, dlogits, head, head_2, out):
    product(tint, dlogits, (head, head_2), away, out)


def back_call(tint, dlogits, heads, away, kind=BF16):
    kernel = functools.partial(back_kernel, away)
    return call(kernel, tint, [dlogits, *heads], [((4, 256, 512), kind)], 2 * 1024 * 256 * 2048, 4 << 20)[0]


def head_kernel(tint, turned, turned_2, *refs):
    out = refs[-1]
    for away in range(4):
        own, other = refs[away], refs[4 + away]
        value = jnp.dot(turned[...], own[0], preferred_element_type=F32)
        value += jnp.dot(turned_2[...], other[0], preferred_element_type=F32)
        out[:, pl.ds(pl.multiple_of(tint[away] * 512, 512), 512)] = value.astype(BF16)


def head_call(tint, turned, turned_2, own, other):
    block = pl.BlockSpec((1, 256, 512), lambda t, tint: (t, 0, 0))
    return pl.pallas_call(
        head_kernel,
        grid_spec=pltpu.PrefetchScalarGridSpec(
            num_scalar_prefetch=1,
            grid=(4,),
            in_specs=[pl.BlockSpec((512, 256), lambda t, tint: (0, 0))] * 2 + [block] * 8,
            out_specs=pl.BlockSpec((512, 2048), lambda t, tint: (0, t)),
        ),
        out_shape=jax.ShapeDtypeStruct((512, 8192), BF16),
        cost_estimate=pl.CostEstimate(flops=2 * 512 * 512 * 8192, bytes_accessed=17 << 20, transcendentals=0),
        compiler_params=pltpu.CompilerParams(vmem_limit_bytes=LIMIT),
    )(tint, turned, turned_2, *own, *other)


def three_parts(value):
    high = value.astype(BF16).astype(F32)
    middle = (value - high).astype(BF16).astype(F32)
    return high, middle, value - high - middle


def join_kernel(came, ours, one, two, three, inner, out, inverse_rms, slots, sems):
    for group in range(16):
        inverse_rms[group * 16 : (group + 1) * 16, :] = jnp.broadcast_to(inverse_of(came, group), (16, 128))
    products = [part[i : i + 1] for part in three_parts(inner[...]) for i in range(2)]
    copies = []
    for t in range(4):
        gain = jnp.zeros((1, 512), F32)
        for group in range(16):
            span = slice(group * 16, (group + 1) * 16)
            total = ours[t, span] + one[t, span].astype(F32) + two[t, span].astype(F32) + three[t, span].astype(F32)
            slots[t * 16 + group, :, :512] = total.astype(BF16)
            pieces = [came[t * 16 + group, i * 16 : (i + 1) * 16, :] for i in range(4)]
            unit = jnp.concatenate(pieces, axis=1).astype(F32) * inverse_rms[span, :1]
            gain += jnp.sum(total * unit, axis=0, keepdims=True)
        parts = [part[:, i * 128 : (i + 1) * 128] for part in three_parts(gain)[:2] for i in range(4)]
        extra = jnp.concatenate(parts + products + [jnp.zeros((2, 128), F32)], axis=0).astype(BF16)
        for group in range(16):
            slots[t * 16 + group, :, 512:] = extra
        span = pl.ds(t * 16, 16)
        copies.append(pltpu.make_async_copy(slots.at[span], out.at[span], sems.at[t]))
        copies[-1].start()
    for copy in copies:
        copy.wait()


def join_call(*operands):
    vmem = pl.BlockSpec(memory_space=pltpu.VMEM)
    return pl.pallas_call(
        join_kernel,
        in_specs=[vmem] * len(operands),
        out_specs=[pl.BlockSpec(memory_space=pl.ANY), vmem],
        out_shape=[pltpu.HBM((64, 16, 640), BF16), pltpu.VMEM((256, 128), F32)],
        scratch_shapes=[pltpu.VMEM((64, 16, 640), BF16), pltpu.SemaphoreType.DMA((4,))],
        cost_estimate=pl.CostEstimate(flops=0, bytes_accessed=6 << 20, transcendentals=0),
        compiler_params=pltpu.CompilerParams(vmem_limit_bytes=LIMIT),
    )(*[pltpu.with_memory_space_constraint(o, pltpu.VMEM) for o in operands])


def tail_kernel(info, terms, rows, inverse_rms, gain, placed, gain_grad):
    sums = [None] * 4
    for chip, colour in enumerate(COLOURS):
        term = terms[chip].astype(F32)
        sums[colour] = term if sums[colour] is None else sums[colour] + term
    products = sum(s[8:14, 512:] for s in sums)
    lane = lax.broadcasted_iota(jnp.int32, (16, 128), 1)
    row = info[2] * 16 + lax.broadcasted_iota(jnp.int32, (16, 128), 0)
    here = [jnp.where(lane + 128 * (i % 2) == row, products[i : i + 1], 0.0) for i in range(6)]
    inner = jnp.sum(sum(here), axis=1, keepdims=True) / 8192
    inverse = inverse_rms[:, :1]
    for colour, total in enumerate(sums):
        span = slice(colour * 512, (colour + 1) * 512)
        gain_grad[colour * 4 : (colour + 1) * 4, :] = total[:4, 512:] + total[4:8, 512:]
        unit = rows[:, span].astype(F32) * inverse
        exit_grad = inverse * (total[:, :512] * gain[:, span] - unit * inner)
        for section in range(16):
            value = jnp.where(info[0] == section, exit_grad[:8], jnp.where(info[1] == section, exit_grad[8:], 0.0))
            placed[section, :, span] = value.astype(BF16)


def tail_call(info, *operands):
    outs = [((16, 8, 2048), BF16, True), ((16, 128), F32)]
    return call(tail_kernel, info, operands, outs, moved=2 << 20)


def hold_kernel(source, out):
    out[...] = source[...]


def add_kernel(exits, from_next, out):
    out[...] = (exits[...].astype(F32) + from_next[...].astype(F32)).astype(BF16)


def local(hidden, section_cotangent, norm_gain, head, labels, loss_mask, exit_on):
    core, x, y, zl, zh = (lax.axis_index(a) for a in ("c", "x", "y", "zl", "zh"))
    device = lax.axis_index(AXES).astype(jnp.int32)
    colour = (x + 2 * y + 3 * (2 * zh + zl)) % 4
    aways = (colour + jnp.arange(4, dtype=jnp.int32)) % 4
    tint = jnp.concatenate([aways, core.reshape(1), device.reshape(1), (device + 8 - 16 * core).reshape(1)]).astype(jnp.int32)

    heads = [head, other_core(head)]
    came = lax.all_to_all(hidden.reshape(16, 8, 2048), PIPE, 0, 0, tiled=True)
    section_ids = jnp.arange(16, dtype=jnp.int32)
    first = jnp.min(jnp.where(exit_on == 1, section_ids, 16))
    second = jnp.max(jnp.where(exit_on == 1, section_ids, -1))
    chosen = jnp.stack([first, second])
    scores = (chosen + 1).astype(F32)
    weights = scores / jnp.sum(scores)

    rows = jnp.concatenate([lax.dynamic_index_in_dim(came, s, 0, False) for s in (first, second)])
    norm_gain, rows = lax.optimization_barrier((norm_gain, rows))
    turns = [norm_gain] + [move(norm_gain, lambda y, z, c, x, k=k: (y, z, c, x + k)) for k in (1, 2, 3)]
    ring = jnp.stack(turns[::-1] * 2)
    gain = lax.dynamic_slice(ring, ((3 - x) % 4, colour * 512), (4, 512))
    token_info, rows = lax.optimization_barrier((jnp.stack([labels, loss_mask]), rows))
    other_info = move(token_info, lambda y, z, c, x: (y, z + 2, c, x))
    both = jnp.where(zh == 0, jnp.stack([token_info, other_info]), jnp.stack([other_info, token_info]))
    by_row = jnp.broadcast_to(
        both.reshape(2, 2, 4, 2, 2, 8).transpose(4, 1, 2, 3, 0, 5)[:, :, :, :, :, None], (2, 2, 4, 2, 2, 2, 8)
    )
    by_row = jnp.where(core == 0, by_row[0], by_row[1])
    row_labels = by_row[0].reshape(1, 256)
    row_weights = (weights[:, None] * by_row[1].astype(F32)).reshape(1, 256)

    quarter = lax.all_to_all(slots_call(rows), CHIPS, 0, 0, tiled=True)
    quarter, row_labels, row_weights, gain = lax.optimization_barrier((quarter, row_labels, row_weights, gain))
    own = norm_call(quarter, gain)

    blocks = [own, to_colour(own, 3), to_colour(own, 2), to_colour(own, 1)]
    early, near = early_call(tint, *heads, own)
    heads = [head, near]
    *blocks[1:], early = lax.optimization_barrier((*blocks[1:], early))
    logits, lse = last_call(tint, heads, blocks[1:], early)
    parts = lax.all_to_all(lse, CHIPS, 0, 0, tiled=True)
    turned, dlogits, inner, product_1 = turn_call(tint, logits, heads, parts, row_labels, row_weights)

    sums = [product_1] + [back_call(tint, dlogits, heads, away) for away in (2, 3)]
    arrived = [to_colour(s, away) for s, away in zip(sums, (1, 2, 3))]
    late, _ = lax.optimization_barrier((dlogits, sums[2]))
    ours = back_call(tint, late, heads, 0, F32)
    ours, turned, *blocks = lax.optimization_barrier((ours, turned, *blocks))
    turned_2 = other_core(turned[512:])
    mates = [other_core(b) for b in blocks]
    inner = inner.reshape(2, 128)
    slots, inverse_rms = join_call(quarter, ours, *arrived, inner)
    terms = lax.all_to_all(slots, CHIPS, 0, 0, tiled=True)
    head_grad = head_call(tint, turned[:512], turned_2, blocks, mates)
    place = (y * 2 + zl) * 2 + zh
    inverse_here = lax.dynamic_slice_in_dim(inverse_rms, place * 16, 16, 0)
    terms, head_grad, inverse_here = lax.optimization_barrier((terms, head_grad, inverse_here))
    info = jnp.concatenate([chosen, place.reshape(1)]).astype(jnp.int32)
    placed, gain_grad = tail_call(info, terms, rows, inverse_here, norm_gain.reshape(1, 2048))
    came = lax.all_to_all(placed, PIPE, 0, 0, tiled=True)
    gain_grad = (gain_grad + other_core(gain_grad)).reshape(2048)
    from_next = move(section_cotangent, back_one)
    from_next = call(hold_kernel, None, [from_next[0]], [((128, 2048), BF16)])[0]
    residual_grad = call(add_kernel, None, [came.reshape(128, 2048), from_next], [((128, 2048), BF16, True)])[0][None]
    return head_grad, residual_grad, gain_grad


def solution(mesh):
    fine = Mesh(mesh.devices.reshape(SIZES), AXES)
    in_specs = (
        P(PIPE, "zh", "x"),
        P(PIPE, "zh", "x"),
        P("x"),
        P(AXES, None),
        P("zh"),
        P("zh"),
        P(),
    )
    out_specs = (P(AXES, None), P(PIPE, "zh", "x"), P("x"))
    return jax.shard_map(local, mesh=fine, in_specs=in_specs, out_specs=out_specs, check_vma=False)
```

time: 169 us -> 161 us (0.953)
  waiting for transfers between devices: 35 us -> 22.1 us
  starting transfers between devices: 53.6 us -> 61.5 us
  local copies, waits for them, and re-layouts: 13 us -> 10.2 us
    ppermute x21 -> x18, starting transfers between devices: 23.6 us -> 35.1 us  [move(): return lax.ppermute(block, AXES, route(step))]
    all_to_all x1, waiting for transfers between devices: 11.3 us -> 3.67 us  [local(): quarter = lax.all_to_all(slots_call(rows), CHIPS, 0, 0, tiled=True)]
    ppermute x21 -> x18, waiting for transfers between devices: 15.6 us -> 8.03 us  [move(): return lax.ppermute(block, AXES, route(step))]
    pallas_call x12 -> x9, Pallas kernels: 21.4 us -> 17.9 us  [call(): pl.pallas_call(kernel, in_specs=smem + [vmem] * len(operands), out_specs=...]
    all_to_all x1, waiting for transfers between devices: 0.2 us -> 3.44 us  [local(): came = lax.all_to_all(hidden.reshape(16, 8, 2048), PIPE, 0, 0, tiled=True)]
    unnamed x41 -> x24, local copies, waits for them, and re-layouts: 10.6 us -> 8.18 us
    pallas_call x0 -> x1, Pallas kernels: none -> 1.88 us  [join_call(): pl.pallas_call(join_kernel, in_specs=[vmem] * len(operands), out_specs=[p...]
  transfers between devices with their start and end apart: 25 -> 22, of which waited for: 9 -> 6; matrix products, arithmetic and copies ran while one was open for 6% -> 7% of each run, Pallas kernels for 14% -> 17%
where the time goes in v5:
time: 161 us; the launch traced here: 160 us
  starting transfers between devices  61.5 us (38%)
  Pallas kernels  37.5 us (23%)
  waiting for transfers between devices  22.1 us (14%)
  blocking collectives  14.7 us (9%)
  local copies, waits for them, and re-layouts  10.2 us (6%)
  other arithmetic  8.5 us (5%)
  between operations  5.07 us (3%)
    ppermute x18, starting transfers between devices, move(): return lax.ppermute(block, AXES, route(step))  35.1 us
    pallas_call x9, Pallas kernels, call(): pl.pallas_call(kernel, in_specs=smem + [vmem] * len(operands), out_specs=...  17.9 us
    all_to_all x1, blocking collectives, local(): parts = lax.all_to_all(lse, CHIPS, 0, 0, tiled=True)  14.7 us
    pallas_call x1, Pallas kernels, head_call(): pl.pallas_call(head_kernel, grid_spec=pltpu.PrefetchScalarGridSpec(num_sc...  9.42 us
    all_to_all x1, starting transfers between devices, local(): quarter = lax.all_to_all(slots_call(rows), CHIPS, 0, 0, tiled=True)  9.33 us
    unnamed x24, local copies, waits for them, and re-layouts  8.18 us
    ppermute x18, waiting for transfers between devices, move(): return lax.ppermute(block, AXES, route(step))  8.03 us
    all_to_all x1, waiting for transfers between devices, local(): came = lax.all_to_all(placed, PIPE, 0, 0, tiled=True)  6.96 us
  transfers between devices with their start and end apart: 22, of which 6 were waited for; matrix products, arithmetic and copies ran while one was open for 7% of the time, Pallas kernels for 17%

profile of v5, /device:TPU:1, one launch (start us, length us, event | category | flops | bytes accessed | tf_op | source)
XLA Modules:
  0.0 159.6 jit_solution(15237214766002284369)
XLA Ops:
  2.1 6.0 %all-to-all-start = ((bf16[16,8,2048]{2,1,0:T(8,128)(2,1)}), bf16[16,8,2048]{2,1,0:T(8,128)(2,1)S(1)}, u32[]{:S(2)}, u32[]{:S(2)}) async-start(bf16[16,8,2048]{2,1,0:T(8,128)(2,1)} %bitcast.36), calls=%async_computation | async-start | bytes 1048576 | tf_op jit(solution)/shard_map/all_to_all | solution.py:351
  14.4 3.4 %all-to-all-done = bf16[16,8,2048]{2,1,0:T(8,128)(2,1)S(1)} async-done(((bf16[16,8,2048]{2,1,0:T(8,128)(2,1)}), bf16[16,8,2048]{2,1,0:T(8,128)(2,1)S(1)}, u32[]{:S(2)}, u32[]{:S(2)}) %all-to-all-start) | async-done | bytes 524320 | tf_op jit(solution)/shard_map/all_to_all | solution.py:351
  19.6 9.3 %all-to-all-start.1 = ((bf16[64,72,128]{2,1,0:T(8,128)(2,1)}), bf16[64,72,128]{2,1,0:T(8,128)(2,1)S(1)}, u32[]{:S(2)}, u32[]{:S(2)}) async-start(bf16[64,72,128]{2,1,0:T(8,128)(2,1)} %shard_map.94), calls=%async_computation.1 | async-start | bytes 2359296 | tf_op jit(solution)/shard_map/all_to_all | solution.py:374
  33.1 2.5 %collective-permute-start = (s32[2,128]{1,0:T(2,128)S(1)}, s32[2,128]{1,0:T(2,128)S(1)}, u32[]{:S(2)}, u32[]{:S(2)}) collective-permute-start(s32[2,128]{1,0:T(2,128)S(1)} %pad_add_fusion), channel_id=1, source_target_pairs={{0,1},{1,0},{2,3},{3,2},{4,5},{5,4},{6,7},{7,6},{8,9},{9,8},{10,11... | collective-permute-start | bytes 3080 | tf_op jit(solution)/shard_map/ppermute | solution.py:34
  35.8 2.7 %collective-permute-start.1 = (f32[2048]{0:T(1024)S(1)}, f32[2048]{0:T(1024)S(1)}, u32[]{:S(2)}, u32[]{:S(2)}) collective-permute-start(f32[2048]{0:T(1024)S(1)} %copy-done.10), channel_id=1, source_target_pairs={{0,6},{1,7},{2,0},{3,1},{4,2},{5,3},{6,4},{7,5},{8,14},{9,15},{10,... | collective-permute-start | bytes 24584 | tf_op jit(solution)/shard_map/ppermute | solution.py:34
  40.0 2.6 %collective-permute-done.1 = f32[2048]{0:T(1024)S(1)} collective-permute-done((f32[2048]{0:T(1024)S(1)}, f32[2048]{0:T(1024)S(1)}, u32[]{:S(2)}, u32[]{:S(2)}) %collective-permute-start.1) | collective-permute-done | bytes 8224 | tf_op jit(solution)/shard_map/ppermute | solution.py:34
  44.4 3.7 %all-to-all-done.1.came = bf16[64,72,128]{2,1,0:T(8,128)(2,1)S(1)} async-done(((bf16[64,72,128]{2,1,0:T(8,128)(2,1)}), bf16[64,72,128]{2,1,0:T(8,128)(2,1)S(1)}, u32[]{:S(2)}, u32[]{:S(2)}) %all-to-all-start.1) | async-done | bytes 1179680 | tf_op jit(solution)/shard_map/all_to_all | solution.py:374
  51.3 3.4 %copy-done = bf16[512,8192]{1,0:T(8,128)(2,1)S(1)} copy-done((bf16[512,8192]{1,0:T(8,128)(2,1)S(1)}, bf16[512,8192]{1,0:T(8,128)(2,1)}, u32[]{:S(2)}) %copy-start) | copy-done | bytes 8388632
  54.7 5.3 %shard_map.96 = (f32[1024,256]{1,0:T(8,128)S(1)}, bf16[16,512,512]{2,1,0:T(8,128)(2,1)S(1)}) custom-call(s32[7]{0:T(128)S(1)} %pad_add_fusion.1.tint, bf16[512,8192]{1,0:T(8,128)(2,1)S(1)} %copy-done, bf16[512,8192]{1,0:T(8,128)(2,1)} %collective-permute-done.4.head_2, bf16[4,256,512]{2,1,0:T(8,128)(2,1)S(1)} %shard_map.95.block.refs_0_), custom_call_target="tpu_custom_call" | custom-call | flops 1073741824 | bytes 9437184 | tf_op jit(solution)/shard_map/pallas_call | solution.py:138
  60.0 3.8 %collective-permute-done.5.block_1.refs_1_ = bf16[4,256,512]{2,1,0:T(8,128)(2,1)} collective-permute-done((bf16[4,256,512]{2,1,0:T(8,128)(2,1)S(1)}, bf16[4,256,512]{2,1,0:T(8,128)(2,1)}, u32[]{:S(2)}, u32[]{:S(2)}) %collective-permute-start.5) | collective-permute-done | bytes 1048608 | tf_op jit(solution)/shard_map/ppermute | solution.py:34
  63.8 6.9 %shard_map.97 = (f32[1024,256]{1,0:T(8,128)S(1)}, f32[64,2,128]{2,1,0:T(2,128)S(1)}, f32[1024,256]{1,0:T(8,128)}) custom-call(s32[7]{0:T(128)S(1)} %pad_add_fusion.1.tint, bf16[512,8192]{1,0:T(8,128)(2,1)S(1)} %copy-done.1, bf16[16,512,512]{2,1,0:T(8,128)(2,1)S(1)} %get-tuple-element.43.near.head_2, ...), custom_call_target="tpu_custom_call" | custom-call | flops 3221225472 | bytes 17825792 | tf_op jit(solution)/shard_map/pallas_call | solution.py:58
  70.7 14.7 %all_to_all.25.parts = f32[64,2,128]{2,1,0:T(2,128)S(1)} all-to-all(f32[64,2,128]{2,1,0:T(2,128)S(1)} %get-tuple-element.50), channel_id=1, replica_groups=mesh['y'=4,'zl'=2,'c'=2,'x'=4,'zh'=2] {'x','y','zl','zh'}, dimensions={0} | all-to-all | bytes 131072 | tf_op jit(solution)/shard_map/all_to_all | solution.py:383
  85.5 3.0 %shard_map.98 = (bf16[1024,256]{1,0:T(8,128)(2,1)S(1)}, bf16[256,1024]{1,0:T(8,128)(2,1)S(1)}, f32[1,256]{1,0:T(1,128)S(1)}, bf16[4,256,512]{2,1,0:T(8,128)(2,1)S(1)}) custom-call(s32[7]{0:T(128)S(1)} %pad_add_fusion.1.tint, f32[1024,256]{1,0:T(8,128)S(1)} %get-tuple-element.49.logits, bf16[512,8192]{1,0:T(8,128)(2,1)S(1)} %copy-done.1, ...), custom_call_target="tpu_custom_call" | custom-call | flops 1073741824 | bytes 5242880 | tf_op jit(solution)/shard_map/pallas_call | solution.py:215
  89.4 2.3 %shard_map.101 = bf16[4,256,512]{2,1,0:T(8,128)(2,1)S(1)} custom-call(s32[7]{0:T(128)S(1)} %pad_add_fusion.1.tint, bf16[256,1024]{1,0:T(8,128)(2,1)S(1)} %get-tuple-element.54.dlogits, bf16[512,8192]{1,0:T(8,128)(2,1)S(1)} %copy-done.1, bf16[16,512,512]{2,1,0:T(8,128)(2,1)S(1)} %get-tuple-element.43.near.head_2), custom_call_target="tpu_custom_call" | custom-call | flops 1073741824 | bytes 4194304 | tf_op jit(solution)/shard_map/pallas_call | solution.py:58
  92.7 2.3 %shard_map.99 = bf16[4,256,512]{2,1,0:T(8,128)(2,1)S(1)} custom-call(s32[7]{0:T(128)S(1)} %pad_add_fusion.1.tint, bf16[256,1024]{1,0:T(8,128)(2,1)S(1)} %get-tuple-element.54.dlogits, bf16[512,8192]{1,0:T(8,128)(2,1)S(1)} %copy-done.1, bf16[16,512,512]{2,1,0:T(8,128)(2,1)S(1)} %get-tuple-element.43.near.head_2), custom_call_target="tpu_custom_call" | custom-call | flops 1073741824 | bytes 4194304 | tf_op jit(solution)/shard_map/pallas_call | solution.py:58
  95.6 2.3 %shard_map.100.ours = f32[4,256,512]{2,1,0:T(8,128)S(1)} custom-call(s32[7]{0:T(128)S(1)} %pad_add_fusion.1.tint, bf16[256,1024]{1,0:T(8,128)(2,1)S(1)} %get-tuple-element.54.dlogits, bf16[512,8192]{1,0:T(8,128)(2,1)S(1)} %copy-done.1, bf16[16,512,512]{2,1,0:T(8,128)(2,1)S(1)} %get-tuple-element.43.near.head_2), custom_call_target="tpu_custom_call" | custom-call | flops 1073741824 | bytes 4194304 | tf_op jit(solution)/shard_map/pallas_call | solution.py:58
  97.9 6.2 %collective-permute-start.12 = (bf16[4,256,512]{2,1,0:T(8,128)(2,1)S(1)}, bf16[4,256,512]{2,1,0:T(8,128)(2,1)}, u32[]{:S(2)}, u32[]{:S(2)}) collective-permute-start(bf16[4,256,512]{2,1,0:T(8,128)(2,1)S(1)} %shard_map.95.block.refs_0_), channel_id=1, source_target_pairs={{0,8},{1,9},{2,10},{3,11},{4,12},{5,13},{6,14},{7,15},{8,0},{9,1},... | collective-permute-start | bytes 3145736 | tf_op jit(solution)/shard_map/ppermute | solution.py:34
  104.3 4.9 %collective-permute-start.14 = (bf16[4,256,512]{2,1,0:T(8,128)(2,1)}, bf16[4,256,512]{2,1,0:T(8,128)(2,1)}, u32[]{:S(2)}, u32[]{:S(2)}) collective-permute-start(bf16[4,256,512]{2,1,0:T(8,128)(2,1)} %collective-permute-done.6.block_2.refs_2_), channel_id=1, source_target_pairs={{0,8},{1,9},{2,10},{3,11},{4,12},{5,13},{6,14},{7,15},{8,0},{9,1},... | collective-permute-start | bytes 3145736 | tf_op jit(solution)/shard_map/ppermute | solution.py:34
  109.2 3.0 %collective-permute-start.15 = (bf16[4,256,512]{2,1,0:T(8,128)(2,1)}, bf16[4,256,512]{2,1,0:T(8,128)(2,1)}, u32[]{:S(2)}, u32[]{:S(2)}) collective-permute-start(bf16[4,256,512]{2,1,0:T(8,128)(2,1)} %collective-permute-done.7.block_3.refs_3_), channel_id=1, source_target_pairs={{0,8},{1,9},{2,10},{3,11},{4,12},{5,13},{6,14},{7,15},{8,0},{9,1},... | collective-permute-start | bytes 3145736 | tf_op jit(solution)/shard_map/ppermute | solution.py:34
  114.8 5.4 %all-to-all-start.3 = ((bf16[64,16,640]{2,1,0:T(8,128)(2,1)}), bf16[64,16,640]{2,1,0:T(8,128)(2,1)S(1)}, u32[]{:S(2)}, u32[]{:S(2)}) async-start(bf16[64,16,640]{2,1,0:T(8,128)(2,1)} %get-tuple-element.59), calls=%async_computation.3 | async-start | bytes 2621440 | tf_op jit(solution)/shard_map/all_to_all | solution.py:395
  121.0 5.3 %collective-permute-start.11 = (bf16[512,256]{1,0:T(8,128)(2,1)}, bf16[512,256]{1,0:T(8,128)(2,1)S(1)}, u32[]{:S(2)}, u32[]{:S(2)}) collective-permute-start(bf16[512,256]{1,0:T(8,128)(2,1)} %get-tuple-element.73), channel_id=1, source_target_pairs={{0,8},{1,9},{2,10},{3,11},{4,12},{5,13},{6,14},{7,15},{8,0},{9,1},... | collective-permute-start | bytes 786440 | tf_op jit(solution)/shard_map/ppermute | solution.py:34
  131.6 9.4 %shard_map.103 = bf16[512,8192]{1,0:T(8,128)(2,1)} custom-call(s32[7]{0:T(128)S(1)} %pad_add_fusion.1.tint, bf16[512,256]{1,0:T(8,128)(2,1)S(1)} %get-tuple-element.74.turned, bf16[512,256]{1,0:T(8,128)(2,1)S(1)} %copy-done.9, bf16[4,256,512]{2,1,0:T(8,128)(2,1)S(1)} %shard_map.95.block.refs_0_, bf16[4,256,512]{2,1,0:T(8,128)(2,1)} %collective-permute-done.5.block_1.refs_1_, ...), custom_call_target="tpu_custom_call" | custom-call | flops 4294967296 | bytes 17825792 | tf_op jit(solution)/shard_map/pallas_call | solution.py:251
  143.4 5.7 %all-to-all-start.4 = ((bf16[16,8,2048]{2,1,0:T(8,128)(2,1)}), bf16[16,8,2048]{2,1,0:T(8,128)(2,1)S(1)}, u32[]{:S(2)}, u32[]{:S(2)}) async-start(bf16[16,8,2048]{2,1,0:T(8,128)(2,1)} %get-tuple-element.69), calls=%async_computation.4 | async-start | bytes 1048576 | tf_op jit(solution)/shard_map/all_to_all | solution.py:402
  151.7 7.0 %all-to-all-done.4 = bf16[16,8,2048]{2,1,0:T(8,128)(2,1)S(1)} async-done(((bf16[16,8,2048]{2,1,0:T(8,128)(2,1)}), bf16[16,8,2048]{2,1,0:T(8,128)(2,1)S(1)}, u32[]{:S(2)}, u32[]{:S(2)}) %all-to-all-start.4) | async-done | bytes 524320 | tf_op jit(solution)/shard_map/all_to_all | solution.py:402
  (83 shorter events, 33.5 us)
Async XLA Ops:
  0.6 50.7 %collective-permute-start.4 = (bf16[512,8192]{1,0:T(8,128)(2,1)}, bf16[512,8192]{1,0:T(8,128)(2,1)}, u32[]{:S(2)}, u32[]{:S(2)}) collective-permute-start(bf16[512,8192]{1,0:T(8,128)(2,1)} %head.11), channel_id=1, source_target_pairs={{0,8},{1,9},{2,10},{3,11},{4,12},{5,13},{6,14},{7,15},{8,0},{9,1},... | collective-permute-start | bytes 25165832 | tf_op jit(solution)/shard_map/ppermute | solution.py:34
  2.1 15.7 %all-to-all-start = ((bf16[16,8,2048]{2,1,0:T(8,128)(2,1)}), bf16[16,8,2048]{2,1,0:T(8,128)(2,1)S(1)}, u32[]{:S(2)}, u32[]{:S(2)}) async-start(bf16[16,8,2048]{2,1,0:T(8,128)(2,1)} %bitcast.36), calls=%async_computation | async-start | bytes 1048576 | tf_op jit(solution)/shard_map/all_to_all | solution.py:351
  8.2 27.6 %copy-start.10 = (f32[2048]{0:T(1024)S(1)}, f32[2048]{0:T(1024)}, u32[]{:S(2)}) copy-start(f32[2048]{0:T(1024)} %param.9) | copy-start | bytes 24580
  19.6 28.4 %all-to-all-start.1 = ((bf16[64,72,128]{2,1,0:T(8,128)(2,1)}), bf16[64,72,128]{2,1,0:T(8,128)(2,1)S(1)}, u32[]{:S(2)}, u32[]{:S(2)}) async-start(bf16[64,72,128]{2,1,0:T(8,128)(2,1)} %shard_map.94), calls=%async_computation.1 | async-start | bytes 2359296 | tf_op jit(solution)/shard_map/all_to_all | solution.py:374
  33.1 6.4 %collective-permute-start = (s32[2,128]{1,0:T(2,128)S(1)}, s32[2,128]{1,0:T(2,128)S(1)}, u32[]{:S(2)}, u32[]{:S(2)}) collective-permute-start(s32[2,128]{1,0:T(2,128)S(1)} %pad_add_fusion), channel_id=1, source_target_pairs={{0,1},{1,0},{2,3},{3,2},{4,5},{5,4},{6,7},{7,6},{8,9},{9,8},{10,11... | collective-permute-start | bytes 3080 | tf_op jit(solution)/shard_map/ppermute | solution.py:34
  35.8 6.8 %collective-permute-start.1 = (f32[2048]{0:T(1024)S(1)}, f32[2048]{0:T(1024)S(1)}, u32[]{:S(2)}, u32[]{:S(2)}) collective-permute-start(f32[2048]{0:T(1024)S(1)} %copy-done.10), channel_id=1, source_target_pairs={{0,6},{1,7},{2,0},{3,1},{4,2},{5,3},{6,4},{7,5},{8,14},{9,15},{10,... | collective-permute-start | bytes 24584 | tf_op jit(solution)/shard_map/ppermute | solution.py:34
  38.4 5.8 %collective-permute-start.2 = (f32[2048]{0:T(1024)S(1)}, f32[2048]{0:T(1024)S(1)}, u32[]{:S(2)}, u32[]{:S(2)}) collective-permute-start(f32[2048]{0:T(1024)S(1)} %copy-done.10), channel_id=1, source_target_pairs={{0,4},{1,5},{2,6},{3,7},{4,0},{5,1},{6,2},{7,3},{8,12},{9,13},{10,... | collective-permute-start | bytes 24584 | tf_op jit(solution)/shard_map/ppermute | solution.py:34
  38.8 5.4 %collective-permute-start.3 = (f32[2048]{0:T(1024)S(1)}, f32[2048]{0:T(1024)S(1)}, u32[]{:S(2)}, u32[]{:S(2)}) collective-permute-start(f32[2048]{0:T(1024)S(1)} %copy-done.10), channel_id=1, source_target_pairs={{0,2},{1,3},{2,4},{3,5},{4,6},{5,7},{6,0},{7,1},{8,10},{9,11},{10,... | collective-permute-start | bytes 24584 | tf_op jit(solution)/shard_map/ppermute | solution.py:34
  48.5 15.3 %collective-permute-start.5 = (bf16[4,256,512]{2,1,0:T(8,128)(2,1)S(1)}, bf16[4,256,512]{2,1,0:T(8,128)(2,1)}, u32[]{:S(2)}, u32[]{:S(2)}) collective-permute-start(bf16[4,256,512]{2,1,0:T(8,128)(2,1)S(1)} %shard_map.95.block.refs_0_), channel_id=1, source_target_pairs={{0,6},{1,7},{2,0},{3,1},{4,2},{5,3},{6,4},{7,5},{8,24},{9,25},{10,... | collective-permute-start | bytes 3145736 | tf_op jit(solution)/shard_map/ppermute | solution.py:34
  48.8 15.1 %collective-permute-start.6 = (bf16[4,256,512]{2,1,0:T(8,128)(2,1)S(1)}, bf16[4,256,512]{2,1,0:T(8,128)(2,1)}, u32[]{:S(2)}, u32[]{:S(2)}) collective-permute-start(bf16[4,256,512]{2,1,0:T(8,128)(2,1)S(1)} %shard_map.95.block.refs_0_), channel_id=1, source_target_pairs={{0,32},{1,33},{2,34},{3,35},{4,36},{5,37},{6,38},{7,39},{8,104},{9... | collective-permute-start | bytes 3145736 | tf_op jit(solution)/shard_map/ppermute | solution.py:34
  49.4 14.4 %collective-permute-start.7 = (bf16[4,256,512]{2,1,0:T(8,128)(2,1)S(1)}, bf16[4,256,512]{2,1,0:T(8,128)(2,1)}, u32[]{:S(2)}, u32[]{:S(2)}) collective-permute-start(bf16[4,256,512]{2,1,0:T(8,128)(2,1)S(1)} %shard_map.95.block.refs_0_), channel_id=1, source_target_pairs={{0,2},{1,3},{2,4},{3,5},{4,6},{5,7},{6,0},{7,1},{8,25},{9,24},{10,... | collective-permute-start | bytes 3145736 | tf_op jit(solution)/shard_map/ppermute | solution.py:34
  88.5 15.9 %collective-permute-start.8 = (bf16[4,256,512]{2,1,0:T(8,128)(2,1)S(1)}, bf16[4,256,512]{2,1,0:T(8,128)(2,1)S(1)}, u32[]{:S(2)}, u32[]{:S(2)}) collective-permute-start(bf16[4,256,512]{2,1,0:T(8,128)(2,1)S(1)} %get-tuple-element.57), channel_id=1, source_target_pairs={{0,2},{1,3},{2,4},{3,5},{4,6},{5,7},{6,0},{7,1},{8,25},{9,24},{10,... | collective-permute-start | bytes 3145736 | tf_op jit(solution)/shard_map/ppermute | solution.py:34
  91.7 17.6 %collective-permute-start.9 = (bf16[4,256,512]{2,1,0:T(8,128)(2,1)S(1)}, bf16[4,256,512]{2,1,0:T(8,128)(2,1)S(1)}, u32[]{:S(2)}, u32[]{:S(2)}) collective-permute-start(bf16[4,256,512]{2,1,0:T(8,128)(2,1)S(1)} %shard_map.101), channel_id=1, source_target_pairs={{0,32},{1,33},{2,34},{3,35},{4,36},{5,37},{6,38},{7,39},{8,104},{9... | collective-permute-start | bytes 3145736 | tf_op jit(solution)/shard_map/ppermute | solution.py:34
  95.0 17.2 %collective-permute-start.10 = (bf16[4,256,512]{2,1,0:T(8,128)(2,1)S(1)}, bf16[4,256,512]{2,1,0:T(8,128)(2,1)S(1)}, u32[]{:S(2)}, u32[]{:S(2)}) collective-permute-start(bf16[4,256,512]{2,1,0:T(8,128)(2,1)S(1)} %shard_map.99), channel_id=1, source_target_pairs={{0,6},{1,7},{2,0},{3,1},{4,2},{5,3},{6,4},{7,5},{8,24},{9,25},{10,... | collective-permute-start | bytes 3145736 | tf_op jit(solution)/shard_map/ppermute | solution.py:34
  97.9 32.8 %collective-permute-start.12 = (bf16[4,256,512]{2,1,0:T(8,128)(2,1)S(1)}, bf16[4,256,512]{2,1,0:T(8,128)(2,1)}, u32[]{:S(2)}, u32[]{:S(2)}) collective-permute-start(bf16[4,256,512]{2,1,0:T(8,128)(2,1)S(1)} %shard_map.95.block.refs_0_), channel_id=1, source_target_pairs={{0,8},{1,9},{2,10},{3,11},{4,12},{5,13},{6,14},{7,15},{8,0},{9,1},... | collective-permute-start | bytes 3145736 | tf_op jit(solution)/shard_map/ppermute | solution.py:34
  104.0 26.6 %collective-permute-start.13 = (bf16[4,256,512]{2,1,0:T(8,128)(2,1)}, bf16[4,256,512]{2,1,0:T(8,128)(2,1)}, u32[]{:S(2)}, u32[]{:S(2)}) collective-permute-start(bf16[4,256,512]{2,1,0:T(8,128)(2,1)} %collective-permute-done.5.block_1.refs_1_), channel_id=1, source_target_pairs={{0,8},{1,9},{2,10},{3,11},{4,12},{5,13},{6,14},{7,15},{8,0},{9,1},... | collective-permute-start | bytes 3145736 | tf_op jit(solution)/shard_map/ppermute | solution.py:34
  104.3 26.3 %collective-permute-start.14 = (bf16[4,256,512]{2,1,0:T(8,128)(2,1)}, bf16[4,256,512]{2,1,0:T(8,128)(2,1)}, u32[]{:S(2)}, u32[]{:S(2)}) collective-permute-start(bf16[4,256,512]{2,1,0:T(8,128)(2,1)} %collective-permute-done.6.block_2.refs_2_), channel_id=1, source_target_pairs={{0,8},{1,9},{2,10},{3,11},{4,12},{5,13},{6,14},{7,15},{8,0},{9,1},... | collective-permute-start | bytes 3145736 | tf_op jit(solution)/shard_map/ppermute | solution.py:34
  109.2 21.4 %collective-permute-start.15 = (bf16[4,256,512]{2,1,0:T(8,128)(2,1)}, bf16[4,256,512]{2,1,0:T(8,128)(2,1)}, u32[]{:S(2)}, u32[]{:S(2)}) collective-permute-start(bf16[4,256,512]{2,1,0:T(8,128)(2,1)} %collective-permute-done.7.block_3.refs_3_), channel_id=1, source_target_pairs={{0,8},{1,9},{2,10},{3,11},{4,12},{5,13},{6,14},{7,15},{8,0},{9,1},... | collective-permute-start | bytes 3145736 | tf_op jit(solution)/shard_map/ppermute | solution.py:34
  114.8 26.9 %all-to-all-start.3 = ((bf16[64,16,640]{2,1,0:T(8,128)(2,1)}), bf16[64,16,640]{2,1,0:T(8,128)(2,1)S(1)}, u32[]{:S(2)}, u32[]{:S(2)}) async-start(bf16[64,16,640]{2,1,0:T(8,128)(2,1)} %get-tuple-element.59), calls=%async_computation.3 | async-start | bytes 2621440 | tf_op jit(solution)/shard_map/all_to_all | solution.py:395
  121.0 6.8 %collective-permute-start.11 = (bf16[512,256]{1,0:T(8,128)(2,1)}, bf16[512,256]{1,0:T(8,128)(2,1)S(1)}, u32[]{:S(2)}, u32[]{:S(2)}) collective-permute-start(bf16[512,256]{1,0:T(8,128)(2,1)} %get-tuple-element.73), channel_id=1, source_target_pairs={{0,8},{1,9},{2,10},{3,11},{4,12},{5,13},{6,14},{7,15},{8,0},{9,1},... | collective-permute-start | bytes 786440 | tf_op jit(solution)/shard_map/ppermute | solution.py:34
  128.4 20.8 %collective-permute-start.16 = (bf16[1,128,2048]{2,1,0:T(8,128)(2,1)}, bf16[1,128,2048]{2,1,0:T(8,128)(2,1)S(1)}, u32[]{:S(2)}, u32[]{:S(2)}) collective-permute-start(bf16[1,128,2048]{2,1,0:T(8,128)(2,1)} %param.8), channel_id=1, source_target_pairs={{8,0},{9,1},{10,2},{11,3},{12,4},{13,5},{14,6},{15,7},{16,8},{17,9... | collective-permute-start | bytes 1572872 | tf_op jit(solution)/shard_map/ppermute | solution.py:34
  131.6 10.1 %copy-start.3 = (bf16[16,2048]{1,0:T(8,128)(2,1)S(1)}, bf16[16,2048]{1,0:T(8,128)(2,1)}, u32[]{:S(2)}) copy-start(bf16[16,2048]{1,0:T(8,128)(2,1)} %copy-done.2) | copy-start | bytes 196612
  143.4 15.3 %all-to-all-start.4 = ((bf16[16,8,2048]{2,1,0:T(8,128)(2,1)}), bf16[16,8,2048]{2,1,0:T(8,128)(2,1)S(1)}, u32[]{:S(2)}, u32[]{:S(2)}) async-start(bf16[16,8,2048]{2,1,0:T(8,128)(2,1)} %get-tuple-element.69), calls=%async_computation.4 | async-start | bytes 1048576 | tf_op jit(solution)/shard_map/all_to_all | solution.py:402
  149.1 2.1 %collective-permute-start.17 = (f32[16,128]{1,0:T(8,128)S(1)}, f32[16,128]{1,0:T(8,128)S(1)}, u32[]{:S(2)}, u32[]{:S(2)}) collective-permute-start(f32[16,128]{1,0:T(8,128)S(1)} %get-tuple-element.70), channel_id=1, source_target_pairs={{0,8},{1,9},{2,10},{3,11},{4,12},{5,13},{6,14},{7,15},{8,0},{9,1},... | collective-permute-start | bytes 24584 | tf_op jit(solution)/shard_map/ppermute | solution.py:34
  (10 other events, 25.9 us)

commit v6 on v5

--- a/solution.py
+++ b/solution.py
@@ -116,57 +116,57 @@
 
 
 def early_kernel(tint, head, head_2, block, total, near, sems):
-    copies = []
+    copies = {}
     for away in range(4):
         for t in range(4):
             at = near_columns(t, away)
-            copies.append(pltpu.make_async_copy(head_2.at[:, columns(tint, t, away)], near.at[at], sems.at[at]))
-            copies[-1].start()
+            for i, source in enumerate((head, head_2)):
+                out = near.at[at, pl.ds(i * 512, 512)]
+                copy = pltpu.make_async_copy(source.at[:, columns(tint, t, away)], out, sems.at[i * 16 + at])
+                copy.start()
+                copies[i, at] = copy
     for t in range(4):
-        part = lax.dot_general(head[:, columns(tint, t, 0)], block[t], NT, preferred_element_type=F32)
-        total[:512, :] = part if t == 0 else total[:512, :] + part
-    for t in range(4):
-        copies[t].wait()
-        part = lax.dot_general(near[near_columns(t, 0)], block[t], NT, preferred_element_type=F32)
-        total[512:, :] = part if t == 0 else total[512:, :] + part
-    for copy in copies[4:]:
-        copy.wait()
+        at = near_columns(t, 0)
+        copies[0, at].wait()
+        copies[1, at].wait()
+        part = lax.dot_general(near[at], block[t], NT, preferred_element_type=F32)
+        total[...] = part if t == 0 else total[...] + part
+    for away in range(1, 4):
+        for t in range(4):
+            for i in range(2):
+                copies[i, near_columns(t, away)].wait()
 
 
 def early_call(tint, head, head_2, block):
     vmem, anywhere = pl.BlockSpec(memory_space=pltpu.VMEM), pl.BlockSpec(memory_space=pl.ANY)
     return pl.pallas_call(
         early_kernel,
-        in_specs=[pl.BlockSpec(memory_space=pltpu.SMEM), vmem, anywhere, vmem],
+        in_specs=[pl.BlockSpec(memory_space=pltpu.SMEM), anywhere, anywhere, vmem],
         out_specs=[vmem] * 2,
-        out_shape=[pltpu.VMEM((1024, 256), F32), pltpu.VMEM((16, 512, 512), BF16)],
-        scratch_shapes=[pltpu.SemaphoreType.DMA((16,))],
-        cost_estimate=pl.CostEstimate(flops=2 * 1024 * 256 * 2048, bytes_accessed=9 << 20, transcendentals=0),
+        out_shape=[pltpu.VMEM((1024, 256), F32), pltpu.VMEM((16, 1024, 512), BF16)],
+        scratch_shapes=[pltpu.SemaphoreType.DMA((32,))],
+        cost_estimate=pl.CostEstimate(flops=2 * 1024 * 256 * 2048, bytes_accessed=17 << 20, transcendentals=0),
         compiler_params=pltpu.CompilerParams(vmem_limit_bytes=LIMIT),
     )(
         tint,
-        pltpu.with_memory_space_constraint(head, pltpu.VMEM),
+        pltpu.with_memory_space_constraint(head, pltpu.HBM),
         pltpu.with_memory_space_constraint(head_2, pltpu.HBM),
         pltpu.with_memory_space_constraint(block, pltpu.VMEM),
     )
 
 
-def last_kernel(tint, head, near, block_1, block_2, block_3, early, logits, lse, total):
-    def step(t, first):
-        for i in range(2):
-            part = None
-            for away, block in ((1, block_1), (2, block_2), (3, block_3)):
-                side = near[near_columns(t, away)] if i else head[:, columns(tint, t, away)]
-                term = lax.dot_general(side, block[t], NT, preferred_element_type=F32)
-                part = term if part is None else part + term
-            span = slice(i * 512, (i + 1) * 512)
-            total[span, :] = part if first else total[span, :] + part
-
-    step(0, True)
+def last_kernel(tint, near, block_1, block_2, block_3, early, logits, lse, total):
+    def part(t):
+        return sum(
+            lax.dot_general(near[near_columns(t, away)], block[t], NT, preferred_element_type=F32)
+            for away, block in ((1, block_1), (2, block_2), (3, block_3))
+        )
+
+    total[...] = part(0)
 
     @pl.loop(1, 4)
     def _(t):
-        step(t, False)
+        total[...] += part(t)
 
     values = early[...] + total[...]
     logits[...] = values
@@ -176,20 +176,18 @@
     lse[...] = jnp.broadcast_to(sums[None], (64, 2, 128))
 
 
-def last_call(tint, heads, blocks, early):
+def last_call(tint, near, blocks, early):
     outs = [((1024, 256), F32, jax.ShapeDtypeStruct), ((64, 2, 128), F32, jax.ShapeDtypeStruct), ((1024, 256), F32)]
-    return call(last_kernel, tint, [*heads, *blocks, early], outs, 6 * 1024 * 256 * 2048, 17 << 20)[:2]
-
-
-def product(tint, dlogits, heads, away, out):
+    return call(last_kernel, tint, [near, *blocks, early], outs, 6 * 1024 * 256 * 2048, 17 << 20)[:2]
+
+
+def product(dlogits, near, away, out):
     @pl.loop(0, 4)
     def _(t):
-        value = jnp.dot(dlogits[:, :512], heads[0][:, columns(tint, t, away)], preferred_element_type=F32)
-        value += jnp.dot(dlogits[:, 512:], heads[1][near_columns(t, away)], preferred_element_type=F32)
-        out[t] = value.astype(out.dtype)
-
-
-def turn_kernel(tint, logits, head, head_2, parts, labels, weights, turned, dlogits, inner, out, held, sem):
+        out[t] = jnp.dot(dlogits[...], near[near_columns(t, away)], preferred_element_type=F32).astype(out.dtype)
+
+
+def turn_kernel(tint, logits, near, parts, labels, weights, turned, turned_2, dlogits, inner, out, held, sem):
     copy = pltpu.make_async_copy(logits, held, sem)
     copy.start()
     lse = parts[...]
@@ -203,21 +201,22 @@
         ids = tint[5 + i] * 512 + lax.broadcasted_iota(jnp.int32, (512, 256), 0)
         hot = jnp.where(ids == labels[...], 1.0, 0.0)
         values = (weights[...] * (probs - hot)).astype(BF16)
-        turned[span, :] = values
+        (turned, turned_2)[i][...] = values
         dlogits[:, span] = values.T
         part = jnp.sum(values.astype(F32) * held[span, :], axis=0, keepdims=True)
         inner[...] = part if i == 0 else inner[...] + part
-    product(tint, dlogits, (head, head_2), 1, out)
-
-
-def turn_call(tint, logits, heads, parts, labels, weights):
+    product(dlogits, near, 1, out)
+
+
+def turn_call(tint, logits, near, parts, labels, weights):
     vmem = pl.BlockSpec(memory_space=pltpu.VMEM)
     return pl.pallas_call(
         turn_kernel,
-        in_specs=[pl.BlockSpec(memory_space=pltpu.SMEM), pl.BlockSpec(memory_space=pl.ANY)] + [vmem] * 5,
-        out_specs=[vmem] * 4,
+        in_specs=[pl.BlockSpec(memory_space=pltpu.SMEM), pl.BlockSpec(memory_space=pl.ANY)] + [vmem] * 4,
+        out_specs=[vmem] * 5,
         out_shape=[
-            pltpu.VMEM((1024, 256), BF16),
+            pltpu.VMEM((512, 256), BF16),
+            pltpu.VMEM((512, 256), BF16),
             pltpu.VMEM((256, 1024), BF16),
             jax.ShapeDtypeStruct((1, 256), F32),
             pltpu.VMEM((4, 256, 512), BF16),
@@ -225,16 +224,16 @@
         scratch_shapes=[pltpu.VMEM((1024, 256), F32), pltpu.SemaphoreType.DMA],
         cost_estimate=pl.CostEstimate(flops=2 * 1024 * 256 * 2048, bytes_accessed=5 << 20, transcendentals=0),
         compiler_params=pltpu.CompilerParams(vmem_limit_bytes=LIMIT),
-    )(tint, logits, *[pltpu.with_memory_space_constraint(h, pltpu.VMEM) for h in heads], parts, labels, weights)
-
-
-def back_kernel(away, tint, dlogits, head, head_2, out):
-    product(tint, dlogits, (head, head_2), away, out)
-
-
-def back_call(tint, dlogits, heads, away, kind=BF16):
+    )(tint, logits, pltpu.with_memory_space_constraint(near, pltpu.VMEM), parts, labels, weights)
+
+
+def back_kernel(away, dlogits, near, out):
+    product(dlogits, near, away, out)
+
+
+def back_call(dlogits, near, away, kind=BF16):
     kernel = functools.partial(back_kernel, away)
-    return call(kernel, tint, [dlogits, *heads], [((4, 256, 512), kind)], 2 * 1024 * 256 * 2048, 4 << 20)[0]
+    return call(kernel, None, [dlogits, near], [((4, 256, 512), kind)], 2 * 1024 * 256 * 2048, 4 << 20)[0]
 
 
 def head_kernel(tint, turned, turned_2, *refs):
@@ -278,14 +277,17 @@
         for group in range(16):
             span = slice(group * 16, (group + 1) * 16)
             total = ours[t, span] + one[t, span].astype(F32) + two[t, span].astype(F32) + three[t, span].astype(F32)
-            slots[t * 16 + group, :, :512] = total.astype(BF16)
+            for i in range(4):
+                slots[t * 16 + group, i * 16 : (i + 1) * 16, :] = total[:, i * 128 : (i + 1) * 128].astype(BF16)
             pieces = [came[t * 16 + group, i * 16 : (i + 1) * 16, :] for i in range(4)]
             unit = jnp.concatenate(pieces, axis=1).astype(F32) * inverse_rms[span, :1]
             gain += jnp.sum(total * unit, axis=0, keepdims=True)
-        parts = [part[:, i * 128 : (i + 1) * 128] for part in three_parts(gain)[:2] for i in range(4)]
-        extra = jnp.concatenate(parts + products + [jnp.zeros((2, 128), F32)], axis=0).astype(BF16)
-        for group in range(16):
-            slots[t * 16 + group, :, 512:] = extra
+        high, middle, _ = three_parts(gain)
+        for share in range(8):
+            part = jnp.concatenate([p[:, share * 64 : (share + 1) * 64] for p in (high, middle)], axis=1)
+            extra = jnp.concatenate([part] + products + [jnp.zeros((1, 128), F32)], axis=0).astype(BF16)
+            slots[t * 16 + share * 2, 64:, :] = extra
+            slots[t * 16 + share * 2 + 1, 64:, :] = extra
         span = pl.ds(t * 16, 16)
         copies.append(pltpu.make_async_copy(slots.at[span], out.at[span], sems.at[t]))
         copies[-1].start()
@@ -299,37 +301,45 @@
         join_kernel,
         in_specs=[vmem] * len(operands),
         out_specs=[pl.BlockSpec(memory_space=pl.ANY), vmem],
-        out_shape=[pltpu.HBM((64, 16, 640), BF16), pltpu.VMEM((256, 128), F32)],
-        scratch_shapes=[pltpu.VMEM((64, 16, 640), BF16), pltpu.SemaphoreType.DMA((4,))],
+        out_shape=[pltpu.HBM((64, 72, 128), BF16), pltpu.VMEM((256, 128), F32)],
+        scratch_shapes=[pltpu.VMEM((64, 72, 128), BF16), pltpu.SemaphoreType.DMA((4,))],
         cost_estimate=pl.CostEstimate(flops=0, bytes_accessed=6 << 20, transcendentals=0),
         compiler_params=pltpu.CompilerParams(vmem_limit_bytes=LIMIT),
     )(*[pltpu.with_memory_space_constraint(o, pltpu.VMEM) for o in operands])
 
 
-def tail_kernel(info, terms, rows, inverse_rms, gain, placed, gain_grad):
-    sums = [None] * 4
+def tail_kernel(info, terms, rows, inverse_rms, gain, placed):
+    sums, extra = [[None] * 4 for _ in range(4)], [None] * 4
     for chip, colour in enumerate(COLOURS):
-        term = terms[chip].astype(F32)
-        sums[colour] = term if sums[colour] is None else sums[colour] + term
-    products = sum(s[8:14, 512:] for s in sums)
+        for i in range(4):
+            term = terms[chip, i * 16 : (i + 1) * 16, :].astype(F32)
+            sums[colour][i] = term if sums[colour][i] is None else sums[colour][i] + term
+        term = terms[chip, 64:, :].astype(F32)
+        extra[colour] = term if extra[colour] is None else extra[colour] + term
+    products = sum(extra)[1:7]
     lane = lax.broadcasted_iota(jnp.int32, (16, 128), 1)
     row = info[2] * 16 + lax.broadcasted_iota(jnp.int32, (16, 128), 0)
     here = [jnp.where(lane + 128 * (i % 2) == row, products[i : i + 1], 0.0) for i in range(6)]
     inner = jnp.sum(sum(here), axis=1, keepdims=True) / 8192
     inverse = inverse_rms[:, :1]
-    for colour, total in enumerate(sums):
+    share = jnp.concatenate([e[:1, :64] + e[:1, 64:] for e in extra], axis=1)
+    parts = [part[:, i * 128 : (i + 1) * 128] for part in three_parts(share)[:2] for i in range(2)]
+    beside = jnp.concatenate(parts + [jnp.zeros((4, 128), F32)], axis=0).astype(BF16)
+    for section in range(16):
+        placed[section, :, 2048:] = beside
+    for colour in range(4):
         span = slice(colour * 512, (colour + 1) * 512)
-        gain_grad[colour * 4 : (colour + 1) * 4, :] = total[:4, 512:] + total[4:8, 512:]
         unit = rows[:, span].astype(F32) * inverse
-        exit_grad = inverse * (total[:, :512] * gain[:, span] - unit * inner)
+        total = jnp.concatenate(sums[colour], axis=1)
+        exit_grad = inverse * (total * gain[:, span] - unit * inner)
         for section in range(16):
             value = jnp.where(info[0] == section, exit_grad[:8], jnp.where(info[1] == section, exit_grad[8:], 0.0))
             placed[section, :, span] = value.astype(BF16)
 
 
 def tail_call(info, *operands):
-    outs = [((16, 8, 2048), BF16, True), ((16, 128), F32)]
-    return call(tail_kernel, info, operands, outs, moved=2 << 20)
+    outs = [((16, 8, 2176), BF16, True)]
+    return call(tail_kernel, info, operands, outs, moved=2 << 20)[0]
 
 
 def hold_kernel(source, out):
@@ -337,7 +347,7 @@
 
 
 def add_kernel(exits, from_next, out):
-    out[...] = (exits[...].astype(F32) + from_next[...].astype(F32)).astype(BF16)
+    out[...] = (exits[:, :, :2048].astype(F32) + from_next[...].astype(F32)).astype(BF16)
 
 
 def local(hidden, section_cotangent, norm_gain, head, labels, loss_mask, exit_on):
@@ -347,7 +357,7 @@
     aways = (colour + jnp.arange(4, dtype=jnp.int32)) % 4
     tint = jnp.concatenate([aways, core.reshape(1), device.reshape(1), (device + 8 - 16 * core).reshape(1)]).astype(jnp.int32)
 
-    heads = [head, other_core(head)]
+    head_2 = other_core(head)
     came = lax.all_to_all(hidden.reshape(16, 8, 2048), PIPE, 0, 0, tiled=True)
     section_ids = jnp.arange(16, dtype=jnp.int32)
     first = jnp.min(jnp.where(exit_on == 1, section_ids, 16))
@@ -376,34 +386,35 @@
     own = norm_call(quarter, gain)
 
     blocks = [own, to_colour(own, 3), to_colour(own, 2), to_colour(own, 1)]
-    early, near = early_call(tint, *heads, own)
-    heads = [head, near]
+    early, near = early_call(tint, head, head_2, own)
     *blocks[1:], early = lax.optimization_barrier((*blocks[1:], early))
-    logits, lse = last_call(tint, heads, blocks[1:], early)
+    logits, lse = last_call(tint, near, blocks[1:], early)
     parts = lax.all_to_all(lse, CHIPS, 0, 0, tiled=True)
-    turned, dlogits, inner, product_1 = turn_call(tint, logits, heads, parts, row_labels, row_weights)
-
-    sums = [product_1] + [back_call(tint, dlogits, heads, away) for away in (2, 3)]
+    turned, turned_2, dlogits, inner, product_1 = turn_call(tint, logits, near, parts, row_labels, row_weights)
+
+    sums = [product_1] + [back_call(dlogits, near, away) for away in (2, 3)]
     arrived = [to_colour(s, away) for s, away in zip(sums, (1, 2, 3))]
     late, _ = lax.optimization_barrier((dlogits, sums[2]))
-    ours = back_call(tint, late, heads, 0, F32)
-    ours, turned, *blocks = lax.optimization_barrier((ours, turned, *blocks))
-    turned_2 = other_core(turned[512:])
+    ours = back_call(late, near, 0, F32)
+    turned_2 = other_core(turned_2)
+    ours, turned_2, *blocks = lax.optimization_barrier((ours, turned_2, *blocks))
     mates = [other_core(b) for b in blocks]
     inner = inner.reshape(2, 128)
     slots, inverse_rms = join_call(quarter, ours, *arrived, inner)
     terms = lax.all_to_all(slots, CHIPS, 0, 0, tiled=True)
-    head_grad = head_call(tint, turned[:512], turned_2, blocks, mates)
+    head_grad = head_call(tint, turned, turned_2, blocks, mates)
     place = (y * 2 + zl) * 2 + zh
     inverse_here = lax.dynamic_slice_in_dim(inverse_rms, place * 16, 16, 0)
     terms, head_grad, inverse_here = lax.optimization_barrier((terms, head_grad, inverse_here))
     info = jnp.concatenate([chosen, place.reshape(1)]).astype(jnp.int32)
-    placed, gain_grad = tail_call(info, terms, rows, inverse_here, norm_gain.reshape(1, 2048))
+    placed = tail_call(info, terms, rows, inverse_here, norm_gain.reshape(1, 2048))
     came = lax.all_to_all(placed, PIPE, 0, 0, tiled=True)
-    gain_grad = (gain_grad + other_core(gain_grad)).reshape(2048)
     from_next = move(section_cotangent, back_one)
-    from_next = call(hold_kernel, None, [from_next[0]], [((128, 2048), BF16)])[0]
-    residual_grad = call(add_kernel, None, [came.reshape(128, 2048), from_next], [((128, 2048), BF16, True)])[0][None]
+    from_next = call(hold_kernel, None, [from_next.reshape(16, 8, 2048)], [((16, 8, 2048), BF16)])[0]
+    residual_grad = call(add_kernel, None, [came, from_next], [((16, 8, 2048), BF16, True)])[0].reshape(1, 128, 2048)
+    came, residual_grad = lax.optimization_barrier((came, residual_grad))
+    shares = came[:, :4, 2048:].astype(F32).reshape(8, 2, 2, 4, 64)
+    gain_grad = jnp.sum(shares, axis=(1, 2)).transpose(1, 0, 2).reshape(2048)
     return head_grad, residual_grad, gain_grad
 
 

time: 161 us -> 158 us (0.981)
  local copies, waits for them, and re-layouts: 10.2 us -> 3.3 us
  waiting for transfers between devices: 22.1 us -> 25.9 us
    unnamed x24 -> x10, local copies, waits for them, and re-layouts: 8.18 us -> 1.91 us
    ppermute x18 -> x17, waiting for transfers between devices: 8.03 us -> 9.98 us  [move(): return lax.ppermute(block, AXES, route(step))]
    all_to_all x1, waiting for transfers between devices: 6.96 us -> 8.81 us  [local(): came = lax.all_to_all(placed, PIPE, 0, 0, tiled=True)]
    ppermute x18 -> x17, starting transfers between devices: 35.1 us -> 35.2 us  [move(): return lax.ppermute(block, AXES, route(step))]
  transfers between devices with their start and end apart: 22 -> 21, of which waited for: 6 -> 6; matrix products, arithmetic and copies ran while one was open for 7% -> 5% of each run, Pallas kernels for 17% -> 18%
where the time goes in v6:
time: 158 us; the launch traced here: 157 us
  starting transfers between devices  61.7 us (39%)
  Pallas kernels  38.3 us (24%)
  waiting for transfers between devices  25.9 us (16%)
  blocking collectives  14.7 us (9%)
  other arithmetic  7.89 us (5%)
  between operations  5.05 us (3%)
  local copies, waits for them, and re-layouts  3.3 us (2%)
    ppermute x17, starting transfers between devices, move(): return lax.ppermute(block, AXES, route(step))  35.2 us
    pallas_call x9, Pallas kernels, call(): pl.pallas_call(kernel, in_specs=smem + [vmem] * len(operands), out_specs=...  17.2 us
    all_to_all x1, blocking collectives, local(): parts = lax.all_to_all(lse, CHIPS, 0, 0, tiled=True)  14.7 us
    ppermute x17, waiting for transfers between devices, move(): return lax.ppermute(block, AXES, route(step))  9.98 us
    all_to_all x1, starting transfers between devices, local(): quarter = lax.all_to_all(slots_call(rows), CHIPS, 0, 0, tiled=True)  9.32 us
    pallas_call x1, Pallas kernels, head_call(): pl.pallas_call(head_kernel, grid_spec=pltpu.PrefetchScalarGridSpec(num_sc...  9.24 us
    all_to_all x1, waiting for transfers between devices, local(): came = lax.all_to_all(placed, PIPE, 0, 0, tiled=True)  8.81 us
    pallas_call x1, Pallas kernels, early_call(): pl.pallas_call(early_kernel, in_specs=[pl.BlockSpec(memory_space=pltpu.SM...  6.72 us
  transfers between devices with their start and end apart: 21, of which 6 were waited for; matrix products, arithmetic and copies ran while one was open for 5% of the time, Pallas kernels for 18%

profile of v6, /device:TPU:1, one launch (start us, length us, event | category | flops | bytes accessed | tf_op | source)
XLA Modules:
  0.0 156.9 jit_solution(13770888044753441792)
XLA Ops:
  2.1 6.0 %all-to-all-start = ((bf16[16,8,2048]{2,1,0:T(8,128)(2,1)}), bf16[16,8,2048]{2,1,0:T(8,128)(2,1)S(1)}, u32[]{:S(2)}, u32[]{:S(2)}) async-start(bf16[16,8,2048]{2,1,0:T(8,128)(2,1)} %bitcast.32), calls=%async_computation | async-start | bytes 1048576 | tf_op jit(solution)/shard_map/all_to_all | solution.py:361
  14.3 3.5 %all-to-all-done = bf16[16,8,2048]{2,1,0:T(8,128)(2,1)S(1)} async-done(((bf16[16,8,2048]{2,1,0:T(8,128)(2,1)}), bf16[16,8,2048]{2,1,0:T(8,128)(2,1)S(1)}, u32[]{:S(2)}, u32[]{:S(2)}) %all-to-all-start) | async-done | bytes 524320 | tf_op jit(solution)/shard_map/all_to_all | solution.py:361
  19.0 9.3 %all-to-all-start.1 = ((bf16[64,72,128]{2,1,0:T(8,128)(2,1)}), bf16[64,72,128]{2,1,0:T(8,128)(2,1)S(1)}, u32[]{:S(2)}, u32[]{:S(2)}) async-start(bf16[64,72,128]{2,1,0:T(8,128)(2,1)} %shard_map.94), calls=%async_computation.1 | async-start | bytes 2359296 | tf_op jit(solution)/shard_map/all_to_all | solution.py:384
  28.4 2.0 %fusion.6 = f32[]{:T(128)} fusion(s32[1]{0:T(128)} %bitcast.8, s32[1]{0:T(128)} %bitcast.7), kind=kLoop, calls=%fused_computation.26 | loop fusion | flops 7 | bytes 12 | tf_op jit(solution)/shard_map/reduce_sum | solution.py:367
  30.4 2.1 %broadcast_divide_fusion = f32[2]{0:T(128)S(1)} fusion(f32[]{:T(128)} %fusion.6, s32[1]{0:T(128)} %bitcast.8, s32[1]{0:T(128)} %bitcast.7), kind=kLoop, calls=%fused_computation.25 | loop fusion | flops 8 | bytes 20 | tf_op jit(solution)/shard_map/div | solution.py:367
  32.5 2.5 %collective-permute-start = (s32[2,128]{1,0:T(2,128)S(1)}, s32[2,128]{1,0:T(2,128)S(1)}, u32[]{:S(2)}, u32[]{:S(2)}) collective-permute-start(s32[2,128]{1,0:T(2,128)S(1)} %pad_add_fusion), channel_id=1, source_target_pairs={{0,1},{1,0},{2,3},{3,2},{4,5},{5,4},{6,7},{7,6},{8,9},{9,8},{10,11... | collective-permute-start | bytes 3080 | tf_op jit(solution)/shard_map/ppermute | solution.py:34
  35.1 2.7 %collective-permute-start.1 = (f32[2048]{0:T(1024)S(1)}, f32[2048]{0:T(1024)S(1)}, u32[]{:S(2)}, u32[]{:S(2)}) collective-permute-start(f32[2048]{0:T(1024)S(1)} %copy-done.4), channel_id=1, source_target_pairs={{0,6},{1,7},{2,0},{3,1},{4,2},{5,3},{6,4},{7,5},{8,14},{9,15},{10,... | collective-permute-start | bytes 24584 | tf_op jit(solution)/shard_map/ppermute | solution.py:34
  39.4 2.6 %collective-permute-done.1 = f32[2048]{0:T(1024)S(1)} collective-permute-done((f32[2048]{0:T(1024)S(1)}, f32[2048]{0:T(1024)S(1)}, u32[]{:S(2)}, u32[]{:S(2)}) %collective-permute-start.1) | collective-permute-done | bytes 8224 | tf_op jit(solution)/shard_map/ppermute | solution.py:34
  43.8 3.7 %all-to-all-done.1.came = bf16[64,72,128]{2,1,0:T(8,128)(2,1)S(1)} async-done(((bf16[64,72,128]{2,1,0:T(8,128)(2,1)}), bf16[64,72,128]{2,1,0:T(8,128)(2,1)S(1)}, u32[]{:S(2)}, u32[]{:S(2)}) %all-to-all-start.1) | async-done | bytes 1179680 | tf_op jit(solution)/shard_map/all_to_all | solution.py:384
  48.8 1.8 %collective-permute-start.7 = (bf16[4,256,512]{2,1,0:T(8,128)(2,1)S(1)}, bf16[4,256,512]{2,1,0:T(8,128)(2,1)}, u32[]{:S(2)}, u32[]{:S(2)}) collective-permute-start(bf16[4,256,512]{2,1,0:T(8,128)(2,1)S(1)} %shard_map.95.block.refs_0_), channel_id=1, source_target_pairs={{0,2},{1,3},{2,4},{3,5},{4,6},{5,7},{6,0},{7,1},{8,25},{9,24},{10,... | collective-permute-start | bytes 3145736 | tf_op jit(solution)/shard_map/ppermute | solution.py:34
  50.7 6.7 %shard_map.96 = (f32[1024,256]{1,0:T(8,128)S(1)}, bf16[16,1024,512]{2,1,0:T(8,128)(2,1)S(1)}) custom-call(s32[7]{0:T(128)S(1)} %pad_add_fusion.1.tint, bf16[512,8192]{1,0:T(8,128)(2,1)} %head.1, bf16[512,8192]{1,0:T(8,128)(2,1)} %collective-permute-done.4.head_2, bf16[4,256,512]{2,1,0:T(8,128)(2,1)S(1)} %shard_map.95.block.refs_0_), custom_call_target="tpu_custom_call" | custom-call | flops 1073741824 | bytes 17825792 | tf_op jit(solution)/shard_map/pallas_call | solution.py:142
  57.4 5.8 %collective-permute-done.5.block_1.refs_1_ = bf16[4,256,512]{2,1,0:T(8,128)(2,1)S(1)} collective-permute-done((bf16[4,256,512]{2,1,0:T(8,128)(2,1)S(1)}, bf16[4,256,512]{2,1,0:T(8,128)(2,1)S(1)}, u32[]{:S(2)}, u32[]{:S(2)}) %collective-permute-start.5) | collective-permute-done | bytes 1048608 | tf_op jit(solution)/shard_map/ppermute | solution.py:34
  63.2 6.7 %shard_map.97 = (f32[1024,256]{1,0:T(8,128)S(1)}, f32[64,2,128]{2,1,0:T(2,128)S(1)}, f32[1024,256]{1,0:T(8,128)}) custom-call(s32[7]{0:T(128)S(1)} %pad_add_fusion.1.tint, bf16[16,1024,512]{2,1,0:T(8,128)(2,1)S(1)} %get-tuple-element.44.near, bf16[4,256,512]{2,1,0:T(8,128)(2,1)S(1)} %collective-permute-done.5.block_1.refs_1_, ...), custom_call_target="tpu_custom_call" | custom-call | flops 3221225472 | bytes 17825792 | tf_op jit(solution)/shard_map/pallas_call | solution.py:58
  69.9 14.7 %all_to_all.25.parts = f32[64,2,128]{2,1,0:T(2,128)S(1)} all-to-all(f32[64,2,128]{2,1,0:T(2,128)S(1)} %get-tuple-element.51), channel_id=1, replica_groups=mesh['y'=4,'zl'=2,'c'=2,'x'=4,'zh'=2] {'x','y','zl','zh'}, dimensions={0} | all-to-all | bytes 131072 | tf_op jit(solution)/shard_map/all_to_all | solution.py:392
  84.6 3.0 %shard_map.98 = (bf16[512,256]{1,0:T(8,128)(2,1)S(1)}, bf16[512,256]{1,0:T(8,128)(2,1)S(1)}, bf16[256,1024]{1,0:T(8,128)(2,1)S(1)}, f32[1,256]{1,0:T(1,128)S(1)}, bf16[4,256,512]{2,1,0:T(8,128)(2,1)S(1)}) custom-call(s32[7]{0:T(128)S(1)} %pad_add_fusion.1.tint, f32[1024,256]{1,0:T(8,128)S(1)} %get-tuple-element.50.logits, ...), custom_call_target="tpu_custom_call" | custom-call | flops 1073741824 | bytes 5242880 | tf_op jit(solution)/shard_map/pallas_call | solution.py:213
  93.6 6.1 %collective-permute-start.8 = (bf16[512,256]{1,0:T(8,128)(2,1)S(1)}, bf16[512,256]{1,0:T(8,128)(2,1)S(1)}, u32[]{:S(2)}, u32[]{:S(2)}) collective-permute-start(bf16[512,256]{1,0:T(8,128)(2,1)S(1)} %get-tuple-element.56), channel_id=1, source_target_pairs={{0,8},{1,9},{2,10},{3,11},{4,12},{5,13},{6,14},{7,15},{8,0},{9,1},... | collective-permute-start | bytes 786440 | tf_op jit(solution)/shard_map/ppermute | solution.py:34
  102.3 6.1 %collective-permute-start.14 = (bf16[4,256,512]{2,1,0:T(8,128)(2,1)}, bf16[4,256,512]{2,1,0:T(8,128)(2,1)}, u32[]{:S(2)}, u32[]{:S(2)}) collective-permute-start(bf16[4,256,512]{2,1,0:T(8,128)(2,1)} %collective-permute-done.6.block_2.refs_2_), channel_id=1, source_target_pairs={{0,8},{1,9},{2,10},{3,11},{4,12},{5,13},{6,14},{7,15},{8,0},{9,1},... | collective-permute-start | bytes 3145736 | tf_op jit(solution)/shard_map/ppermute | solution.py:34
  108.4 2.5 %collective-permute-start.15 = (bf16[4,256,512]{2,1,0:T(8,128)(2,1)}, bf16[4,256,512]{2,1,0:T(8,128)(2,1)}, u32[]{:S(2)}, u32[]{:S(2)}) collective-permute-start(bf16[4,256,512]{2,1,0:T(8,128)(2,1)} %collective-permute-done.7.block_3.refs_3_), channel_id=1, source_target_pairs={{0,8},{1,9},{2,10},{3,11},{4,12},{5,13},{6,14},{7,15},{8,0},{9,1},... | collective-permute-start | bytes 3145736 | tf_op jit(solution)/shard_map/ppermute | solution.py:34
  110.9 2.2 %shard_map.102 = (bf16[64,72,128]{2,1,0:T(8,128)(2,1)}, f32[256,128]{1,0:T(8,128)S(1)}) custom-call(bf16[64,72,128]{2,1,0:T(8,128)(2,1)S(1)} %all-to-all-done.1.came, f32[4,256,512]{2,1,0:T(8,128)S(1)} %shard_map.100.ours, bf16[4,256,512]{2,1,0:T(8,128)(2,1)S(1)} %collective-permute-done.9.one, bf16[4,256,512]{2,1,0:T(8,128)(2,1)S(1)} %collective-permute-done.10.two, ...), custom_call_target="tpu_custom_call" | custom-call | bytes 6291456 | tf_op jit(solution)/shard_map/pallas_call | solution.py:300
  113.1 5.3 %all-to-all-start.3 = ((bf16[64,72,128]{2,1,0:T(8,128)(2,1)}), bf16[64,72,128]{2,1,0:T(8,128)(2,1)S(1)}, u32[]{:S(2)}, u32[]{:S(2)}) async-start(bf16[64,72,128]{2,1,0:T(8,128)(2,1)} %get-tuple-element.60), calls=%async_computation.3 | async-start | bytes 2359296 | tf_op jit(solution)/shard_map/all_to_all | solution.py:404
  118.3 6.7 %collective-permute-start.16 = (bf16[1,128,2048]{2,1,0:T(8,128)(2,1)}, bf16[1,128,2048]{2,1,0:T(8,128)(2,1)}, u32[]{:S(2)}, u32[]{:S(2)}) collective-permute-start(bf16[1,128,2048]{2,1,0:T(8,128)(2,1)} %param.8), channel_id=1, source_target_pairs={{8,0},{9,1},{10,2},{11,3},{12,4},{13,5},{14,6},{15,7},{16,8},{17,9... | collective-permute-start | bytes 1572872 | tf_op jit(solution)/shard_map/ppermute | solution.py:34
  128.4 9.2 %shard_map.103 = bf16[512,8192]{1,0:T(8,128)(2,1)} custom-call(s32[7]{0:T(128)S(1)} %pad_add_fusion.1.tint, bf16[512,256]{1,0:T(8,128)(2,1)S(1)} %copy-done.1, bf16[512,256]{1,0:T(8,128)(2,1)S(1)} %copy-done.3, bf16[4,256,512]{2,1,0:T(8,128)(2,1)S(1)} %shard_map.95.block.refs_0_, bf16[4,256,512]{2,1,0:T(8,128)(2,1)S(1)} %collective-permute-done.5.block_1.refs_1_, ...), custom_call_target="tpu_custom_call" | custom-call | flops 4294967296 | bytes 17825792 | tf_op jit(solution)/shard_map/pallas_call | solution.py:250
  139.4 5.9 %all-to-all-start.4 = ((bf16[16,8,2176]{2,1,0:T(8,128)(2,1)}), bf16[16,8,2176]{2,1,0:T(8,128)(2,1)S(1)}, u32[]{:S(2)}, u32[]{:S(2)}) async-start(bf16[16,8,2176]{2,1,0:T(8,128)(2,1)} %shard_map.104), calls=%async_computation.4 | async-start | bytes 1114112 | tf_op jit(solution)/shard_map/all_to_all | solution.py:411
  146.3 8.8 %all-to-all-done.4.exits = bf16[16,8,2176]{2,1,0:T(8,128)(2,1)S(1)} async-done(((bf16[16,8,2176]{2,1,0:T(8,128)(2,1)}), bf16[16,8,2176]{2,1,0:T(8,128)(2,1)S(1)}, u32[]{:S(2)}, u32[]{:S(2)}) %all-to-all-start.4) | async-done | bytes 557088 | tf_op jit(solution)/shard_map/all_to_all | solution.py:411
  (70 shorter events, 26.0 us)
Async XLA Ops:
  0.6 50.1 %collective-permute-start.4 = (bf16[512,8192]{1,0:T(8,128)(2,1)}, bf16[512,8192]{1,0:T(8,128)(2,1)}, u32[]{:S(2)}, u32[]{:S(2)}) collective-permute-start(bf16[512,8192]{1,0:T(8,128)(2,1)} %head.1), channel_id=1, source_target_pairs={{0,8},{1,9},{2,10},{3,11},{4,12},{5,13},{6,14},{7,15},{8,0},{9,1},... | collective-permute-start | bytes 25165832 | tf_op jit(solution)/shard_map/ppermute | solution.py:34
  2.1 15.7 %all-to-all-start = ((bf16[16,8,2048]{2,1,0:T(8,128)(2,1)}), bf16[16,8,2048]{2,1,0:T(8,128)(2,1)S(1)}, u32[]{:S(2)}, u32[]{:S(2)}) async-start(bf16[16,8,2048]{2,1,0:T(8,128)(2,1)} %bitcast.32), calls=%async_computation | async-start | bytes 1048576 | tf_op jit(solution)/shard_map/all_to_all | solution.py:361
  8.2 26.9 %copy-start.4 = (f32[2048]{0:T(1024)S(1)}, f32[2048]{0:T(1024)}, u32[]{:S(2)}) copy-start(f32[2048]{0:T(1024)} %param.9) | copy-start | bytes 24580
  19.0 28.4 %all-to-all-start.1 = ((bf16[64,72,128]{2,1,0:T(8,128)(2,1)}), bf16[64,72,128]{2,1,0:T(8,128)(2,1)S(1)}, u32[]{:S(2)}, u32[]{:S(2)}) async-start(bf16[64,72,128]{2,1,0:T(8,128)(2,1)} %shard_map.94), calls=%async_computation.1 | async-start | bytes 2359296 | tf_op jit(solution)/shard_map/all_to_all | solution.py:384
  32.5 6.4 %collective-permute-start = (s32[2,128]{1,0:T(2,128)S(1)}, s32[2,128]{1,0:T(2,128)S(1)}, u32[]{:S(2)}, u32[]{:S(2)}) collective-permute-start(s32[2,128]{1,0:T(2,128)S(1)} %pad_add_fusion), channel_id=1, source_target_pairs={{0,1},{1,0},{2,3},{3,2},{4,5},{5,4},{6,7},{7,6},{8,9},{9,8},{10,11... | collective-permute-start | bytes 3080 | tf_op jit(solution)/shard_map/ppermute | solution.py:34
  35.1 6.9 %collective-permute-start.1 = (f32[2048]{0:T(1024)S(1)}, f32[2048]{0:T(1024)S(1)}, u32[]{:S(2)}, u32[]{:S(2)}) collective-permute-start(f32[2048]{0:T(1024)S(1)} %copy-done.4), channel_id=1, source_target_pairs={{0,6},{1,7},{2,0},{3,1},{4,2},{5,3},{6,4},{7,5},{8,14},{9,15},{10,... | collective-permute-start | bytes 24584 | tf_op jit(solution)/shard_map/ppermute | solution.py:34
  37.8 5.8 %collective-permute-start.2 = (f32[2048]{0:T(1024)S(1)}, f32[2048]{0:T(1024)S(1)}, u32[]{:S(2)}, u32[]{:S(2)}) collective-permute-start(f32[2048]{0:T(1024)S(1)} %copy-done.4), channel_id=1, source_target_pairs={{0,4},{1,5},{2,6},{3,7},{4,0},{5,1},{6,2},{7,3},{8,12},{9,13},{10,... | collective-permute-start | bytes 24584 | tf_op jit(solution)/shard_map/ppermute | solution.py:34
  38.2 5.4 %collective-permute-start.3 = (f32[2048]{0:T(1024)S(1)}, f32[2048]{0:T(1024)S(1)}, u32[]{:S(2)}, u32[]{:S(2)}) collective-permute-start(f32[2048]{0:T(1024)S(1)} %copy-done.4), channel_id=1, source_target_pairs={{0,2},{1,3},{2,4},{3,5},{4,6},{5,7},{6,0},{7,1},{8,10},{9,11},{10,... | collective-permute-start | bytes 24584 | tf_op jit(solution)/shard_map/ppermute | solution.py:34
  47.8 15.3 %collective-permute-start.5 = (bf16[4,256,512]{2,1,0:T(8,128)(2,1)S(1)}, bf16[4,256,512]{2,1,0:T(8,128)(2,1)S(1)}, u32[]{:S(2)}, u32[]{:S(2)}) collective-permute-start(bf16[4,256,512]{2,1,0:T(8,128)(2,1)S(1)} %shard_map.95.block.refs_0_), channel_id=1, source_target_pairs={{0,6},{1,7},{2,0},{3,1},{4,2},{5,3},{6,4},{7,5},{8,24},{9,25},{10,... | collective-permute-start | bytes 3145736 | tf_op jit(solution)/shard_map/ppermute | solution.py:34
  48.1 15.1 %collective-permute-start.6 = (bf16[4,256,512]{2,1,0:T(8,128)(2,1)S(1)}, bf16[4,256,512]{2,1,0:T(8,128)(2,1)}, u32[]{:S(2)}, u32[]{:S(2)}) collective-permute-start(bf16[4,256,512]{2,1,0:T(8,128)(2,1)S(1)} %shard_map.95.block.refs_0_), channel_id=1, source_target_pairs={{0,32},{1,33},{2,34},{3,35},{4,36},{5,37},{6,38},{7,39},{8,104},{9... | collective-permute-start | bytes 3145736 | tf_op jit(solution)/shard_map/ppermute | solution.py:34
  48.8 14.4 %collective-permute-start.7 = (bf16[4,256,512]{2,1,0:T(8,128)(2,1)S(1)}, bf16[4,256,512]{2,1,0:T(8,128)(2,1)}, u32[]{:S(2)}, u32[]{:S(2)}) collective-permute-start(bf16[4,256,512]{2,1,0:T(8,128)(2,1)S(1)} %shard_map.95.block.refs_0_), channel_id=1, source_target_pairs={{0,2},{1,3},{2,4},{3,5},{4,6},{5,7},{6,0},{7,1},{8,25},{9,24},{10,... | collective-permute-start | bytes 3145736 | tf_op jit(solution)/shard_map/ppermute | solution.py:34
  87.6 2.7 %copy-start = (bf16[512,256]{1,0:T(8,128)(2,1)}, bf16[512,256]{1,0:T(8,128)(2,1)S(1)}, u32[]{:S(2)}) copy-start(bf16[512,256]{1,0:T(8,128)(2,1)S(1)} %get-tuple-element.61.turned) | copy-start | bytes 786436
  87.6 14.7 %collective-permute-start.9 = (bf16[4,256,512]{2,1,0:T(8,128)(2,1)S(1)}, bf16[4,256,512]{2,1,0:T(8,128)(2,1)S(1)}, u32[]{:S(2)}, u32[]{:S(2)}) collective-permute-start(bf16[4,256,512]{2,1,0:T(8,128)(2,1)S(1)} %get-tuple-element.58), channel_id=1, source_target_pairs={{0,2},{1,3},{2,4},{3,5},{4,6},{5,7},{6,0},{7,1},{8,25},{9,24},{10,... | collective-permute-start | bytes 3145736 | tf_op jit(solution)/shard_map/ppermute | solution.py:34
  90.3 18.1 %collective-permute-start.10 = (bf16[4,256,512]{2,1,0:T(8,128)(2,1)S(1)}, bf16[4,256,512]{2,1,0:T(8,128)(2,1)S(1)}, u32[]{:S(2)}, u32[]{:S(2)}) collective-permute-start(bf16[4,256,512]{2,1,0:T(8,128)(2,1)S(1)} %shard_map.101), channel_id=1, source_target_pairs={{0,32},{1,33},{2,34},{3,35},{4,36},{5,37},{6,38},{7,39},{8,104},{9... | collective-permute-start | bytes 3145736 | tf_op jit(solution)/shard_map/ppermute | solution.py:34
  93.1 17.8 %collective-permute-start.11 = (bf16[4,256,512]{2,1,0:T(8,128)(2,1)S(1)}, bf16[4,256,512]{2,1,0:T(8,128)(2,1)S(1)}, u32[]{:S(2)}, u32[]{:S(2)}) collective-permute-start(bf16[4,256,512]{2,1,0:T(8,128)(2,1)S(1)} %shard_map.99), channel_id=1, source_target_pairs={{0,6},{1,7},{2,0},{3,1},{4,2},{5,3},{6,4},{7,5},{8,24},{9,25},{10,... | collective-permute-start | bytes 3145736 | tf_op jit(solution)/shard_map/ppermute | solution.py:34
  93.6 7.9 %collective-permute-start.8 = (bf16[512,256]{1,0:T(8,128)(2,1)S(1)}, bf16[512,256]{1,0:T(8,128)(2,1)S(1)}, u32[]{:S(2)}, u32[]{:S(2)}) collective-permute-start(bf16[512,256]{1,0:T(8,128)(2,1)S(1)} %get-tuple-element.56), channel_id=1, source_target_pairs={{0,8},{1,9},{2,10},{3,11},{4,12},{5,13},{6,14},{7,15},{8,0},{9,1},... | collective-permute-start | bytes 786440 | tf_op jit(solution)/shard_map/ppermute | solution.py:34
  101.5 11.6 %copy-start.2 = (bf16[512,256]{1,0:T(8,128)(2,1)}, bf16[512,256]{1,0:T(8,128)(2,1)S(1)}, u32[]{:S(2)}) copy-start(bf16[512,256]{1,0:T(8,128)(2,1)S(1)} %collective-permute-done.8.turned_2) | copy-start | bytes 786436
  101.5 25.0 %collective-permute-start.12 = (bf16[4,256,512]{2,1,0:T(8,128)(2,1)S(1)}, bf16[4,256,512]{2,1,0:T(8,128)(2,1)}, u32[]{:S(2)}, u32[]{:S(2)}) collective-permute-start(bf16[4,256,512]{2,1,0:T(8,128)(2,1)S(1)} %shard_map.95.block.refs_0_), channel_id=1, source_target_pairs={{0,8},{1,9},{2,10},{3,11},{4,12},{5,13},{6,14},{7,15},{8,0},{9,1},... | collective-permute-start | bytes 3145736 | tf_op jit(solution)/shard_map/ppermute | solution.py:34
  101.8 24.7 %collective-permute-start.13 = (bf16[4,256,512]{2,1,0:T(8,128)(2,1)S(1)}, bf16[4,256,512]{2,1,0:T(8,128)(2,1)}, u32[]{:S(2)}, u32[]{:S(2)}) collective-permute-start(bf16[4,256,512]{2,1,0:T(8,128)(2,1)S(1)} %collective-permute-done.5.block_1.refs_1_), channel_id=1, source_target_pairs={{0,8},{1,9},{2,10},{3,11},{4,12},{5,13},{6,14},{7,15},{8,0},{9,1},... | collective-permute-start | bytes 3145736 | tf_op jit(solution)/shard_map/ppermute | solution.py:34
  102.3 24.2 %collective-permute-start.14 = (bf16[4,256,512]{2,1,0:T(8,128)(2,1)}, bf16[4,256,512]{2,1,0:T(8,128)(2,1)}, u32[]{:S(2)}, u32[]{:S(2)}) collective-permute-start(bf16[4,256,512]{2,1,0:T(8,128)(2,1)} %collective-permute-done.6.block_2.refs_2_), channel_id=1, source_target_pairs={{0,8},{1,9},{2,10},{3,11},{4,12},{5,13},{6,14},{7,15},{8,0},{9,1},... | collective-permute-start | bytes 3145736 | tf_op jit(solution)/shard_map/ppermute | solution.py:34
  108.4 18.1 %collective-permute-start.15 = (bf16[4,256,512]{2,1,0:T(8,128)(2,1)}, bf16[4,256,512]{2,1,0:T(8,128)(2,1)}, u32[]{:S(2)}, u32[]{:S(2)}) collective-permute-start(bf16[4,256,512]{2,1,0:T(8,128)(2,1)} %collective-permute-done.7.block_3.refs_3_), channel_id=1, source_target_pairs={{0,8},{1,9},{2,10},{3,11},{4,12},{5,13},{6,14},{7,15},{8,0},{9,1},... | collective-permute-start | bytes 3145736 | tf_op jit(solution)/shard_map/ppermute | solution.py:34
  113.1 24.6 %all-to-all-start.3 = ((bf16[64,72,128]{2,1,0:T(8,128)(2,1)}), bf16[64,72,128]{2,1,0:T(8,128)(2,1)S(1)}, u32[]{:S(2)}, u32[]{:S(2)}) async-start(bf16[64,72,128]{2,1,0:T(8,128)(2,1)} %get-tuple-element.60), calls=%async_computation.3 | async-start | bytes 2359296 | tf_op jit(solution)/shard_map/all_to_all | solution.py:404
  118.3 26.9 %collective-permute-start.16 = (bf16[1,128,2048]{2,1,0:T(8,128)(2,1)}, bf16[1,128,2048]{2,1,0:T(8,128)(2,1)}, u32[]{:S(2)}, u32[]{:S(2)}) collective-permute-start(bf16[1,128,2048]{2,1,0:T(8,128)(2,1)} %param.8), channel_id=1, source_target_pairs={{8,0},{9,1},{10,2},{11,3},{12,4},{13,5},{14,6},{15,7},{16,8},{17,9... | collective-permute-start | bytes 1572872 | tf_op jit(solution)/shard_map/ppermute | solution.py:34
  139.4 15.8 %all-to-all-start.4 = ((bf16[16,8,2176]{2,1,0:T(8,128)(2,1)}), bf16[16,8,2176]{2,1,0:T(8,128)(2,1)S(1)}, u32[]{:S(2)}, u32[]{:S(2)}) async-start(bf16[16,8,2176]{2,1,0:T(8,128)(2,1)} %shard_map.104), calls=%async_computation.4 | async-start | bytes 1114112 | tf_op jit(solution)/shard_map/all_to_all | solution.py:411
  (2 other events, 1.9 us)

commit v7 on v6

--- a/solution.py
+++ b/solution.py
@@ -155,21 +155,20 @@
     )
 
 
-def last_kernel(tint, near, block_1, block_2, block_3, early, logits, lse, total):
+def last_kernel(tint, near, block_1, block_2, block_3, early, logits, lse):
     def part(t):
         return sum(
             lax.dot_general(near[near_columns(t, away)], block[t], NT, preferred_element_type=F32)
             for away, block in ((1, block_1), (2, block_2), (3, block_3))
         )
 
-    total[...] = part(0)
+    logits[...] = early[...] + part(0)
 
     @pl.loop(1, 4)
     def _(t):
-        total[...] += part(t)
-
-    values = early[...] + total[...]
-    logits[...] = values
+        logits[...] += part(t)
+
+    values = logits[...]
     top = jnp.max(values, axis=0, keepdims=True)
     sums = top + jnp.log(jnp.sum(jnp.exp(values - top), axis=0, keepdims=True))
     sums = jnp.concatenate([sums[:, :128], sums[:, 128:]], axis=0)
@@ -177,8 +176,8 @@
 
 
 def last_call(tint, near, blocks, early):
-    outs = [((1024, 256), F32, jax.ShapeDtypeStruct), ((64, 2, 128), F32, jax.ShapeDtypeStruct), ((1024, 256), F32)]
-    return call(last_kernel, tint, [near, *blocks, early], outs, 6 * 1024 * 256 * 2048, 17 << 20)[:2]
+    outs = [((1024, 256), F32, jax.ShapeDtypeStruct), ((64, 2, 128), F32, jax.ShapeDtypeStruct)]
+    return call(last_kernel, tint, [near, *blocks, early], outs, 6 * 1024 * 256 * 2048, 17 << 20)
 
 
 def product(dlogits, near, away, out):

time: 158 us -> 157 us (level)
  no operation moved by 1% of the time
where the time goes in v7:
time: 157 us; the launch traced here: 156 us
  starting transfers between devices  61.7 us (39%)
  Pallas kernels  37.5 us (24%)
  waiting for transfers between devices  25.9 us (16%)
  blocking collectives  14.8 us (9%)
  other arithmetic  7.89 us (5%)
  between operations  5.05 us (3%)
  local copies, waits for them, and re-layouts  3.3 us (2%)
    ppermute x17, starting transfers between devices, move(): return lax.ppermute(block, AXES, route(step))  35.2 us
    pallas_call x9, Pallas kernels, call(): pl.pallas_call(kernel, in_specs=smem + [vmem] * len(operands), out_specs=...  16.4 us
    all_to_all x1, blocking collectives, local(): parts = lax.all_to_all(lse, CHIPS, 0, 0, tiled=True)  14.8 us
    ppermute x17, waiting for transfers between devices, move(): return lax.ppermute(block, AXES, route(step))  9.98 us
    all_to_all x1, starting transfers between devices, local(): quarter = lax.all_to_all(slots_call(rows), CHIPS, 0, 0, tiled=True)  9.32 us
    pallas_call x1, Pallas kernels, head_call(): pl.pallas_call(head_kernel, grid_spec=pltpu.PrefetchScalarGridSpec(num_sc...  9.24 us
    all_to_all x1, waiting for transfers between devices, local(): came = lax.all_to_all(placed, PIPE, 0, 0, tiled=True)  8.81 us
    pallas_call x1, Pallas kernels, early_call(): pl.pallas_call(early_kernel, in_specs=[pl.BlockSpec(memory_space=pltpu.SM...  6.72 us
  transfers between devices with their start and end apart: 21, of which 6 were waited for; matrix products, arithmetic and copies ran while one was open for 5% of the time, Pallas kernels for 18%

profile of v7, /device:TPU:1, one launch (start us, length us, event | category | flops | bytes accessed | tf_op | source)
XLA Modules:
  0.0 156.1 jit_solution(8726338797599423655)
XLA Ops:
  2.1 6.0 %all-to-all-start = ((bf16[16,8,2048]{2,1,0:T(8,128)(2,1)}), bf16[16,8,2048]{2,1,0:T(8,128)(2,1)S(1)}, u32[]{:S(2)}, u32[]{:S(2)}) async-start(bf16[16,8,2048]{2,1,0:T(8,128)(2,1)} %bitcast.32), calls=%async_computation | async-start | bytes 1048576 | tf_op jit(solution)/shard_map/all_to_all | solution.py:360
  14.3 3.5 %all-to-all-done = bf16[16,8,2048]{2,1,0:T(8,128)(2,1)S(1)} async-done(((bf16[16,8,2048]{2,1,0:T(8,128)(2,1)}), bf16[16,8,2048]{2,1,0:T(8,128)(2,1)S(1)}, u32[]{:S(2)}, u32[]{:S(2)}) %all-to-all-start) | async-done | bytes 524320 | tf_op jit(solution)/shard_map/all_to_all | solution.py:360
  19.0 9.3 %all-to-all-start.1 = ((bf16[64,72,128]{2,1,0:T(8,128)(2,1)}), bf16[64,72,128]{2,1,0:T(8,128)(2,1)S(1)}, u32[]{:S(2)}, u32[]{:S(2)}) async-start(bf16[64,72,128]{2,1,0:T(8,128)(2,1)} %shard_map.94), calls=%async_computation.1 | async-start | bytes 2359296 | tf_op jit(solution)/shard_map/all_to_all | solution.py:383
  28.4 2.0 %fusion.6 = f32[]{:T(128)} fusion(s32[1]{0:T(128)} %bitcast.8, s32[1]{0:T(128)} %bitcast.7), kind=kLoop, calls=%fused_computation.26 | loop fusion | flops 7 | bytes 12 | tf_op jit(solution)/shard_map/reduce_sum | solution.py:366
  30.4 2.1 %broadcast_divide_fusion = f32[2]{0:T(128)S(1)} fusion(f32[]{:T(128)} %fusion.6, s32[1]{0:T(128)} %bitcast.8, s32[1]{0:T(128)} %bitcast.7), kind=kLoop, calls=%fused_computation.25 | loop fusion | flops 8 | bytes 20 | tf_op jit(solution)/shard_map/div | solution.py:366
  32.5 2.5 %collective-permute-start = (s32[2,128]{1,0:T(2,128)S(1)}, s32[2,128]{1,0:T(2,128)S(1)}, u32[]{:S(2)}, u32[]{:S(2)}) collective-permute-start(s32[2,128]{1,0:T(2,128)S(1)} %pad_add_fusion), channel_id=1, source_target_pairs={{0,1},{1,0},{2,3},{3,2},{4,5},{5,4},{6,7},{7,6},{8,9},{9,8},{10,11... | collective-permute-start | bytes 3080 | tf_op jit(solution)/shard_map/ppermute | solution.py:34
  35.1 2.7 %collective-permute-start.1 = (f32[2048]{0:T(1024)S(1)}, f32[2048]{0:T(1024)S(1)}, u32[]{:S(2)}, u32[]{:S(2)}) collective-permute-start(f32[2048]{0:T(1024)S(1)} %copy-done.4), channel_id=1, source_target_pairs={{0,6},{1,7},{2,0},{3,1},{4,2},{5,3},{6,4},{7,5},{8,14},{9,15},{10,... | collective-permute-start | bytes 24584 | tf_op jit(solution)/shard_map/ppermute | solution.py:34
  39.4 2.6 %collective-permute-done.1 = f32[2048]{0:T(1024)S(1)} collective-permute-done((f32[2048]{0:T(1024)S(1)}, f32[2048]{0:T(1024)S(1)}, u32[]{:S(2)}, u32[]{:S(2)}) %collective-permute-start.1) | collective-permute-done | bytes 8224 | tf_op jit(solution)/shard_map/ppermute | solution.py:34
  43.8 3.7 %all-to-all-done.1.came = bf16[64,72,128]{2,1,0:T(8,128)(2,1)S(1)} async-done(((bf16[64,72,128]{2,1,0:T(8,128)(2,1)}), bf16[64,72,128]{2,1,0:T(8,128)(2,1)S(1)}, u32[]{:S(2)}, u32[]{:S(2)}) %all-to-all-start.1) | async-done | bytes 1179680 | tf_op jit(solution)/shard_map/all_to_all | solution.py:383
  48.8 1.8 %collective-permute-start.7 = (bf16[4,256,512]{2,1,0:T(8,128)(2,1)S(1)}, bf16[4,256,512]{2,1,0:T(8,128)(2,1)}, u32[]{:S(2)}, u32[]{:S(2)}) collective-permute-start(bf16[4,256,512]{2,1,0:T(8,128)(2,1)S(1)} %shard_map.95.block.refs_0_), channel_id=1, source_target_pairs={{0,2},{1,3},{2,4},{3,5},{4,6},{5,7},{6,0},{7,1},{8,25},{9,24},{10,... | collective-permute-start | bytes 3145736 | tf_op jit(solution)/shard_map/ppermute | solution.py:34
  50.7 6.7 %shard_map.96 = (f32[1024,256]{1,0:T(8,128)S(1)}, bf16[16,1024,512]{2,1,0:T(8,128)(2,1)S(1)}) custom-call(s32[7]{0:T(128)S(1)} %pad_add_fusion.1.tint, bf16[512,8192]{1,0:T(8,128)(2,1)} %head.1, bf16[512,8192]{1,0:T(8,128)(2,1)} %collective-permute-done.4.head_2, bf16[4,256,512]{2,1,0:T(8,128)(2,1)S(1)} %shard_map.95.block.refs_0_), custom_call_target="tpu_custom_call" | custom-call | flops 1073741824 | bytes 17825792 | tf_op jit(solution)/shard_map/pallas_call | solution.py:142
  57.4 5.8 %collective-permute-done.5.block_1.refs_1_ = bf16[4,256,512]{2,1,0:T(8,128)(2,1)S(1)} collective-permute-done((bf16[4,256,512]{2,1,0:T(8,128)(2,1)S(1)}, bf16[4,256,512]{2,1,0:T(8,128)(2,1)S(1)}, u32[]{:S(2)}, u32[]{:S(2)}) %collective-permute-start.5) | collective-permute-done | bytes 1048608 | tf_op jit(solution)/shard_map/ppermute | solution.py:34
  63.2 5.9 %shard_map.97 = (f32[1024,256]{1,0:T(8,128)S(1)}, f32[64,2,128]{2,1,0:T(2,128)S(1)}) custom-call(s32[7]{0:T(128)S(1)} %pad_add_fusion.1.tint, bf16[16,1024,512]{2,1,0:T(8,128)(2,1)S(1)} %get-tuple-element.44.near, bf16[4,256,512]{2,1,0:T(8,128)(2,1)S(1)} %collective-permute-done.5.block_1.refs_1_, ...), custom_call_target="tpu_custom_call" | custom-call | flops 3221225472 | bytes 17825792 | tf_op jit(solution)/shard_map/pallas_call | solution.py:58
  69.1 14.8 %all_to_all.25.parts = f32[64,2,128]{2,1,0:T(2,128)S(1)} all-to-all(f32[64,2,128]{2,1,0:T(2,128)S(1)} %get-tuple-element.51), channel_id=1, replica_groups=mesh['y'=4,'zl'=2,'c'=2,'x'=4,'zh'=2] {'x','y','zl','zh'}, dimensions={0} | all-to-all | bytes 131072 | tf_op jit(solution)/shard_map/all_to_all | solution.py:391
  83.8 3.0 %shard_map.98 = (bf16[512,256]{1,0:T(8,128)(2,1)S(1)}, bf16[512,256]{1,0:T(8,128)(2,1)S(1)}, bf16[256,1024]{1,0:T(8,128)(2,1)S(1)}, f32[1,256]{1,0:T(1,128)S(1)}, bf16[4,256,512]{2,1,0:T(8,128)(2,1)S(1)}) custom-call(s32[7]{0:T(128)S(1)} %pad_add_fusion.1.tint, f32[1024,256]{1,0:T(8,128)S(1)} %get-tuple-element.50.logits, ...), custom_call_target="tpu_custom_call" | custom-call | flops 1073741824 | bytes 5242880 | tf_op jit(solution)/shard_map/pallas_call | solution.py:212
  92.9 6.1 %collective-permute-start.8 = (bf16[512,256]{1,0:T(8,128)(2,1)S(1)}, bf16[512,256]{1,0:T(8,128)(2,1)S(1)}, u32[]{:S(2)}, u32[]{:S(2)}) collective-permute-start(bf16[512,256]{1,0:T(8,128)(2,1)S(1)} %get-tuple-element.56), channel_id=1, source_target_pairs={{0,8},{1,9},{2,10},{3,11},{4,12},{5,13},{6,14},{7,15},{8,0},{9,1},... | collective-permute-start | bytes 786440 | tf_op jit(solution)/shard_map/ppermute | solution.py:34
  101.5 6.1 %collective-permute-start.14 = (bf16[4,256,512]{2,1,0:T(8,128)(2,1)}, bf16[4,256,512]{2,1,0:T(8,128)(2,1)}, u32[]{:S(2)}, u32[]{:S(2)}) collective-permute-start(bf16[4,256,512]{2,1,0:T(8,128)(2,1)} %collective-permute-done.6.block_2.refs_2_), channel_id=1, source_target_pairs={{0,8},{1,9},{2,10},{3,11},{4,12},{5,13},{6,14},{7,15},{8,0},{9,1},... | collective-permute-start | bytes 3145736 | tf_op jit(solution)/shard_map/ppermute | solution.py:34
  107.6 2.5 %collective-permute-start.15 = (bf16[4,256,512]{2,1,0:T(8,128)(2,1)}, bf16[4,256,512]{2,1,0:T(8,128)(2,1)}, u32[]{:S(2)}, u32[]{:S(2)}) collective-permute-start(bf16[4,256,512]{2,1,0:T(8,128)(2,1)} %collective-permute-done.7.block_3.refs_3_), channel_id=1, source_target_pairs={{0,8},{1,9},{2,10},{3,11},{4,12},{5,13},{6,14},{7,15},{8,0},{9,1},... | collective-permute-start | bytes 3145736 | tf_op jit(solution)/shard_map/ppermute | solution.py:34
  110.1 2.2 %shard_map.102 = (bf16[64,72,128]{2,1,0:T(8,128)(2,1)}, f32[256,128]{1,0:T(8,128)S(1)}) custom-call(bf16[64,72,128]{2,1,0:T(8,128)(2,1)S(1)} %all-to-all-done.1.came, f32[4,256,512]{2,1,0:T(8,128)S(1)} %shard_map.100.ours, bf16[4,256,512]{2,1,0:T(8,128)(2,1)S(1)} %collective-permute-done.9.one, bf16[4,256,512]{2,1,0:T(8,128)(2,1)S(1)} %collective-permute-done.10.two, ...), custom_call_target="tpu_custom_call" | custom-call | bytes 6291456 | tf_op jit(solution)/shard_map/pallas_call | solution.py:299
  112.3 5.3 %all-to-all-start.3 = ((bf16[64,72,128]{2,1,0:T(8,128)(2,1)}), bf16[64,72,128]{2,1,0:T(8,128)(2,1)S(1)}, u32[]{:S(2)}, u32[]{:S(2)}) async-start(bf16[64,72,128]{2,1,0:T(8,128)(2,1)} %get-tuple-element.60), calls=%async_computation.3 | async-start | bytes 2359296 | tf_op jit(solution)/shard_map/all_to_all | solution.py:403
  117.6 6.7 %collective-permute-start.16 = (bf16[1,128,2048]{2,1,0:T(8,128)(2,1)}, bf16[1,128,2048]{2,1,0:T(8,128)(2,1)}, u32[]{:S(2)}, u32[]{:S(2)}) collective-permute-start(bf16[1,128,2048]{2,1,0:T(8,128)(2,1)} %param.8), channel_id=1, source_target_pairs={{8,0},{9,1},{10,2},{11,3},{12,4},{13,5},{14,6},{15,7},{16,8},{17,9... | collective-permute-start | bytes 1572872 | tf_op jit(solution)/shard_map/ppermute | solution.py:34
  127.7 9.2 %shard_map.103 = bf16[512,8192]{1,0:T(8,128)(2,1)} custom-call(s32[7]{0:T(128)S(1)} %pad_add_fusion.1.tint, bf16[512,256]{1,0:T(8,128)(2,1)S(1)} %copy-done.1, bf16[512,256]{1,0:T(8,128)(2,1)S(1)} %copy-done.3, bf16[4,256,512]{2,1,0:T(8,128)(2,1)S(1)} %shard_map.95.block.refs_0_, bf16[4,256,512]{2,1,0:T(8,128)(2,1)S(1)} %collective-permute-done.5.block_1.refs_1_, ...), custom_call_target="tpu_custom_call" | custom-call | flops 4294967296 | bytes 17825792 | tf_op jit(solution)/shard_map/pallas_call | solution.py:249
  138.6 5.9 %all-to-all-start.4 = ((bf16[16,8,2176]{2,1,0:T(8,128)(2,1)}), bf16[16,8,2176]{2,1,0:T(8,128)(2,1)S(1)}, u32[]{:S(2)}, u32[]{:S(2)}) async-start(bf16[16,8,2176]{2,1,0:T(8,128)(2,1)} %shard_map.104), calls=%async_computation.4 | async-start | bytes 1114112 | tf_op jit(solution)/shard_map/all_to_all | solution.py:410
  145.6 8.8 %all-to-all-done.4.exits = bf16[16,8,2176]{2,1,0:T(8,128)(2,1)S(1)} async-done(((bf16[16,8,2176]{2,1,0:T(8,128)(2,1)}), bf16[16,8,2176]{2,1,0:T(8,128)(2,1)S(1)}, u32[]{:S(2)}, u32[]{:S(2)}) %all-to-all-start.4) | async-done | bytes 557088 | tf_op jit(solution)/shard_map/all_to_all | solution.py:410
  (70 shorter events, 26.0 us)
Async XLA Ops:
  0.6 50.1 %collective-permute-start.4 = (bf16[512,8192]{1,0:T(8,128)(2,1)}, bf16[512,8192]{1,0:T(8,128)(2,1)}, u32[]{:S(2)}, u32[]{:S(2)}) collective-permute-start(bf16[512,8192]{1,0:T(8,128)(2,1)} %head.1), channel_id=1, source_target_pairs={{0,8},{1,9},{2,10},{3,11},{4,12},{5,13},{6,14},{7,15},{8,0},{9,1},... | collective-permute-start | bytes 25165832 | tf_op jit(solution)/shard_map/ppermute | solution.py:34
  2.1 15.7 %all-to-all-start = ((bf16[16,8,2048]{2,1,0:T(8,128)(2,1)}), bf16[16,8,2048]{2,1,0:T(8,128)(2,1)S(1)}, u32[]{:S(2)}, u32[]{:S(2)}) async-start(bf16[16,8,2048]{2,1,0:T(8,128)(2,1)} %bitcast.32), calls=%async_computation | async-start | bytes 1048576 | tf_op jit(solution)/shard_map/all_to_all | solution.py:360
  8.2 26.9 %copy-start.4 = (f32[2048]{0:T(1024)S(1)}, f32[2048]{0:T(1024)}, u32[]{:S(2)}) copy-start(f32[2048]{0:T(1024)} %param.9) | copy-start | bytes 24580
  19.0 28.4 %all-to-all-start.1 = ((bf16[64,72,128]{2,1,0:T(8,128)(2,1)}), bf16[64,72,128]{2,1,0:T(8,128)(2,1)S(1)}, u32[]{:S(2)}, u32[]{:S(2)}) async-start(bf16[64,72,128]{2,1,0:T(8,128)(2,1)} %shard_map.94), calls=%async_computation.1 | async-start | bytes 2359296 | tf_op jit(solution)/shard_map/all_to_all | solution.py:383
  32.5 6.4 %collective-permute-start = (s32[2,128]{1,0:T(2,128)S(1)}, s32[2,128]{1,0:T(2,128)S(1)}, u32[]{:S(2)}, u32[]{:S(2)}) collective-permute-start(s32[2,128]{1,0:T(2,128)S(1)} %pad_add_fusion), channel_id=1, source_target_pairs={{0,1},{1,0},{2,3},{3,2},{4,5},{5,4},{6,7},{7,6},{8,9},{9,8},{10,11... | collective-permute-start | bytes 3080 | tf_op jit(solution)/shard_map/ppermute | solution.py:34
  35.1 6.9 %collective-permute-start.1 = (f32[2048]{0:T(1024)S(1)}, f32[2048]{0:T(1024)S(1)}, u32[]{:S(2)}, u32[]{:S(2)}) collective-permute-start(f32[2048]{0:T(1024)S(1)} %copy-done.4), channel_id=1, source_target_pairs={{0,6},{1,7},{2,0},{3,1},{4,2},{5,3},{6,4},{7,5},{8,14},{9,15},{10,... | collective-permute-start | bytes 24584 | tf_op jit(solution)/shard_map/ppermute | solution.py:34
  37.8 5.8 %collective-permute-start.2 = (f32[2048]{0:T(1024)S(1)}, f32[2048]{0:T(1024)S(1)}, u32[]{:S(2)}, u32[]{:S(2)}) collective-permute-start(f32[2048]{0:T(1024)S(1)} %copy-done.4), channel_id=1, source_target_pairs={{0,4},{1,5},{2,6},{3,7},{4,0},{5,1},{6,2},{7,3},{8,12},{9,13},{10,... | collective-permute-start | bytes 24584 | tf_op jit(solution)/shard_map/ppermute | solution.py:34
  38.2 5.4 %collective-permute-start.3 = (f32[2048]{0:T(1024)S(1)}, f32[2048]{0:T(1024)S(1)}, u32[]{:S(2)}, u32[]{:S(2)}) collective-permute-start(f32[2048]{0:T(1024)S(1)} %copy-done.4), channel_id=1, source_target_pairs={{0,2},{1,3},{2,4},{3,5},{4,6},{5,7},{6,0},{7,1},{8,10},{9,11},{10,... | collective-permute-start | bytes 24584 | tf_op jit(solution)/shard_map/ppermute | solution.py:34
  47.8 15.3 %collective-permute-start.5 = (bf16[4,256,512]{2,1,0:T(8,128)(2,1)S(1)}, bf16[4,256,512]{2,1,0:T(8,128)(2,1)S(1)}, u32[]{:S(2)}, u32[]{:S(2)}) collective-permute-start(bf16[4,256,512]{2,1,0:T(8,128)(2,1)S(1)} %shard_map.95.block.refs_0_), channel_id=1, source_target_pairs={{0,6},{1,7},{2,0},{3,1},{4,2},{5,3},{6,4},{7,5},{8,24},{9,25},{10,... | collective-permute-start | bytes 3145736 | tf_op jit(solution)/shard_map/ppermute | solution.py:34
  48.1 15.1 %collective-permute-start.6 = (bf16[4,256,512]{2,1,0:T(8,128)(2,1)S(1)}, bf16[4,256,512]{2,1,0:T(8,128)(2,1)}, u32[]{:S(2)}, u32[]{:S(2)}) collective-permute-start(bf16[4,256,512]{2,1,0:T(8,128)(2,1)S(1)} %shard_map.95.block.refs_0_), channel_id=1, source_target_pairs={{0,32},{1,33},{2,34},{3,35},{4,36},{5,37},{6,38},{7,39},{8,104},{9... | collective-permute-start | bytes 3145736 | tf_op jit(solution)/shard_map/ppermute | solution.py:34
  48.8 14.4 %collective-permute-start.7 = (bf16[4,256,512]{2,1,0:T(8,128)(2,1)S(1)}, bf16[4,256,512]{2,1,0:T(8,128)(2,1)}, u32[]{:S(2)}, u32[]{:S(2)}) collective-permute-start(bf16[4,256,512]{2,1,0:T(8,128)(2,1)S(1)} %shard_map.95.block.refs_0_), channel_id=1, source_target_pairs={{0,2},{1,3},{2,4},{3,5},{4,6},{5,7},{6,0},{7,1},{8,25},{9,24},{10,... | collective-permute-start | bytes 3145736 | tf_op jit(solution)/shard_map/ppermute | solution.py:34
  86.8 2.7 %copy-start = (bf16[512,256]{1,0:T(8,128)(2,1)}, bf16[512,256]{1,0:T(8,128)(2,1)S(1)}, u32[]{:S(2)}) copy-start(bf16[512,256]{1,0:T(8,128)(2,1)S(1)} %get-tuple-element.61.turned) | copy-start | bytes 786436
  86.8 14.7 %collective-permute-start.9 = (bf16[4,256,512]{2,1,0:T(8,128)(2,1)S(1)}, bf16[4,256,512]{2,1,0:T(8,128)(2,1)S(1)}, u32[]{:S(2)}, u32[]{:S(2)}) collective-permute-start(bf16[4,256,512]{2,1,0:T(8,128)(2,1)S(1)} %get-tuple-element.58), channel_id=1, source_target_pairs={{0,2},{1,3},{2,4},{3,5},{4,6},{5,7},{6,0},{7,1},{8,25},{9,24},{10,... | collective-permute-start | bytes 3145736 | tf_op jit(solution)/shard_map/ppermute | solution.py:34
  89.5 18.1 %collective-permute-start.10 = (bf16[4,256,512]{2,1,0:T(8,128)(2,1)S(1)}, bf16[4,256,512]{2,1,0:T(8,128)(2,1)S(1)}, u32[]{:S(2)}, u32[]{:S(2)}) collective-permute-start(bf16[4,256,512]{2,1,0:T(8,128)(2,1)S(1)} %shard_map.101), channel_id=1, source_target_pairs={{0,32},{1,33},{2,34},{3,35},{4,36},{5,37},{6,38},{7,39},{8,104},{9... | collective-permute-start | bytes 3145736 | tf_op jit(solution)/shard_map/ppermute | solution.py:34
  92.3 17.8 %collective-permute-start.11 = (bf16[4,256,512]{2,1,0:T(8,128)(2,1)S(1)}, bf16[4,256,512]{2,1,0:T(8,128)(2,1)S(1)}, u32[]{:S(2)}, u32[]{:S(2)}) collective-permute-start(bf16[4,256,512]{2,1,0:T(8,128)(2,1)S(1)} %shard_map.99), channel_id=1, source_target_pairs={{0,6},{1,7},{2,0},{3,1},{4,2},{5,3},{6,4},{7,5},{8,24},{9,25},{10,... | collective-permute-start | bytes 3145736 | tf_op jit(solution)/shard_map/ppermute | solution.py:34
  92.9 7.9 %collective-permute-start.8 = (bf16[512,256]{1,0:T(8,128)(2,1)S(1)}, bf16[512,256]{1,0:T(8,128)(2,1)S(1)}, u32[]{:S(2)}, u32[]{:S(2)}) collective-permute-start(bf16[512,256]{1,0:T(8,128)(2,1)S(1)} %get-tuple-element.56), channel_id=1, source_target_pairs={{0,8},{1,9},{2,10},{3,11},{4,12},{5,13},{6,14},{7,15},{8,0},{9,1},... | collective-permute-start | bytes 786440 | tf_op jit(solution)/shard_map/ppermute | solution.py:34
  100.8 11.6 %copy-start.2 = (bf16[512,256]{1,0:T(8,128)(2,1)}, bf16[512,256]{1,0:T(8,128)(2,1)S(1)}, u32[]{:S(2)}) copy-start(bf16[512,256]{1,0:T(8,128)(2,1)S(1)} %collective-permute-done.8.turned_2) | copy-start | bytes 786436
  100.8 25.0 %collective-permute-start.12 = (bf16[4,256,512]{2,1,0:T(8,128)(2,1)S(1)}, bf16[4,256,512]{2,1,0:T(8,128)(2,1)}, u32[]{:S(2)}, u32[]{:S(2)}) collective-permute-start(bf16[4,256,512]{2,1,0:T(8,128)(2,1)S(1)} %shard_map.95.block.refs_0_), channel_id=1, source_target_pairs={{0,8},{1,9},{2,10},{3,11},{4,12},{5,13},{6,14},{7,15},{8,0},{9,1},... | collective-permute-start | bytes 3145736 | tf_op jit(solution)/shard_map/ppermute | solution.py:34
  101.0 24.7 %collective-permute-start.13 = (bf16[4,256,512]{2,1,0:T(8,128)(2,1)S(1)}, bf16[4,256,512]{2,1,0:T(8,128)(2,1)}, u32[]{:S(2)}, u32[]{:S(2)}) collective-permute-start(bf16[4,256,512]{2,1,0:T(8,128)(2,1)S(1)} %collective-permute-done.5.block_1.refs_1_), channel_id=1, source_target_pairs={{0,8},{1,9},{2,10},{3,11},{4,12},{5,13},{6,14},{7,15},{8,0},{9,1},... | collective-permute-start | bytes 3145736 | tf_op jit(solution)/shard_map/ppermute | solution.py:34
  101.5 24.2 %collective-permute-start.14 = (bf16[4,256,512]{2,1,0:T(8,128)(2,1)}, bf16[4,256,512]{2,1,0:T(8,128)(2,1)}, u32[]{:S(2)}, u32[]{:S(2)}) collective-permute-start(bf16[4,256,512]{2,1,0:T(8,128)(2,1)} %collective-permute-done.6.block_2.refs_2_), channel_id=1, source_target_pairs={{0,8},{1,9},{2,10},{3,11},{4,12},{5,13},{6,14},{7,15},{8,0},{9,1},... | collective-permute-start | bytes 3145736 | tf_op jit(solution)/shard_map/ppermute | solution.py:34
  107.6 18.1 %collective-permute-start.15 = (bf16[4,256,512]{2,1,0:T(8,128)(2,1)}, bf16[4,256,512]{2,1,0:T(8,128)(2,1)}, u32[]{:S(2)}, u32[]{:S(2)}) collective-permute-start(bf16[4,256,512]{2,1,0:T(8,128)(2,1)} %collective-permute-done.7.block_3.refs_3_), channel_id=1, source_target_pairs={{0,8},{1,9},{2,10},{3,11},{4,12},{5,13},{6,14},{7,15},{8,0},{9,1},... | collective-permute-start | bytes 3145736 | tf_op jit(solution)/shard_map/ppermute | solution.py:34
  112.3 24.6 %all-to-all-start.3 = ((bf16[64,72,128]{2,1,0:T(8,128)(2,1)}), bf16[64,72,128]{2,1,0:T(8,128)(2,1)S(1)}, u32[]{:S(2)}, u32[]{:S(2)}) async-start(bf16[64,72,128]{2,1,0:T(8,128)(2,1)} %get-tuple-element.60), calls=%async_computation.3 | async-start | bytes 2359296 | tf_op jit(solution)/shard_map/all_to_all | solution.py:403
  117.6 26.9 %collective-permute-start.16 = (bf16[1,128,2048]{2,1,0:T(8,128)(2,1)}, bf16[1,128,2048]{2,1,0:T(8,128)(2,1)}, u32[]{:S(2)}, u32[]{:S(2)}) collective-permute-start(bf16[1,128,2048]{2,1,0:T(8,128)(2,1)} %param.8), channel_id=1, source_target_pairs={{8,0},{9,1},{10,2},{11,3},{12,4},{13,5},{14,6},{15,7},{16,8},{17,9... | collective-permute-start | bytes 1572872 | tf_op jit(solution)/shard_map/ppermute | solution.py:34
  138.6 15.8 %all-to-all-start.4 = ((bf16[16,8,2176]{2,1,0:T(8,128)(2,1)}), bf16[16,8,2176]{2,1,0:T(8,128)(2,1)S(1)}, u32[]{:S(2)}, u32[]{:S(2)}) async-start(bf16[16,8,2176]{2,1,0:T(8,128)(2,1)} %shard_map.104), calls=%async_computation.4 | async-start | bytes 1114112 | tf_op jit(solution)/shard_map/all_to_all | solution.py:410
  (2 other events, 1.9 us)
